TPU v7x, 256 devices: a whole 4x4x8 slice. The times are simulated.
256 devices in a mesh: tm: 32 (over y, z), space: 8 (over x, core).
Axes of the slice: x: 4, y: 4, z: 8, core: 2. Of those that a mesh axis runs over, the one named last changes fastest.
Arguments:
- source: float32 [256, 320, 64], P('tm', None, 'space'), may hold values from -21 to 21
- decay_rate: float32 [256, 320, 64], P('tm', None, 'space'), may hold values from 0.4 to 1
- blocks: bfloat16 [64, 7, 102400], P('space'), may hold values from -0.0048828125 to 0.0048828125
- neighbours: int32 [6, 64], P(None, 'space'), may hold values from 0 to 7
- interface_jacobian_blocks: bfloat16 [2, 16, 102400], P(None, 'space'), may hold values from -0.0048828125 to 0.0048828125
- face_element_owner: int32 [2, 16], P(None, 'space'), may hold values from 0 to 7
- pairing: int32 [8, 2], P('space'), may hold values from 0 to 1, each once within a row
Outputs:
- adjoint: float32 [256, 320, 64], P('tm', None, 'space')
- residual: float32 [256, 320, 64], P('tm', None, 'space')
Inputs may be any that keep to these rules, and one draw needn't show every extreme that they name: `neighbours`: element indices local to the element's own partition. `face_element_owner`: element indices local to the slot's own partition. `pairing`: each row is a permutation of 0 to 1.
All inputs are finite; a program needn't handle non-finite values.
Results may differ from a plain program's by a relative error of at most 0.0003.
Values sent between devices are 32-bit elements; how exact they have to be, the bound alone decides.
No kernel may reach another device: no remote copies, remote signals or barrier semaphores. Data moves between devices by JAX's collectives and lax.ppermute only.
A program may use at most 128 MiB of HBM per device.

v0:
```python
import jax
import jax.numpy as jnp
from jax import lax
from jax.sharding import PartitionSpec as P

epsilon = 1e-06


def prefix(value, axis, combine, identity):
    length, mine = (lax.axis_size(axis), lax.axis_index(axis))
    everything = jax.tree.map(lambda part: lax.all_gather(part, axis), value)
    start = jax.tree.map(
        lambda part, zero: jnp.broadcast_to(jnp.asarray(zero, part.dtype), part.shape),
        value,
        identity,
    )

    def step(k, before):
        at = length - 1 - k
        reached = at > mine
        new = combine(before, jax.tree.map(lambda part: part[at], everything))
        return jax.tree.map(lambda a, b: jnp.where(reached, a, b), new, before)

    return lax.fori_loop(0, length, step, start)


def spread(block, axis, holder):
    block = jnp.where(lax.axis_index(axis) == holder, block, jnp.zeros_like(block))
    return lax.psum(block, axis)


def with_halo(cells, sides, width):
    for axis, dim in sides:
        count = lax.axis_size(axis)
        head = lax.slice_in_dim(cells, 0, width, axis=dim)
        tail = lax.slice_in_dim(cells, cells.shape[dim] - width, cells.shape[dim], axis=dim)
        cells = jnp.concatenate(
            [
                lax.ppermute(tail, axis, [(i, (i + 1) % count) for i in range(count)]),
                cells,
                lax.ppermute(head, axis, [((i + 1) % count, i) for i in range(count)]),
            ],
            axis=dim,
        )
    return cells


def compose(earlier, later):
    return (later[0] * earlier[0], later[1] + later[0] * earlier[1])


def local_maps(field, decay_rate):

    def compose_step(carry, inputs):
        product, offset = carry
        slab_rate, slab_value = inputs
        return ((product * slab_rate, slab_value + slab_rate * offset), None)

    initial = (jnp.ones(field.shape[1:], jnp.float32), jnp.zeros(field.shape[1:], jnp.float32))
    result_maps, unused = lax.scan(compose_step, initial, (decay_rate, field), reverse=True)
    return result_maps


def sweep(field, decay_rate, entering):

    def sweep_step(carried, inputs):
        slab_rate, slab_value = inputs
        carried = slab_value + slab_rate * carried
        return (carried, carried)

    unused_last, solved = lax.scan(sweep_step, entering, (decay_rate, field), reverse=True)
    return solved


def periodic_chain(field, decay_rate):
    own_map = local_maps(field, decay_rate)
    identity = (jnp.ones_like(own_map[0]), jnp.zeros_like(own_map[1]))
    beyond = prefix(own_map, "tm", compose, identity)
    whole_loop = compose(beyond, own_map)
    closing = spread(whole_loop[1] / (1.0 - whole_loop[0]), "tm", 0)
    entering = beyond[0] * closing + beyond[1]
    return sweep(field, decay_rate, entering)


def apply_spatial(
    field, blocks, neighbours, interface_jacobian_blocks, face_element_owner, pairing
):
    width = field.shape[1]
    block_data = blocks.astype(jnp.float32).reshape(blocks.shape[0], blocks.shape[1], width, width)
    contribs = jnp.einsum("efnm,tne->tfme", block_data, field, precision=lax.Precision.HIGHEST)
    result = contribs[:, 0]
    for face in range(neighbours.shape[0]):
        result = result.at[:, :, neighbours[face]].add(contribs[:, face + 1])
    upper_ids = face_element_owner[0]
    lower_ids = face_element_owner[1]
    slot_order = pairing[0]
    couple_data = interface_jacobian_blocks.astype(jnp.float32).reshape(
        2, interface_jacobian_blocks.shape[1], width, width
    )
    upward = jnp.einsum(
        "inm,tni->tmi", couple_data[0], field[:, :, upper_ids], precision=lax.Precision.HIGHEST
    )
    downward = jnp.einsum(
        "inm,tni->tmi", couple_data[1], field[:, :, lower_ids], precision=lax.Precision.HIGHEST
    )
    placed = jnp.zeros_like(downward).at[:, :, slot_order].set(downward)
    packet = jnp.concatenate([placed, upward], axis=2)
    slot_count = upward.shape[2]
    extended = with_halo(packet, (("space", 2),), slot_count)
    from_below = extended[:, :, :slot_count]
    from_above = extended[:, :, 3 * slot_count :]
    result = result.at[:, :, lower_ids].add(from_below[:, :, slot_order])
    return result.at[:, :, upper_ids].add(from_above)


def shards(
    source, decay_rate, blocks, neighbours, interface_jacobian_blocks, face_element_owner, pairing
):
    norm_source = jnp.sqrt(lax.psum(jnp.sum(source * source), ("tm", "space")) + epsilon)
    vectors = [source / norm_source]
    solutions = []
    outputs = []
    columns = []
    for column in range(2):
        current = vectors[column]
        chained = periodic_chain(current, decay_rate)
        applied = current + apply_spatial(
            chained, blocks, neighbours, interface_jacobian_blocks, face_element_owner, pairing
        )
        solutions.append(chained)
        outputs.append(applied)
        local_dots = tuple((jnp.sum(vector * applied) for vector in vectors))
        coeffs = lax.psum(local_dots, ("tm", "space"))
        remainder = applied
        for vector, projected in zip(vectors, coeffs):
            remainder = remainder - projected * vector
        height = jnp.sqrt(lax.psum(jnp.sum(remainder * remainder), ("tm", "space")) + epsilon)
        columns.append((coeffs, height))
        vectors.append(remainder / height)
    along_first = columns[0][0][0]
    height_one = columns[0][1]
    cross_first = columns[1][0][0]
    along_second = columns[1][0][1]
    height_two = columns[1][1]
    radius_one = jnp.sqrt(along_first * along_first + height_one * height_one)
    cosine_one = along_first / radius_one
    sine_one = height_one / radius_one
    upper_right = cosine_one * cross_first + sine_one * along_second
    pivot_two = cosine_one * along_second - sine_one * cross_first
    radius_two = jnp.sqrt(pivot_two * pivot_two + height_two * height_two)
    weight_two = -(norm_source * sine_one) * (pivot_two / radius_two) / radius_two
    weight_one = (norm_source * cosine_one - upper_right * weight_two) / radius_one
    adjoint = weight_one * solutions[0] + weight_two * solutions[1]
    residual = source - weight_one * outputs[0] - weight_two * outputs[1]
    return (adjoint, residual)


def solution(mesh):
    in_specs = (
        P("tm", None, "space"),
        P("tm", None, "space"),
        P("space", None, None),
        P(None, "space"),
        P(None, "space", None),
        P(None, "space"),
        P("space", None),
    )
    out_specs = (P("tm", None, "space"), P("tm", None, "space"))
    return jax.shard_map(shards, mesh=mesh, in_specs=in_specs, out_specs=out_specs, check_vma=False)
```

profile of v0, /device:TPU:1, one launch (start us, length us, event | category | flops | bytes accessed | tf_op | source)
XLA Modules:
  0.0 951.8 jit_solution(8771441311318364907)
XLA Ops:
  0.7 1.5 multiply_reduce_fusion.5
  2.2 81.4 %psum.56 = f32[]{:T(128)} all-reduce(f32[]{:T(128)} %multiply_reduce_fusion.5), channel_id=1, replica_groups=mesh['tm'=32,'space'=8] {'tm','space'}, use_global_device_ids=true, to_apply=%region_1.0 | all-reduce | flops 1 | bytes 8 | tf_op jit(solution)/shard_map/psum | solution.py:119
  84.2 0.9 copy_divide_fusion
  85.1 5.7 while.104
  85.1 0.7 bitcast_add_fusion.6
  85.8 0.7 bitcast_add_fusion.6
  86.6 0.7 bitcast_add_fusion.6
  87.3 0.7 bitcast_add_fusion.6
  88.0 0.7 bitcast_add_fusion.6
  88.7 0.7 bitcast_add_fusion.6
  89.4 0.7 bitcast_add_fusion.6
  90.1 0.7 bitcast_add_fusion.6
  90.8 35.1 %all-gather.4 = f32[32,320,8]{1,2,0:T(8,128)S(1)} all-gather(f32[1,320,8]{1,2,0:T(8,128)S(1)} %bitcast.208), channel_id=2, replica_groups=mesh['tm'=32,'space'=8] {'tm'}, dimensions={0}, use_global_device_ids=true | all-gather | bytes 337920 | tf_op jit(solution)/shard_map/all_gather | solution.py:11
  125.9 36.4 %all-gather.5 = f32[32,320,8]{1,2,0:T(8,128)S(1)} all-gather(f32[1,320,8]{1,2,0:T(8,128)S(1)} %bitcast.209), channel_id=3, replica_groups=mesh['tm'=32,'space'=8] {'tm'}, dimensions={0}, use_global_device_ids=true | all-gather | bytes 337920 | tf_op jit(solution)/shard_map/all_gather | solution.py:11
  162.3 1.5 while.105
  163.8 112.4 %psum.57 = f32[320,8]{0,1:T(8,128)S(1)} all-reduce(f32[320,8]{0,1:T(8,128)S(1)} %divide_select_fusion.1), channel_id=1, replica_groups=mesh['tm'=32,'space'=8] {'tm'}, use_global_device_ids=true, to_apply=%region_6.7 | all-reduce | flops 2560 | bytes 20480 | tf_op jit(solution)/shard_map/psum | solution.py:29
  276.3 5.7 while.102
  276.3 0.7 bitcast_dynamic-update-slice_fusion.2
  284.1 52.4 %collective-permute-start = (f32[8,320,2]{1,0,2:T(8,128)S(1)}, f32[8,320,2]{1,0,2:T(8,128)S(1)}, u32[]{:S(2)}, u32[]{:S(2)}) collective-permute-start(f32[8,320,2]{1,0,2:T(8,128)S(1)} %convolution_bitcast_fusion.2), channel_id=1, source_target_pairs={{0,1},{1,2},{2,3},{3,4},{4,5},{5,6},{6,7},{7,0},{8,9},{9,10},{10,1... | collective-permute-start | bytes 61448 | tf_op jit(solution)/shard_map/ppermute | solution.py:39
  338.6 0.8 collective-permute-start.1
  339.4 18.7 %reshape.266 = bf16[8,7,320,320]{3,2,0,1:T(8,128)(2,1)} reshape(bf16[8,7,102400]{2,0,1:T(8,128)(2,1)} %param.21) | data formatting | bytes 22937600 | tf_op jit(solution)/shard_map/reshape | solution.py:89
  358.1 8.6 fusion.6
  367.5 0.8 scatter_fusion
  368.3 0.8 scatter_fusion.1
  369.1 0.8 scatter_fusion.2
  369.9 0.8 scatter_fusion.3
  370.8 0.8 scatter_fusion.4
  371.6 0.8 scatter_fusion.5
  374.8 73.6 %psum.58 = f32[]{:T(128)} all-reduce(f32[]{:T(128)} %multiply_reduce_fusion.4), channel_id=1, replica_groups=mesh['tm'=32,'space'=8] {'tm','space'}, use_global_device_ids=true, to_apply=%region_19.20 | all-reduce | flops 1 | bytes 8 | tf_op jit(solution)/shard_map/psum | solution.py:133
  448.4 1.2 multiply_reduce_fusion.3
  449.6 74.3 %psum.59 = f32[]{:T(128)} all-reduce(f32[]{:T(128)} %multiply_reduce_fusion.3), channel_id=1, replica_groups=mesh['tm'=32,'space'=8] {'tm','space'}, use_global_device_ids=true, to_apply=%region_21.22 | all-reduce | flops 1 | bytes 8 | tf_op jit(solution)/shard_map/psum | solution.py:137
  525.2 5.7 while.106
  525.3 0.7 bitcast_add_fusion.7
  526.0 0.7 bitcast_add_fusion.7
  526.7 0.7 bitcast_add_fusion.7
  527.4 0.7 bitcast_add_fusion.7
  528.1 0.7 bitcast_add_fusion.7
  528.8 0.7 bitcast_add_fusion.7
  529.5 0.7 bitcast_add_fusion.7
  530.3 0.7 bitcast_add_fusion.7
  531.0 36.6 %all-gather.6 = f32[32,320,8]{1,2,0:T(8,128)S(1)} all-gather(f32[1,320,8]{1,2,0:T(8,128)S(1)} %bitcast.206), channel_id=4, replica_groups=mesh['tm'=32,'space'=8] {'tm'}, dimensions={0}, use_global_device_ids=true | all-gather | bytes 337920 | tf_op jit(solution)/shard_map/all_gather | solution.py:11
  567.6 35.3 %all-gather.7 = f32[32,320,8]{1,2,0:T(8,128)S(1)} all-gather(f32[1,320,8]{1,2,0:T(8,128)S(1)} %bitcast.207), channel_id=5, replica_groups=mesh['tm'=32,'space'=8] {'tm'}, dimensions={0}, use_global_device_ids=true | all-gather | bytes 337920 | tf_op jit(solution)/shard_map/all_gather | solution.py:11
  602.9 1.5 while.107
  604.4 113.0 %psum.60 = f32[320,8]{0,1:T(8,128)S(1)} all-reduce(f32[320,8]{0,1:T(8,128)S(1)} %divide_select_fusion), channel_id=1, replica_groups=mesh['tm'=32,'space'=8] {'tm'}, use_global_device_ids=true, to_apply=%region_26.27 | all-reduce | flops 2560 | bytes 20480 | tf_op jit(solution)/shard_map/psum | solution.py:29
  717.5 6.7 while.103
  717.5 0.7 fusion.38
  718.3 0.7 fusion.38
  719.2 0.7 fusion.38
  720.0 0.7 fusion.38
  720.8 0.7 fusion.38
  721.7 0.7 fusion.38
  722.5 0.7 fusion.38
  723.4 0.7 fusion.38
  724.2 8.6 convolution_bitcast_fusion
  734.3 52.8 %collective-permute-start.2 = (f32[8,320,2]{1,0,2:T(8,128)S(1)}, f32[8,320,2]{1,0,2:T(8,128)S(1)}, u32[]{:S(2)}, u32[]{:S(2)}) collective-permute-start(f32[8,320,2]{1,0,2:T(8,128)S(1)} %convolution_bitcast_fusion.1), channel_id=1, source_target_pairs={{0,1},{1,2},{2,3},{3,4},{4,5},{5,6},{6,7},{7,0},{8,9},{9,10},{10,1... | collective-permute-start | bytes 61448 | tf_op jit(solution)/shard_map/ppermute | solution.py:39
  789.9 0.8 scatter_fusion.9
  790.7 0.8 scatter_fusion.10
  791.5 0.8 scatter_fusion.11
  792.4 0.8 scatter_fusion.12
  793.2 0.8 scatter_fusion.13
  794.0 0.8 scatter_fusion.14
  797.3 73.4 %all-reduce = (f32[]{:T(128)}, f32[]{:T(128)}) all-reduce(f32[]{:T(128)} %get-tuple-element.881, f32[]{:T(128)} %get-tuple-element.880), channel_id=1, replica_groups=mesh['tm'=32,'space'=8] {'tm','space'}, use_global_device_ids=true, to_apply=%region_41.42 | all-reduce | flops 2 | bytes 16 | tf_op jit(solution)/shard_map/psum | solution.py:133
  871.9 2.0 multiply_reduce_fusion
  875.2 74.3 %psum.63 = f32[]{:T(128)} all-reduce(f32[]{:T(128)} %multiply_reduce_fusion), channel_id=1, replica_groups=mesh['tm'=32,'space'=8] {'tm','space'}, use_global_device_ids=true, to_apply=%region_43.44 | all-reduce | flops 1 | bytes 8 | tf_op jit(solution)/shard_map/psum | solution.py:137
  (156 shorter events, 20.6 us)
Async XLA Ops:
  90.8 191.2 %copy-start.3 = (s32[2,2]{1,0:T(2,128)S(1)}, s32[2,2]{1,0:T(2,128)}, u32[]{:S(2)}) copy-start(s32[2,2]{1,0:T(2,128)} %param.24) | copy-start | bytes 52
  90.8 191.2 %copy-start.1 = (bf16[2,2,102400]{2,1,0:T(2,128)(2,1)S(1)}, bf16[2,2,102400]{2,1,0:T(2,128)(2,1)}, u32[]{:S(2)}) copy-start(bf16[2,2,102400]{2,1,0:T(2,128)(2,1)} %param.23) | copy-start | bytes 2457604
  283.2 53.3 %copy-start.4 = (s32[1,2]{1,0:T(1,128)S(1)}, s32[1,2]{1,0:T(1,128)}, u32[]{:S(2)}) copy-start(s32[1,2]{1,0:T(1,128)} %param.25) | copy-start | bytes 28
  284.1 88.3 %collective-permute-start = (f32[8,320,2]{1,0,2:T(8,128)S(1)}, f32[8,320,2]{1,0,2:T(8,128)S(1)}, u32[]{:S(2)}, u32[]{:S(2)}) collective-permute-start(f32[8,320,2]{1,0,2:T(8,128)S(1)} %convolution_bitcast_fusion.2), channel_id=1, source_target_pairs={{0,1},{1,2},{2,3},{3,4},{4,5},{5,6},{6,7},{7,0},{8,9},{9,10},{10,1... | collective-permute-start | bytes 61448 | tf_op jit(solution)/shard_map/ppermute | solution.py:39
  338.6 35.0 %collective-permute-start.1 = (f32[8,320,2]{1,0,2:T(8,128)S(1)}, f32[8,320,2]{1,0,2:T(8,128)S(1)}, u32[]{:S(2)}, u32[]{:S(2)}) collective-permute-start(f32[8,320,2]{1,0,2:T(8,128)S(1)} %scatter_fusion.7), channel_id=1, source_target_pairs={{1,0},{2,1},{3,2},{4,3},{5,4},{6,5},{7,6},{0,7},{9,8},{10,9},{11,1... | collective-permute-start | bytes 61448 | tf_op jit(solution)/shard_map/ppermute | solution.py:41
  358.1 8.6 copy-start
  366.7 0.7 copy-start.2
  734.3 60.6 %collective-permute-start.2 = (f32[8,320,2]{1,0,2:T(8,128)S(1)}, f32[8,320,2]{1,0,2:T(8,128)S(1)}, u32[]{:S(2)}, u32[]{:S(2)}) collective-permute-start(f32[8,320,2]{1,0,2:T(8,128)S(1)} %convolution_bitcast_fusion.1), channel_id=1, source_target_pairs={{0,1},{1,2},{2,3},{3,4},{4,5},{5,6},{6,7},{7,0},{8,9},{9,10},{10,1... | collective-permute-start | bytes 61448 | tf_op jit(solution)/shard_map/ppermute | solution.py:39
  788.0 8.0 collective-permute-start.3
where the time goes:
time: 956 us; the launch traced here: 952 us
  blocking collectives  746 us (78%)
  starting transfers between devices  106 us (11%)
  other arithmetic  43.6 us (5%)
  local copies, waits for them, and re-layouts  27.8 us (3%)
  matrix products  18.4 us (2%)
    psum x2, blocking collectives, spread(): return lax.psum(block, axis)  225 us
    psum x2, blocking collectives, shards(): lax.psum(jnp.sum(remainder * remainder), ('tm', 'space')) + epsilon  149 us
    psum x2, blocking collectives, shards(): coeffs = lax.psum(local_dots, ('tm', 'space'))  147 us
    all_gather x4, blocking collectives, prefix(): everything = jax.tree.map(lambda part: lax.all_gather(part, axis), value)  143 us
    ppermute x2, starting transfers between devices, with_halo(): lax.ppermute(tail, axis, [(i, (i + 1) % count) for i in range(count)])  105 us
    psum x1, blocking collectives, shards(): lax.psum(jnp.sum(source * source), ('tm', 'space')) + epsilon  81.4 us
  transfers between devices with their start and end apart: 4, of which 0 were waited for; matrix products, arithmetic and copies ran while one was open for 4% of the time, Pallas kernels for 0%

commit v1 on v0

v1 whole, which is shorter than its diff:
```python
import jax
import jax.numpy as jnp
from jax import lax
from jax.experimental import pallas as pl
from jax.experimental.pallas import tpu as pltpu
from jax.sharding import PartitionSpec as P

EPSILON = 1e-06
F32 = jnp.float32
BF16 = jnp.bfloat16
SLABS = 8
ELEMENTS = 8
WIDTH = 320
FACES = 7
ROWS = SLABS * ELEMENTS
PAIRS = WIDTH // 2
DEPTH = PAIRS * ELEMENTS
LANES = 2 * WIDTH
GROUPS = 32
DEVICES = 256
TINY = 1e-30

VMEM = pl.BlockSpec(memory_space=pltpu.VMEM)
SMEM = pl.BlockSpec(memory_space=pltpu.SMEM)
ANY = pl.BlockSpec(memory_space=pl.ANY)


def iota(shape, dim):
    return lax.broadcasted_iota(jnp.int32, shape, dim)


def struct(*shape):
    return jax.ShapeDtypeStruct(shape, F32)


def params(mib):
    return pltpu.CompilerParams(vmem_limit_bytes=mib * 1024 * 1024)


def maps_kernel(source_ref, decay_ref, out_ref):
    product = jnp.ones((ELEMENTS, WIDTH), F32)
    offset = jnp.zeros((ELEMENTS, WIDTH), F32)
    for t in reversed(range(SLABS)):
        offset = source_ref[t] + decay_ref[t] * offset
        product = product * decay_ref[t]
    for j in range(GROUPS):
        out_ref[j, 0:ELEMENTS] = product
        out_ref[j, ELEMENTS:] = offset


def entering_value(mine, product_of, offset_of):
    product = jnp.ones((ELEMENTS, WIDTH), F32)
    offset = jnp.zeros((ELEMENTS, WIDTH), F32)
    for j in reversed(range(GROUPS)):
        offset = offset_of(j) + product_of(j) * offset
        product = product * product_of(j)
    value = offset / (1.0 - product)
    for j in reversed(range(1, GROUPS)):
        value = jnp.where(j > mine, offset_of(j) + product_of(j) * value, value)
    return value


def operate_kernel(first, *refs):
    if first:
        mine, neighbours, owner, pairing, field, decay, maps, blocks, couple = refs[:9]
        refs = refs[9:]
        offset_of = lambda j: maps[j, ELEMENTS:]
    else:
        mine, neighbours, owner, pairing, field, decay, maps, offsets, blocks, couple = refs[:10]
        refs = refs[10:]
        offset_of = lambda j: offsets[j]
    chained, local, up, down, raw, weights, spread, total, sems = refs
    copies = [
        pltpu.make_async_copy(blocks.at[f], raw.at[f], sems.at[f]) for f in range(FACES)
    ]
    for copy in copies:
        copy.start()

    value = entering_value(mine[0], lambda j: maps[j, 0:ELEMENTS], offset_of)
    for t in reversed(range(SLABS)):
        value = field[t] + decay[t] * value
        chained[t] = value
    z = chained[...].reshape(ROWS, WIDTH)
    high = z.astype(BF16)
    low = (z - high.astype(F32)).astype(BF16)
    parts = jnp.concatenate([high, low], axis=0)

    row = iota((4 * 2 * SLABS, 2 * ROWS), 0)
    col = iota((4 * 2 * SLABS, 2 * ROWS), 1)
    slot = row // (2 * SLABS)
    at = jnp.where(
        slot < 2,
        jnp.where(slot == 0, owner[0, 0], owner[0, 1]),
        jnp.where(slot == 2, owner[1, 0], owner[1, 1]),
    )
    pick = (row % (2 * SLABS)) * ELEMENTS + at == col
    pick = jnp.where(pick, 1.0, 0.0).astype(BF16)
    picked = jnp.dot(pick, parts, preferred_element_type=F32).astype(BF16)
    for side in range(2):
        for i in range(2):
            k = (2 * side + i) * 2 * SLABS
            both = jnp.dot(
                picked[k : k + 2 * SLABS], couple[side, i], preferred_element_type=F32
            )
            both = both[:SLABS] + both[SLABS:]
            if side == 0:
                up[i] = both
            else:
                down[pairing[0, i]] = both

    span = 1024
    n = iota((256, span), 0)
    lane = iota((256, span), 1)
    same = jnp.where(iota((128, 128), 0) // 8 == iota((128, 128), 1) // 8, 1.0, 0.0).astype(BF16)
    own = iota((2 * ROWS, DEPTH), 0) % ELEMENTS == iota((2 * ROWS, DEPTH), 1) % ELEMENTS
    for b in range(2):
        expand = jnp.where(n == 2 * (lane // ELEMENTS) + b, 1.0, 0.0).astype(BF16)
        wide = jnp.concatenate(
            [
                jnp.dot(parts[:, :256], expand, preferred_element_type=F32),
                jnp.dot(parts[:, 256:], expand[:64, :256], preferred_element_type=F32),
            ],
            axis=1,
        )
        wide = jnp.where(own, wide, 0.0).astype(BF16)
        spread[b * 2 * ROWS : (b + 1) * 2 * ROWS] = jnp.dot(
            same, wide, preferred_element_type=F32
        ).astype(BF16)

    total[...] = jnp.zeros_like(total)
    e = iota((2 * ELEMENTS, 128), 1) % ELEMENTS
    d = iota((2 * ELEMENTS, 128), 0) % ELEMENTS

    def face(f, carry):
        pltpu.make_async_copy(blocks.at[f], raw.at[f], sems.at[f]).wait()
        to = e
        for k in range(ELEMENTS):
            to = jnp.where((e == k) & (f > 0), neighbours[jnp.maximum(f - 1, 0), k], to)
        mask = jnp.where(to == d, 1.0, 0.0).astype(BF16)
        mask = jnp.concatenate([mask] * (DEPTH // 128), axis=1)
        mask = jnp.concatenate([mask] * (4 * ROWS // 16), axis=0)
        for k in range(PAIRS // 2):
            two = [
                raw[f, :, (2 * k + i) * LANES : (2 * k + i + 1) * LANES].astype(F32)
                for i in range(2)
            ]
            weights[k * 16 : (k + 1) * 16] = jnp.concatenate(two, axis=0).astype(BF16)
        total[...] += jnp.dot(spread[...] * mask, weights[...], preferred_element_type=F32)
        return carry

    lax.fori_loop(0, FACES, face, 0)
    result = (
        total[0:ROWS, :WIDTH]
        + total[ROWS : 2 * ROWS, :WIDTH]
        + (total[2 * ROWS : 3 * ROWS, :] + total[3 * ROWS :, :])[:, WIDTH:]
    )
    local[...] = result.reshape(SLABS, ELEMENTS, WIDTH)


def operate(first, scalars, field, decay, gathered, blocks, couple):
    def kernel(*refs):
        operate_kernel(first, *refs)

    return pl.pallas_call(
        kernel,
        out_shape=(
            struct(SLABS, ELEMENTS, WIDTH),
            struct(SLABS, ELEMENTS, WIDTH),
            struct(2, SLABS, WIDTH),
            struct(2, SLABS, WIDTH),
        ),
        in_specs=[SMEM] * 4 + [VMEM] * (2 + len(gathered)) + [ANY, VMEM],
        out_specs=(VMEM,) * 4,
        scratch_shapes=[
            pltpu.VMEM((FACES, ELEMENTS, WIDTH * WIDTH), BF16),
            pltpu.VMEM((DEPTH, LANES), BF16),
            pltpu.VMEM((4 * ROWS, DEPTH), BF16),
            pltpu.VMEM((4 * ROWS, LANES), F32),
            pltpu.SemaphoreType.DMA((FACES,)),
        ],
        compiler_params=params(48),
    )(*scalars, field, decay, *gathered, blocks, couple)


def add_halo(owner, pairing, local, below, above, out):
    at = iota((ELEMENTS, WIDTH), 0)
    for t in range(SLABS):
        value = local[t]
        for k in range(2):
            value = value + jnp.where(
                at == owner[1, k], below[pairing[0, k], pl.ds(t, 1)], 0.0
            )
            value = value + jnp.where(at == owner[0, k], above[k, pl.ds(t, 1)], 0.0)
        out[t] = value


def middle_kernel(owner, pairing, local, below, above, decay, image, out):
    add_halo(owner, pairing, local, below, above, image)
    offset = jnp.zeros((ELEMENTS, WIDTH), F32)
    for t in reversed(range(SLABS)):
        offset = image[t] + decay[t] * offset
    for j in range(GROUPS):
        out[j] = offset


def total_of(x):
    return jnp.sum(jnp.sum(x, axis=0), keepdims=True)


def gram_kernel(owner, pairing, local, below, above, source, image0, image1, out):
    add_halo(owner, pairing, local, below, above, image1)
    s = source[...]
    largest = [
        jnp.maximum(jnp.max(jnp.max(jnp.abs(image[...]), axis=0), keepdims=True), TINY)
        for image in (image0, image1)
    ]
    one = jnp.ones((1, 1), F32)
    g0 = image0[...] * (1.0 / largest[0])
    g1 = image1[...] * (1.0 / largest[1])
    entries = [
        (total_of(s * s), one, one),
        (total_of(s * g0), largest[0], one),
        (total_of(g0 * g0), largest[0], largest[0]),
        (total_of(s * g1), largest[1], one),
        (total_of(g0 * g1), largest[0], largest[1]),
        (total_of(g1 * g1), largest[1], largest[1]),
    ]
    lane = iota((8, 128), 1)
    row = jnp.ones((8, 128), F32)
    for k, entry in enumerate(entries):
        for i, value in enumerate(entry):
            row = jnp.where(lane == k + 16 * i, value, row)
    for j in range(DEVICES // 8):
        out[j * 8 : (j + 1) * 8] = row


def last_kernel(gram, source, first_chain, second_chain, image0, image1, adjoint, residual):
    every = gram[...]
    scale_a = pltpu.roll(every, 128 - 16, 1)
    scale_b = pltpu.roll(every, 128 - 32, 1)
    top_a = jnp.max(scale_a, axis=0, keepdims=True)
    top_b = jnp.max(scale_b, axis=0, keepdims=True)
    sums = jnp.sum(every * (scale_a / top_a) * (scale_b / top_b), axis=0, keepdims=True)
    lane = iota((1, 128), 1)

    def entry(row, k):
        return jnp.sum(jnp.where(lane == k, row, 0.0), axis=1, keepdims=True)

    ss, s0, g00, s1, g01, g11 = (entry(sums, k) for k in range(6))
    a0 = entry(top_a, 1)
    a1 = entry(top_a, 3)
    square = ss + EPSILON
    norm = jnp.sqrt(square)
    r0 = a0 / norm
    kappa = EPSILON / square - r0 * (s0 / norm)
    rest = r0 * r0 * g00 + 2.0 * kappa * r0 * (s0 / norm) + kappa * kappa * (ss / square)
    h10 = jnp.sqrt(jnp.maximum(rest, 0.0) + EPSILON)
    beta = 1.0 / (norm * h10)
    b0 = r0 / h10
    b1 = (a1 / norm) / h10
    cross = b0 * b1 * g01 + kappa * beta * b1 * s1
    delta = cross + kappa * (b0 * b0 * g00 + kappa * beta * b0 * s0)
    lost = EPSILON / (h10 * h10)
    h00 = 1.0 - kappa
    h11 = (1.0 - lost) + delta
    near = EPSILON * (1.0 - kappa) * beta
    h01 = (b1 * s1 + kappa * b0 * s0 + near) / norm
    c1 = kappa + lost - delta
    mu = (b1 * s1 + beta * EPSILON) / square
    rest = (
        b1 * b1 * g11
        + c1 * c1 * (1.0 - lost)
        + mu * mu * ss
        + 2.0 * c1 * cross
        - 2.0 * mu * b1 * s1
        - 2.0 * c1 * mu * near
    )
    h21 = jnp.sqrt(jnp.maximum(rest, 0.0) + EPSILON)
    radius_one = jnp.sqrt(h00 * h00 + h10 * h10)
    cosine = h00 / radius_one
    sine = h10 / radius_one
    upper = cosine * h01 + sine * h11
    pivot = cosine * h11 - sine * h01
    radius_two = jnp.sqrt(pivot * pivot + h21 * h21)
    y1 = -(norm * sine) * (pivot / radius_two) / radius_two
    y0 = (norm * cosine - upper * y1) / radius_one
    p0 = y0 / norm
    p1 = y1 * beta
    p2 = p1 * kappa
    for t in range(SLABS):
        adjoint[t] = (p0 + p2) * first_chain[t] + p1 * second_chain[t]
        residual[t] = (
            (1.0 - p0 - p2) * source[t] - (p0 + p1 + p2) * image0[t] - p1 * image1[t]
        )


def shards(
    source, decay_rate, blocks, neighbours, interface_jacobian_blocks, face_element_owner, pairing
):
    source = jnp.transpose(source, (0, 2, 1))
    decay = jnp.transpose(decay_rate, (0, 2, 1))
    blocks = jnp.transpose(blocks, (1, 0, 2))
    couple = interface_jacobian_blocks.reshape(2, 2, WIDTH, WIDTH)
    mine = lax.axis_index("tm").astype(jnp.int32).reshape(1)
    scalars = (mine, neighbours, face_element_owner, pairing)
    owner_pairing = (face_element_owner, pairing)
    field_shape = struct(SLABS, ELEMENTS, WIDTH)
    upward = [(i, (i + 1) % 8) for i in range(8)]
    downward = [((i + 1) % 8, i) for i in range(8)]

    maps = pl.pallas_call(
        maps_kernel,
        out_shape=struct(GROUPS, 2 * ELEMENTS, WIDTH),
        in_specs=[VMEM] * 2,
        out_specs=VMEM,
    )(source, decay)
    maps = lax.all_to_all(maps, "tm", 0, 0, tiled=True)
    chain0, local, up, down = operate(True, scalars, source, decay, (maps,), blocks, couple)
    below = lax.ppermute(up, "space", upward)
    above = lax.ppermute(down, "space", downward)
    image0, offsets = pl.pallas_call(
        middle_kernel,
        out_shape=(field_shape, struct(GROUPS, ELEMENTS, WIDTH)),
        in_specs=[SMEM] * 2 + [VMEM] * 4,
        out_specs=(VMEM,) * 2,
    )(*owner_pairing, local, below, above, decay)
    offsets = lax.all_to_all(offsets, "tm", 0, 0, tiled=True)
    chain1, local, up, down = operate(
        False, scalars, image0, decay, (maps, offsets), blocks, couple
    )
    below = lax.ppermute(up, "space", upward)
    above = lax.ppermute(down, "space", downward)
    image1, gram = pl.pallas_call(
        gram_kernel,
        out_shape=(field_shape, struct(DEVICES, 128)),
        in_specs=[SMEM] * 2 + [VMEM] * 5,
        out_specs=(VMEM,) * 2,
    )(*owner_pairing, local, below, above, source, image0)
    gram = lax.all_to_all(gram, ("tm", "space"), 0, 0, tiled=True)
    adjoint, residual = pl.pallas_call(
        last_kernel,
        out_shape=(field_shape, field_shape),
        in_specs=[VMEM] * 6,
        out_specs=(VMEM,) * 2,
    )(gram, source, chain0, chain1, image0, image1)
    return (jnp.transpose(adjoint, (0, 2, 1)), jnp.transpose(residual, (0, 2, 1)))


def solution(mesh):
    in_specs = (
        P("tm", None, "space"),
        P("tm", None, "space"),
        P("space", None, None),
        P(None, "space"),
        P(None, "space", None),
        P(None, "space"),
        P("space", None),
    )
    out_specs = (P("tm", None, "space"), P("tm", None, "space"))
    return jax.shard_map(shards, mesh=mesh, in_specs=in_specs, out_specs=out_specs, check_vma=False)
```

time: 956 us -> 119 us (0.12)
  blocking collectives: 746 us -> 39.6 us
  starting transfers between devices: 106 us -> 21.1 us
  other arithmetic: 43.6 us -> 0 us
  Pallas kernels: 0 us -> 23.4 us
  waiting for transfers between devices: 0.01 us -> 23.3 us
  matrix products: 18.4 us -> 0 us
  local copies, waits for them, and re-layouts: 27.8 us -> 10.5 us
    psum x7 -> x0, blocking collectives: 602 us -> none  [the longest x2 225 us: spread(): return lax.psum(block, axis)]
    all_gather x4 -> x0, blocking collectives: 143 us -> none  [prefix(): everything = jax.tree.map(lambda part: lax.all_gather(part, axis), value)]
    ppermute x4, starting transfers between devices: 106 us -> 9.02 us  [the longest x2 8.67 us: shards(): below = lax.ppermute(up, 'space', upward)]
    all_to_all x0 -> x2, blocking collectives: none -> 39.6 us  [the longest x1 23 us: shards(): gram = lax.all_to_all(gram, ('tm', 'space'), 0, 0, tiled=True)]
    pallas_call x0 -> x6, Pallas kernels: none -> 23.4 us  [the longest x2 15.4 us: operate(): pl.pallas_call(kernel, out_shape=(struct(SLABS, ELEMENTS, WIDTH), struct(...]
    dot_general x6 -> x0, matrix products: 18.4 us -> none  [the longest x2 17.2 us: apply_spatial(): jnp.einsum('efnm,tne->tfme', block_data, field, precision=lax.Precision.H...]
    add x27 -> x0, other arithmetic: 17.2 us -> none  [the longest x16 11.4 us: compose_step(): return ((product * slab_rate, slab_value + slab_rate * offset), None)]
    all_to_all x0 -> x1, waiting for transfers between devices: none -> 17.2 us  [shards(): maps = lax.all_to_all(maps, 'tm', 0, 0, tiled=True)]
  transfers between devices with their start and end apart: 4 -> 5, of which waited for: 0 -> 5; matrix products, arithmetic and copies ran while one was open for 4% -> 2% of each run, Pallas kernels for 0% -> 0%
where the time goes in v1:
time: 119 us
  blocking collectives  39.6 us (33%)
  Pallas kernels  23.4 us (20%)
  waiting for transfers between devices  23.3 us (20%)
  starting transfers between devices  21.1 us (18%)
  local copies, waits for them, and re-layouts  10.5 us (9%)
    all_to_all x1, blocking collectives, shards(): gram = lax.all_to_all(gram, ('tm', 'space'), 0, 0, tiled=True)  23 us
    all_to_all x1, waiting for transfers between devices, shards(): maps = lax.all_to_all(maps, 'tm', 0, 0, tiled=True)  17.2 us
    all_to_all x1, blocking collectives, shards(): offsets = lax.all_to_all(offsets, 'tm', 0, 0, tiled=True)  16.6 us
    pallas_call x2, Pallas kernels, operate(): pl.pallas_call(kernel, out_shape=(struct(SLABS, ELEMENTS, WIDTH), struct(...  15.4 us
    all_to_all x1, starting transfers between devices, shards(): maps = lax.all_to_all(maps, 'tm', 0, 0, tiled=True)  12 us
    ppermute x2, starting transfers between devices, shards(): below = lax.ppermute(up, 'space', upward)  8.67 us
    unnamed x36, local copies, waits for them, and re-layouts  8.46 us
    ppermute x2, waiting for transfers between devices, shards(): above = lax.ppermute(down, 'space', downward)  4.52 us
  transfers between devices with their start and end apart: 5, of which 5 were waited for; matrix products, arithmetic and copies ran while one was open for 2% of the time, Pallas kernels for 0%

profile of v1, /device:TPU:1, one launch (start us, length us, event | category | flops | bytes accessed | tf_op | source)
XLA Modules:
  0.0 118.7 jit_solution(12668039089401451008)
XLA Ops:
  0.6 0.0 copy-start.1
  0.6 0.0 copy-start.13
  0.7 0.0 copy-start.11
  0.7 0.0 copy-start.9
  0.7 1.9 %shard_map.86 = f32[32,16,320]{2,1,0:T(8,128)} custom-call(f32[8,8,320]{2,1,0:T(8,128)} %bitcast.14, f32[8,8,320]{2,1,0:T(8,128)} %bitcast.10), custom_call_target="tpu_custom_call" | custom-call | tf_op jit(solution)/shard_map/pallas_call | solution.py:311
  2.6 12.0 %all-to-all-start = ((f32[32,16,320]{2,1,0:T(8,128)}), f32[32,16,320]{2,1,0:T(8,128)S(1)}, u32[]{:S(2)}, u32[]{:S(2)}) async-start(f32[32,16,320]{2,1,0:T(8,128)} %shard_map.86), calls=%async_computation | async-start | bytes 1572864 | tf_op jit(solution)/shard_map/all_to_all | solution.py:317
  14.7 2.1 %reshape.13.refs_8_.refs_9_ = bf16[2,2,320,320]{3,2,1,0:T(8,128)(2,1)S(1)} reshape(bf16[2,2,102400]{2,1,0:T(2,128)(2,1)} %param.11) | data formatting | bytes 1638400 | tf_op jit(solution)/shard_map/reshape | solution.py:303
  16.8 17.2 %all-to-all-done.refs_6_ = f32[32,16,320]{2,1,0:T(8,128)S(1)} async-done(((f32[32,16,320]{2,1,0:T(8,128)}), f32[32,16,320]{2,1,0:T(8,128)S(1)}, u32[]{:S(2)}, u32[]{:S(2)}) %all-to-all-start) | async-done | bytes 655392 | tf_op jit(solution)/shard_map/all_to_all | solution.py:317
  33.9 0.0 copy-start
  33.9 0.9 copy-done
  34.8 0.0 copy-start.2
  34.8 0.9 copy-done.2
  35.7 0.0 copy-start.8
  35.7 0.7 copy-done.8
  36.4 0.0 copy-start.10
  36.4 0.7 copy-done.10
  37.1 0.0 copy-start.12
  37.1 0.7 copy-done.12
  37.7 7.7 %shard_map.87 = (f32[8,8,320]{2,1,0:T(8,128)S(1)}, f32[8,8,320]{2,1,0:T(8,128)S(1)}, f32[2,8,320]{2,1,0:T(8,128)S(1)}, f32[2,8,320]{2,1,0:T(8,128)S(1)}) custom-call(s32[1]{0:T(128)} %bitcast.refs_0_, s32[6,8]{1,0:T(8,128)S(1)} %copy-done.8, s32[2,2]{1,0:T(2,128)S(1)} %copy-done.10, s32[1,2]{1,0:T(1,128)S(1)} %copy-done.12, f32[8,8,320]{2,1,0:T(8,128)S(1)} %bitcast.17, ...), custom_call_target="tpu_custom_call" | custom-call | tf_op jit(solution)/shard_map/pallas_call | solution.py:164
  45.4 0.0 copy-start.4
  45.4 0.6 copy-done.4
  46.1 0.0 copy-start.7
  46.1 0.6 copy-done.7
  46.7 6.2 %collective-permute-start = (f32[2,8,320]{2,1,0:T(8,128)S(1)}, f32[2,8,320]{2,1,0:T(8,128)S(1)}, u32[]{:S(2)}, u32[]{:S(2)}) collective-permute-start(f32[2,8,320]{2,1,0:T(8,128)S(1)} %get-tuple-element.17), channel_id=1, source_target_pairs={{0,1},{1,2},{2,3},{3,4},{4,5},{5,6},{6,7},{7,0},{8,9},{9,10},{10,1... | collective-permute-start | bytes 61448 | tf_op jit(solution)/shard_map/ppermute | solution.py:319
  52.9 0.0 collective-permute-start.1
  52.9 0.9 collective-permute-done.below
  53.8 0.0 copy-start.14
  53.8 2.3 %collective-permute-done.1.above = f32[2,8,320]{2,1,0:T(8,128)S(1)} collective-permute-done((f32[2,8,320]{2,1,0:T(8,128)S(1)}, f32[2,8,320]{2,1,0:T(8,128)S(1)}, u32[]{:S(2)}, u32[]{:S(2)}) %collective-permute-start.1) | collective-permute-done | bytes 20512 | tf_op jit(solution)/shard_map/ppermute | solution.py:320
  56.1 0.0 copy-start.16
  56.1 0.0 copy-done.14
  56.1 0.6 copy-done.16
  56.7 1.8 %shard_map.88 = (f32[8,8,320]{2,1,0:T(8,128)}, f32[32,8,320]{2,1,0:T(8,128)}) custom-call(s32[2,2]{1,0:T(2,128)} %owner.3, s32[1,2]{1,0:T(1,128)} %pairing.3, f32[8,8,320]{2,1,0:T(8,128)} %copy-done.7, f32[2,8,320]{2,1,0:T(8,128)} %copy-done.14, f32[2,8,320]{2,1,0:T(8,128)} %copy-done.16, f32[8,8,320]{2,1,0:T(8,128)} %bitcast.11), custom_call_target="tpu_custom_call" | custom-call | tf_op jit(solution)/shard_map/pallas_call | solution.py:321
  58.6 16.6 %all_to_all.21.refs_7_ = f32[32,8,320]{2,1,0:T(8,128)S(1)} all-to-all(f32[32,8,320]{2,1,0:T(8,128)} %get-tuple-element.20), channel_id=1, replica_groups=mesh['tm'=32,'space'=8] {'tm'}, dimensions={0} | all-to-all | bytes 655360 | tf_op jit(solution)/shard_map/all_to_all | solution.py:327
  75.2 0.0 copy-done.1
  75.2 0.0 copy-done.13
  75.2 0.0 copy-done.11
  75.2 0.0 copy-done.9
  75.2 0.0 copy-start.3
  75.2 0.9 copy-done.3
  76.1 7.7 %shard_map.89 = (f32[8,8,320]{2,1,0:T(8,128)S(1)}, f32[8,8,320]{2,1,0:T(8,128)S(1)}, f32[2,8,320]{2,1,0:T(8,128)S(1)}, f32[2,8,320]{2,1,0:T(8,128)S(1)}) custom-call(s32[1]{0:T(128)} %bitcast.refs_0_, s32[6,8]{1,0:T(8,128)S(1)} %copy-done.9, s32[2,2]{1,0:T(2,128)S(1)} %copy-done.11, s32[1,2]{1,0:T(1,128)S(1)} %copy-done.13, f32[8,8,320]{2,1,0:T(8,128)S(1)} %copy-done.3, ...), custom_call_target="tpu_custom_call" | custom-call | tf_op jit(solution)/shard_map/pallas_call | solution.py:164
  83.8 0.0 copy-start.5
  83.8 0.6 copy-done.5
  84.4 0.0 copy-start.6
  84.4 0.6 copy-done.6
  85.1 2.5 %collective-permute-start.2 = (f32[2,8,320]{2,1,0:T(8,128)S(1)}, f32[2,8,320]{2,1,0:T(8,128)S(1)}, u32[]{:S(2)}, u32[]{:S(2)}) collective-permute-start(f32[2,8,320]{2,1,0:T(8,128)S(1)} %get-tuple-element.22), channel_id=1, source_target_pairs={{0,1},{1,2},{2,3},{3,4},{4,5},{5,6},{6,7},{7,0},{8,9},{9,10},{10,1... | collective-permute-start | bytes 61448 | tf_op jit(solution)/shard_map/ppermute | solution.py:331
  87.6 0.3 collective-permute-start.3
  87.9 0.7 collective-permute-done.2.below
  88.6 0.0 copy-start.15
  88.6 2.2 %collective-permute-done.3.above = f32[2,8,320]{2,1,0:T(8,128)S(1)} collective-permute-done((f32[2,8,320]{2,1,0:T(8,128)S(1)}, f32[2,8,320]{2,1,0:T(8,128)S(1)}, u32[]{:S(2)}, u32[]{:S(2)}) %collective-permute-start.3) | collective-permute-done | bytes 20512 | tf_op jit(solution)/shard_map/ppermute | solution.py:332
  90.8 0.0 copy-start.17
  90.8 0.0 copy-done.15
  90.8 0.6 copy-done.17
  91.4 2.0 %shard_map.90 = (f32[8,8,320]{2,1,0:T(8,128)}, f32[256,128]{1,0:T(8,128)}) custom-call(s32[2,2]{1,0:T(2,128)} %owner.3, s32[1,2]{1,0:T(1,128)} %pairing.3, f32[8,8,320]{2,1,0:T(8,128)} %copy-done.6, f32[2,8,320]{2,1,0:T(8,128)} %copy-done.15, f32[2,8,320]{2,1,0:T(8,128)} %copy-done.17, f32[8,8,320]{2,1,0:T(8,128)} %bitcast.15, ...), custom_call_target="tpu_custom_call" | custom-call | tf_op jit(solution)/shard_map/pallas_call | solution.py:333
  93.5 23.0 %all_to_all.22 = f32[256,1,128]{2,1,0:T(1,128)} all-to-all(f32[256,1,128]{2,1,0:T(1,128)} %bitcast.21), channel_id=1, replica_groups=mesh['tm'=32,'space'=8] {'tm','space'}, dimensions={0} | all-to-all | bytes 262144 | tf_op jit(solution)/shard_map/all_to_all | solution.py:339
  116.5 2.2 %shard_map.91 = (f32[8,8,320]{2,1,0:T(8,128)}, f32[8,8,320]{2,1,0:T(8,128)}) custom-call(f32[256,128]{1,0:T(8,128)} %bitcast.20, f32[8,8,320]{2,1,0:T(8,128)} %bitcast.16, f32[8,8,320]{2,1,0:T(8,128)} %copy-done.4, f32[8,8,320]{2,1,0:T(8,128)} %copy-done.5, f32[8,8,320]{2,1,0:T(8,128)} %get-tuple-element.19.refs_4_.image0, f32[8,8,320]{2,1,0:T(8,128)} %get-tuple-element.27.image1), custom_call_target="tpu_custom_call" | custom-call | tf_op jit(solution)/shard_map/pallas_call | solution.py:340
Async XLA Ops:
  0.6 74.6 %copy-start.1 = (f32[8,320,8]{1,2,0:T(8,128)S(1)}, f32[8,320,8]{1,2,0:T(8,128)}, u32[]{:S(2)}) copy-start(f32[8,320,8]{1,2,0:T(8,128)} %param.8) | copy-start | bytes 245764
  0.6 74.5 %copy-start.13 = (s32[1,2]{1,0:T(1,128)S(1)}, s32[1,2]{1,0:T(1,128)}, u32[]{:S(2)}) copy-start(s32[1,2]{1,0:T(1,128)} %pairing.3) | copy-start | bytes 28
  0.7 74.5 %copy-start.11 = (s32[2,2]{1,0:T(2,128)S(1)}, s32[2,2]{1,0:T(2,128)}, u32[]{:S(2)}) copy-start(s32[2,2]{1,0:T(2,128)} %owner.3) | copy-start | bytes 52
  0.7 74.5 %copy-start.9 = (s32[6,8]{1,0:T(8,128)S(1)}, s32[6,8]{1,0:T(8,128)}, u32[]{:S(2)}) copy-start(s32[6,8]{1,0:T(8,128)} %refs_1_.3) | copy-start | bytes 580
  2.6 31.3 %all-to-all-start = ((f32[32,16,320]{2,1,0:T(8,128)}), f32[32,16,320]{2,1,0:T(8,128)S(1)}, u32[]{:S(2)}, u32[]{:S(2)}) async-start(f32[32,16,320]{2,1,0:T(8,128)} %shard_map.86), calls=%async_computation | async-start | bytes 1572864 | tf_op jit(solution)/shard_map/all_to_all | solution.py:317
  33.9 0.9 copy-start
  34.8 0.9 copy-start.2
  35.7 0.7 copy-start.8
  36.4 0.7 copy-start.10
  37.1 0.7 copy-start.12
  45.4 0.6 copy-start.4
  46.1 0.6 copy-start.7
  46.7 7.1 %collective-permute-start = (f32[2,8,320]{2,1,0:T(8,128)S(1)}, f32[2,8,320]{2,1,0:T(8,128)S(1)}, u32[]{:S(2)}, u32[]{:S(2)}) collective-permute-start(f32[2,8,320]{2,1,0:T(8,128)S(1)} %get-tuple-element.17), channel_id=1, source_target_pairs={{0,1},{1,2},{2,3},{3,4},{4,5},{5,6},{6,7},{7,0},{8,9},{9,10},{10,1... | collective-permute-start | bytes 61448 | tf_op jit(solution)/shard_map/ppermute | solution.py:319
  52.9 3.3 %collective-permute-start.1 = (f32[2,8,320]{2,1,0:T(8,128)S(1)}, f32[2,8,320]{2,1,0:T(8,128)S(1)}, u32[]{:S(2)}, u32[]{:S(2)}) collective-permute-start(f32[2,8,320]{2,1,0:T(8,128)S(1)} %get-tuple-element.18), channel_id=1, source_target_pairs={{1,0},{2,1},{3,2},{4,3},{5,4},{6,5},{7,6},{0,7},{9,8},{10,9},{11,1... | collective-permute-start | bytes 61448 | tf_op jit(solution)/shard_map/ppermute | solution.py:320
  53.8 2.3 %copy-start.14 = (f32[2,8,320]{2,1,0:T(8,128)}, f32[2,8,320]{2,1,0:T(8,128)S(1)}, u32[]{:S(2)}) copy-start(f32[2,8,320]{2,1,0:T(8,128)S(1)} %collective-permute-done.below) | copy-start | bytes 61444
  56.1 0.6 copy-start.16
  75.2 0.9 copy-start.3
  83.8 0.6 copy-start.5
  84.4 0.6 copy-start.6
  85.1 3.5 %collective-permute-start.2 = (f32[2,8,320]{2,1,0:T(8,128)S(1)}, f32[2,8,320]{2,1,0:T(8,128)S(1)}, u32[]{:S(2)}, u32[]{:S(2)}) collective-permute-start(f32[2,8,320]{2,1,0:T(8,128)S(1)} %get-tuple-element.22), channel_id=1, source_target_pairs={{0,1},{1,2},{2,3},{3,4},{4,5},{5,6},{6,7},{7,0},{8,9},{9,10},{10,1... | collective-permute-start | bytes 61448 | tf_op jit(solution)/shard_map/ppermute | solution.py:331
  87.6 3.3 %collective-permute-start.3 = (f32[2,8,320]{2,1,0:T(8,128)S(1)}, f32[2,8,320]{2,1,0:T(8,128)S(1)}, u32[]{:S(2)}, u32[]{:S(2)}) collective-permute-start(f32[2,8,320]{2,1,0:T(8,128)S(1)} %get-tuple-element.23), channel_id=1, source_target_pairs={{1,0},{2,1},{3,2},{4,3},{5,4},{6,5},{7,6},{0,7},{9,8},{10,9},{11,1... | collective-permute-start | bytes 61448 | tf_op jit(solution)/shard_map/ppermute | solution.py:332
  88.6 2.2 %copy-start.15 = (f32[2,8,320]{2,1,0:T(8,128)}, f32[2,8,320]{2,1,0:T(8,128)S(1)}, u32[]{:S(2)}) copy-start(f32[2,8,320]{2,1,0:T(8,128)S(1)} %collective-permute-done.2.below) | copy-start | bytes 61444
  90.8 0.6 copy-start.17

commit v2 on v1

v2 whole, which is shorter than its diff:
```python
import jax
import jax.numpy as jnp
from jax import lax
from jax.experimental import pallas as pl
from jax.experimental.pallas import tpu as pltpu
from jax.sharding import PartitionSpec as P

EPSILON = 1e-06
F32 = jnp.float32
BF16 = jnp.bfloat16
SLABS = 8
ELEMENTS = 8
WIDTH = 320
FACES = 7
ROWS = SLABS * ELEMENTS
PAIRS = WIDTH // 2
DEPTH = PAIRS * ELEMENTS
LANES = 2 * WIDTH
RING = 8
LINES = 4
DEVICES = 256
TINY = 1e-30
SPAN = 1024
SMALL_MIB = 4
OPERATE_MIB = 8
WIDE_MIB = 46
RESIDENT = (True, True)
WHOLE_MIB = 54

VMEM = pl.BlockSpec(memory_space=pltpu.VMEM)
SMEM = pl.BlockSpec(memory_space=pltpu.SMEM)
HBM = pl.BlockSpec(memory_space=pltpu.HBM)


def iota(shape, dim):
    return lax.broadcasted_iota(jnp.int32, shape, dim)


def struct(*shape):
    return jax.ShapeDtypeStruct(shape, F32)


def params(mib):
    return pltpu.CompilerParams(vmem_limit_bytes=mib * 1024 * 1024)


def maps_kernel(source_ref, decay_ref, out_ref, source, decay, sems):
    copies = [
        pltpu.make_async_copy(source_ref, source, sems.at[0]),
        pltpu.make_async_copy(decay_ref, decay, sems.at[1]),
    ]
    for copy in copies:
        copy.start()
    for copy in copies:
        copy.wait()
    product = jnp.ones((ELEMENTS, WIDTH), F32)
    offset = jnp.zeros((ELEMENTS, WIDTH), F32)
    for t in reversed(range(SLABS)):
        offset = source[t] + decay[t] * offset
        product = product * decay[t]
    for j in range(RING):
        out_ref[j, 0:ELEMENTS] = product
        out_ref[j, ELEMENTS:] = offset


def prepare_kernel(
    mine,
    neighbours,
    owner,
    pairing,
    source,
    decay,
    couple,
    faces,
    pick,
    halo,
    source_out,
    decay_out,
    couple_out,
):
    source_out[...] = source[...]
    decay_out[...] = decay[...]
    couple_out[...] = couple[...]
    at = iota((ELEMENTS, WIDTH), 0)

    def chosen(condition):
        return jnp.where(condition, 1.0, 0.0)

    for i in range(2):
        below = jnp.zeros((ELEMENTS, WIDTH), F32)
        for k in range(2):
            below = below + jnp.where(
                (at == owner[1, k]) & (pairing[0, k] == i), 1.0, 0.0
            )
        halo[i] = below
        halo[2 + i] = chosen(at == owner[0, i])
    halo[4] = chosen(at * 0 == pairing[0, 0])
    halo[5] = (at * 0 + mine[0] % RING).astype(F32)
    halo[6] = (at * 0 + mine[0] // RING).astype(F32)

    row = iota((4 * 2 * SLABS, 2 * ROWS), 0)
    col = iota((4 * 2 * SLABS, 2 * ROWS), 1)
    slot = row // (2 * SLABS)
    element = jnp.where(
        slot < 2,
        jnp.where(slot == 0, owner[0, 0], owner[0, 1]),
        jnp.where(slot == 2, owner[1, 0], owner[1, 1]),
    )
    pick[...] = chosen((row % (2 * SLABS)) * ELEMENTS + element == col).astype(BF16)

    e = iota((2 * ELEMENTS, 128), 1) % ELEMENTS
    d = iota((2 * ELEMENTS, 128), 0) % ELEMENTS
    for f in range(FACES):
        to = e
        if f > 0:
            for k in range(ELEMENTS):
                to = jnp.where(e == k, neighbours[f - 1, k], to)
        faces[f] = chosen(to == d).astype(BF16)


def line_kernel(first, *refs):
    if first:
        halo, maps, out, later = refs
        offset_of = lambda j: maps[j, ELEMENTS:]
    else:
        halo, maps, offsets, out, later = refs
        offset_of = lambda j: offsets[j]
    mine = halo[5]
    product = jnp.ones((ELEMENTS, WIDTH), F32)
    offset = jnp.zeros((ELEMENTS, WIDTH), F32)
    for j in reversed(range(RING)):
        if j < RING - 1:
            after = mine == j
            keep = jnp.where(after, offset, keep)
            keep_product = jnp.where(after, product, keep_product)
        else:
            keep, keep_product = offset, product
        offset = offset_of(j) + maps[j, 0:ELEMENTS] * offset
        product = product * maps[j, 0:ELEMENTS]
    if first:
        later[0:ELEMENTS] = keep_product
        later[ELEMENTS:] = keep
        for j in range(LINES):
            out[j, 0:ELEMENTS] = product
            out[j, ELEMENTS:] = offset
    else:
        later[...] = keep
        for j in range(LINES):
            out[j] = offset


def chain_kernel(first, *refs):
    if first:
        field, decay, lines, later = refs[:4]
        refs = refs[4:]
        offset_of = lambda j: lines[j, ELEMENTS:]
        later_offset = later[ELEMENTS:]
    else:
        field, decay, lines, later, line_offsets, later_offsets = refs[:6]
        refs = refs[6:]
        offset_of = lambda j: line_offsets[j]
        later_offset = later_offsets[...]
    pick, halo, couple, chained, spread, up, down = refs

    product = jnp.ones((ELEMENTS, WIDTH), F32)
    offset = jnp.zeros((ELEMENTS, WIDTH), F32)
    for j in reversed(range(LINES)):
        offset = offset_of(j) + lines[j, 0:ELEMENTS] * offset
        product = product * lines[j, 0:ELEMENTS]
    value = offset / (1.0 - product)
    for j in reversed(range(1, LINES)):
        value = jnp.where(halo[6] < j, offset_of(j) + lines[j, 0:ELEMENTS] * value, value)
    value = later_offset + later[0:ELEMENTS] * value
    for t in reversed(range(SLABS)):
        value = field[t] + decay[t] * value
        chained[t] = value
    z = chained[...].reshape(ROWS, WIDTH)
    high = z.astype(BF16)
    low = (z - high.astype(F32)).astype(BF16)
    parts = jnp.concatenate([high, low], axis=0)

    picked = jnp.dot(pick[...], parts, preferred_element_type=F32).astype(BF16)
    products = []
    for k in range(4):
        both = jnp.dot(
            picked[k * 2 * SLABS : (k + 1) * 2 * SLABS],
            couple[k // 2, k % 2],
            preferred_element_type=F32,
        )
        products.append(both[:SLABS] + both[SLABS:])
    up[0] = products[0]
    up[1] = products[1]
    straight = halo[4] > 0.5
    down[0] = jnp.where(straight, products[2], products[3])
    down[1] = jnp.where(straight, products[3], products[2])

    same = jnp.where(iota((128, 128), 0) // 8 == iota((128, 128), 1) // 8, 1.0, 0.0).astype(BF16)
    own = iota((2 * ROWS, DEPTH), 0) % ELEMENTS == iota((2 * ROWS, DEPTH), 1) % ELEMENTS
    n = iota((256, SPAN), 0)
    lane = iota((256, SPAN), 1)
    for b in range(2):
        expand = jnp.where(n == 2 * (lane // ELEMENTS) + b, 1.0, 0.0).astype(BF16)
        wide = jnp.concatenate(
            [
                jnp.dot(parts[:, :256], expand, preferred_element_type=F32),
                jnp.dot(parts[:, 256:], expand[:64, :256], preferred_element_type=F32),
            ],
            axis=1,
        )
        wide = jnp.where(own, wide, 0.0).astype(BF16)
        spread[b * 2 * ROWS : (b + 1) * 2 * ROWS] = jnp.dot(
            same, wide, preferred_element_type=F32
        ).astype(BF16)


def local_kernel(resident, *refs):
    if resident:
        spread, faces, weights, local, low, middle, high = refs
    else:
        spread, faces, stored, local, weights, low, middle, high, sems = refs
        copies = [
            pltpu.make_async_copy(stored.at[f], weights.at[f], sems.at[f]) for f in range(FACES)
        ]
        for copy in copies:
            copy.start()
    half = 2 * ROWS
    for f in range(FACES):
        mask = jnp.concatenate([faces[f]] * (DEPTH // 128), axis=1)
        mask = jnp.concatenate([mask] * (4 * ROWS // 16), axis=0)
        left = spread[...] * mask
        if not resident:
            copies[f].wait()
        parts = (
            (low, left[:half], slice(0, 256)),
            (middle, left, slice(256, 384)),
            (high, left[half:], slice(384, LANES)),
        )
        for sums, rows, lanes in parts:
            part = jnp.dot(rows, weights[f, :, lanes], preferred_element_type=F32)
            if f == 0:
                sums[...] = part
            else:
                sums[...] += part
    even = low[:ROWS] + low[ROWS:]
    even_end = middle[:ROWS] + middle[ROWS:half]
    odd_start = middle[half : half + ROWS] + middle[half + ROWS :]
    odd = high[:ROWS] + high[ROWS:]
    result = jnp.concatenate([even, even_end[:, :64]], axis=1) + jnp.concatenate(
        [odd_start[:, 64:], odd], axis=1
    )
    local[...] = result.reshape(SLABS, ELEMENTS, WIDTH)


def along(x, groups):
    return lax.all_to_all(x, "tm", 0, 0, axis_index_groups=groups, tiled=True)


def operate(first, field, decay, start, known, tables, weights, couple):
    faces, pick, halo = tables
    depth = 2 * ELEMENTS if first else ELEMENTS
    along_z = [[y * RING + z for z in range(RING)] for y in range(LINES)]
    along_y = [[y * RING + z for y in range(LINES)] for z in range(RING)]

    def compose(*refs):
        line_kernel(first, *refs)

    def chain(*refs):
        chain_kernel(first, *refs)

    gathered = along(start, along_z)
    own = (gathered,) if first else (known[0], gathered)
    line, later = pl.pallas_call(
        compose,
        out_shape=(struct(LINES, depth, WIDTH), struct(depth, WIDTH)),
        in_specs=[VMEM] * (1 + len(own)),
        out_specs=(VMEM,) * 2,
        compiler_params=params(SMALL_MIB),
        cost_estimate=pl.CostEstimate(flops=10 * 10**9, bytes_accessed=2 * 10**6, transcendentals=0),
    )(halo, *own)
    lines = along(line, along_y)
    if first:
        known = (gathered, lines, later)
    chained, spread, up, down = pl.pallas_call(
        chain,
        out_shape=(
            struct(SLABS, ELEMENTS, WIDTH),
            jax.ShapeDtypeStruct((4 * ROWS, DEPTH), BF16),
            struct(2, SLABS, WIDTH),
            struct(2, SLABS, WIDTH),
        ),
        in_specs=[VMEM] * (7 if first else 9),
        out_specs=(VMEM,) * 4,
        compiler_params=params(OPERATE_MIB),
        cost_estimate=pl.CostEstimate(flops=10 * 10**9, bytes_accessed=2 * 10**6, transcendentals=0),
    )(field, decay, *known[1:], *(() if first else (lines, later)), pick, halo, couple)
    below = lax.ppermute(up, "space", [(i, (i + 1) % 8) for i in range(8)])
    above = lax.ppermute(down, "space", [((i + 1) % 8, i) for i in range(8)])
    resident = RESIDENT[0 if first else 1]

    def local_part(*refs):
        local_kernel(resident, *refs)

    scratch = [
        pltpu.VMEM((2 * ROWS, 256), F32),
        pltpu.VMEM((4 * ROWS, 128), F32),
        pltpu.VMEM((2 * ROWS, 256), F32),
    ]
    if not resident:
        scratch = [
            pltpu.VMEM((FACES, DEPTH, LANES), BF16),
            *scratch,
            pltpu.SemaphoreType.DMA((FACES,)),
        ]
    local = pl.pallas_call(
        local_part,
        out_shape=struct(SLABS, ELEMENTS, WIDTH),
        in_specs=[VMEM] * 2 + [VMEM if resident else HBM],
        out_specs=VMEM,
        scratch_shapes=scratch,
        compiler_params=params(OPERATE_MIB if resident else WIDE_MIB),
        cost_estimate=pl.CostEstimate(
            flops=2 * FACES * 4 * ROWS * DEPTH * LANES,
            bytes_accessed=2 * FACES * DEPTH * LANES,
            transcendentals=0,
        ),
    )(spread, faces, weights)
    return chained, local, below, above, known


def add_halo(halo, local, below, above, out):
    for t in range(SLABS):
        value = local[t]
        for k in range(2):
            value = value + halo[k] * below[k, t : t + 1]
            value = value + halo[2 + k] * above[k, t : t + 1]
        out[t] = value


def middle_kernel(halo, local, below, above, decay, image, out):
    add_halo(halo, local, below, above, image)
    offset = jnp.zeros((ELEMENTS, WIDTH), F32)
    for t in reversed(range(SLABS)):
        offset = image[t] + decay[t] * offset
    for j in range(RING):
        out[j] = offset


def total_of(x):
    return jnp.sum(jnp.sum(x, axis=0), keepdims=True)


def gram_kernel(halo, local, below, above, source, image0, image1, out):
    add_halo(halo, local, below, above, image1)
    s = source[...]
    largest = [
        jnp.maximum(jnp.max(jnp.max(jnp.abs(image[...]), axis=0), keepdims=True), TINY)
        for image in (image0, image1)
    ]
    one = jnp.ones((1, 1), F32)
    g0 = image0[...] * (1.0 / largest[0])
    g1 = image1[...] * (1.0 / largest[1])
    entries = [
        (total_of(s * s), one, one),
        (total_of(s * g0), largest[0], one),
        (total_of(g0 * g0), largest[0], largest[0]),
        (total_of(s * g1), largest[1], one),
        (total_of(g0 * g1), largest[0], largest[1]),
        (total_of(g1 * g1), largest[1], largest[1]),
    ]
    lane = iota((8, 128), 1)
    row = jnp.ones((8, 128), F32)
    for k, entry in enumerate(entries):
        for i, value in enumerate(entry):
            row = jnp.where(lane == k + 16 * i, value, row)
    for j in range(DEVICES // 8):
        out[j * 8 : (j + 1) * 8] = row


def last_kernel(gram, source, first_chain, second_chain, image0, image1, adjoint, residual):
    every = gram[...]
    scale_a = pltpu.roll(every, 128 - 16, 1)
    scale_b = pltpu.roll(every, 128 - 32, 1)
    top_a = jnp.max(scale_a, axis=0, keepdims=True)
    top_b = jnp.max(scale_b, axis=0, keepdims=True)
    sums = jnp.sum(every * (scale_a / top_a) * (scale_b / top_b), axis=0, keepdims=True)
    lane = iota((1, 128), 1)

    def entry(row, k):
        return jnp.sum(jnp.where(lane == k, row, 0.0), axis=1, keepdims=True)

    ss, s0, g00, s1, g01, g11 = (entry(sums, k) for k in range(6))
    a0 = entry(top_a, 1)
    a1 = entry(top_a, 3)
    square = ss + EPSILON
    norm = jnp.sqrt(square)
    r0 = a0 / norm
    kappa = EPSILON / square - r0 * (s0 / norm)
    rest = r0 * r0 * g00 + 2.0 * kappa * r0 * (s0 / norm) + kappa * kappa * (ss / square)
    h10 = jnp.sqrt(jnp.maximum(rest, 0.0) + EPSILON)
    beta = 1.0 / (norm * h10)
    b0 = r0 / h10
    b1 = (a1 / norm) / h10
    cross = b0 * b1 * g01 + kappa * beta * b1 * s1
    delta = cross + kappa * (b0 * b0 * g00 + kappa * beta * b0 * s0)
    lost = EPSILON / (h10 * h10)
    h00 = 1.0 - kappa
    h11 = (1.0 - lost) + delta
    near = EPSILON * (1.0 - kappa) * beta
    h01 = (b1 * s1 + kappa * b0 * s0 + near) / norm
    c1 = kappa + lost - delta
    mu = (b1 * s1 + beta * EPSILON) / square
    rest = (
        b1 * b1 * g11
        + c1 * c1 * (1.0 - lost)
        + mu * mu * ss
        + 2.0 * c1 * cross
        - 2.0 * mu * b1 * s1
        - 2.0 * c1 * mu * near
    )
    h21 = jnp.sqrt(jnp.maximum(rest, 0.0) + EPSILON)
    radius_one = jnp.sqrt(h00 * h00 + h10 * h10)
    cosine = h00 / radius_one
    sine = h10 / radius_one
    upper = cosine * h01 + sine * h11
    pivot = cosine * h11 - sine * h01
    radius_two = jnp.sqrt(pivot * pivot + h21 * h21)
    y1 = -(norm * sine) * (pivot / radius_two) / radius_two
    y0 = (norm * cosine - upper * y1) / radius_one
    p0 = y0 / norm
    p1 = y1 * beta
    p2 = p1 * kappa
    for t in range(SLABS):
        adjoint[t] = (p0 + p2) * first_chain[t] + p1 * second_chain[t]
        residual[t] = (
            (1.0 - p0 - p2) * source[t] - (p0 + p1 + p2) * image0[t] - p1 * image1[t]
        )


def shards(
    source, decay_rate, blocks, neighbours, interface_jacobian_blocks, face_element_owner, pairing
):
    source = jnp.transpose(source, (0, 2, 1))
    decay = jnp.transpose(decay_rate, (0, 2, 1))
    weights = jnp.transpose(blocks, (1, 0, 2)).reshape(FACES, ELEMENTS, PAIRS, LANES)
    weights = jnp.transpose(weights, (0, 2, 1, 3)).reshape(FACES, DEPTH, LANES)
    couple = interface_jacobian_blocks.reshape(2, 2, WIDTH, WIDTH)
    mine = lax.axis_index("tm").astype(jnp.int32).reshape(1)
    field_shape = struct(SLABS, ELEMENTS, WIDTH)
    maps = pl.pallas_call(
        maps_kernel,
        out_shape=struct(RING, 2 * ELEMENTS, WIDTH),
        in_specs=[HBM] * 2,
        out_specs=VMEM,
        scratch_shapes=[pltpu.VMEM((SLABS, ELEMENTS, WIDTH), F32)] * 2
        + [pltpu.SemaphoreType.DMA((2,))],
        compiler_params=params(WHOLE_MIB),
    )(source, decay)
    *tables, source, decay, couple = pl.pallas_call(
        prepare_kernel,
        out_shape=(
            jax.ShapeDtypeStruct((FACES, 2 * ELEMENTS, 128), BF16),
            jax.ShapeDtypeStruct((4 * 2 * SLABS, 2 * ROWS), BF16),
            struct(7, ELEMENTS, WIDTH),
            field_shape,
            field_shape,
            jax.ShapeDtypeStruct((2, 2, WIDTH, WIDTH), BF16),
        ),
        in_specs=[SMEM] * 4 + [VMEM] * 3,
        out_specs=(VMEM,) * 6,
        compiler_params=params(SMALL_MIB),
    )(mine, neighbours, face_element_owner, pairing, source, decay, couple)
    halo = tables[2]
    chain0, local, below, above, known = operate(
        True, source, decay, maps, None, tables, weights, couple
    )
    image0, offsets = pl.pallas_call(
        middle_kernel,
        out_shape=(field_shape, struct(RING, ELEMENTS, WIDTH)),
        in_specs=[VMEM] * 5,
        out_specs=(VMEM,) * 2,
        compiler_params=params(SMALL_MIB),
    )(halo, local, below, above, decay)
    chain1, local, below, above, known = operate(
        False, image0, decay, offsets, known, tables, weights, couple
    )
    image1, gram = pl.pallas_call(
        gram_kernel,
        out_shape=(field_shape, struct(DEVICES, 128)),
        in_specs=[VMEM] * 6,
        out_specs=(VMEM,) * 2,
        compiler_params=params(SMALL_MIB),
    )(halo, local, below, above, source, image0)
    gram = lax.all_to_all(gram, ("tm", "space"), 0, 0, tiled=True)
    adjoint, residual = pl.pallas_call(
        last_kernel,
        out_shape=(field_shape, field_shape),
        in_specs=[VMEM] * 6,
        out_specs=(VMEM,) * 2,
        compiler_params=params(SMALL_MIB),
    )(gram, source, chain0, chain1, image0, image1)
    return (jnp.transpose(adjoint, (0, 2, 1)), jnp.transpose(residual, (0, 2, 1)))


def solution(mesh):
    in_specs = (
        P("tm", None, "space"),
        P("tm", None, "space"),
        P("space", None, None),
        P(None, "space"),
        P(None, "space", None),
        P(None, "space"),
        P("space", None),
    )
    out_specs = (P("tm", None, "space"), P("tm", None, "space"))
    return jax.shard_map(shards, mesh=mesh, in_specs=in_specs, out_specs=out_specs, check_vma=False)
```

time: 119 us -> 85.8 us (0.72)
  waiting for transfers between devices: 23.3 us -> 3.59 us
  Pallas kernels: 23.4 us -> 11.2 us
  blocking collectives: 39.6 us -> 45.8 us
  local copies, waits for them, and re-layouts: 10.5 us -> 5.89 us
  starting transfers between devices: 21.1 us -> 18.2 us
    all_to_all x1, waiting for transfers between devices: 17.2 us -> 2.17 us  [along(): return lax.all_to_all(x, 'tm', 0, 0, axis_index_groups=groups, tiled=True)]
    all_to_all x1 -> x3, blocking collectives: 16.6 us -> 26.2 us  [along(): return lax.all_to_all(x, 'tm', 0, 0, axis_index_groups=groups, tiled=True)]
    pallas_call x4 -> x9, Pallas kernels: 19.2 us -> 9.78 us  [the longest x2 5.32 us: operate(): pl.pallas_call(local_part, out_shape=struct(SLABS, ELEMENTS, WIDTH), in_s...]
    ppermute x4, waiting for transfers between devices: 6.15 us -> 1.42 us  [the longest x2 1.41 us: operate(): above = lax.ppermute(down, 'space', [((i + 1) % 8, i) for i in range(8)])]
    unnamed x36 -> x16, local copies, waits for them, and re-layouts: 8.46 us -> 3.81 us
    all_to_all x1, blocking collectives: 23 us -> 19.7 us  [shards(): gram = lax.all_to_all(gram, ('tm', 'space'), 0, 0, tiled=True)]
    all_to_all x1, starting transfers between devices: 12 us -> 9.03 us  [along(): return lax.all_to_all(x, 'tm', 0, 0, axis_index_groups=groups, tiled=True)]
    pallas_call x1, Pallas kernels: 2.03 us -> 0.34 us  [shards(): pl.pallas_call(gram_kernel, out_shape=(field_shape, struct(DEVICES, 128))...]
  transfers between devices with their start and end apart: 5 -> 5, of which waited for: 5 -> 3; matrix products, arithmetic and copies ran while one was open for 2% -> 2% of each run, Pallas kernels for 0% -> 7%
where the time goes in v2:
time: 85.8 us; the launch traced here: 85.4 us
  blocking collectives  45.8 us (53%)
  starting transfers between devices  18.2 us (21%)
  Pallas kernels  11.2 us (13%)
  local copies, waits for them, and re-layouts  5.89 us (7%)
  waiting for transfers between devices  3.59 us (4%)
    all_to_all x3, blocking collectives, along(): return lax.all_to_all(x, 'tm', 0, 0, axis_index_groups=groups, tiled=True)  26.2 us
    all_to_all x1, blocking collectives, shards(): gram = lax.all_to_all(gram, ('tm', 'space'), 0, 0, tiled=True)  19.7 us
    ppermute x2, starting transfers between devices, operate(): below = lax.ppermute(up, 'space', [(i, (i + 1) % 8) for i in range(8)])  9.15 us
    all_to_all x1, starting transfers between devices, along(): return lax.all_to_all(x, 'tm', 0, 0, axis_index_groups=groups, tiled=True)  9.03 us
    pallas_call x2, Pallas kernels, operate(): pl.pallas_call(local_part, out_shape=struct(SLABS, ELEMENTS, WIDTH), in_s...  5.32 us
    unnamed x16, local copies, waits for them, and re-layouts  3.81 us
    all_to_all x1, waiting for transfers between devices, along(): return lax.all_to_all(x, 'tm', 0, 0, axis_index_groups=groups, tiled=True)  2.17 us
    reshape x1, local copies, waits for them, and re-layouts, shards(): couple = interface_jacobian_blocks.reshape(2, 2, WIDTH, WIDTH)  2.07 us
  transfers between devices with their start and end apart: 5, of which 3 were waited for; matrix products, arithmetic and copies ran while one was open for 2% of the time, Pallas kernels for 7%

profile of v2, /device:TPU:1, one launch (start us, length us, event | category | flops | bytes accessed | tf_op | source)
XLA Modules:
  0.0 85.4 jit_solution(11626107534576451012)
XLA Ops:
  0.6 1.7 %shard_map.87 = f32[8,16,320]{2,1,0:T(8,128)} custom-call(f32[8,8,320]{2,1,0:T(8,128)} %bitcast.21, f32[8,8,320]{2,1,0:T(8,128)} %bitcast.23), custom_call_target="tpu_custom_call" | custom-call | tf_op jit(solution)/shard_map/pallas_call | solution.py:449
  2.3 9.0 %all-to-all-start = ((f32[8,16,320]{2,1,0:T(8,128)}), f32[8,16,320]{2,1,0:T(8,128)S(1)}, u32[]{:S(2)}, u32[]{:S(2)}) async-start(f32[8,16,320]{2,1,0:T(8,128)} %shard_map.87), calls=%async_computation | async-start | bytes 393216 | tf_op jit(solution)/shard_map/all_to_all | solution.py:255
  11.3 2.1 %reshape.19.couple = bf16[2,2,320,320]{3,2,1,0:T(8,128)(2,1)S(1)} reshape(bf16[2,2,102400]{2,1,0:T(2,128)(2,1)} %param.11) | data formatting | bytes 1638400 | tf_op jit(solution)/shard_map/reshape | solution.py:446
  13.4 0.0 copy-start
  13.4 0.9 %copy-done = f32[8,320,8]{1,2,0:T(8,128)S(1)} copy-done((f32[8,320,8]{1,2,0:T(8,128)S(1)}, f32[8,320,8]{1,2,0:T(8,128)}, u32[]{:S(2)}) %copy-start) | copy-done | bytes 81944
  14.3 0.0 copy-start.1
  14.3 0.9 %copy-done.1 = f32[8,320,8]{1,2,0:T(8,128)S(1)} copy-done((f32[8,320,8]{1,2,0:T(8,128)S(1)}, f32[8,320,8]{1,2,0:T(8,128)}, u32[]{:S(2)}) %copy-start.1) | copy-done | bytes 81944
  15.2 0.0 copy-start.2
  15.2 0.7 copy-done.2
  15.9 0.0 copy-start.3
  15.9 0.7 copy-done.3
  16.6 0.0 copy-start.4
  16.6 0.7 copy-done.4
  17.2 0.7 shard_map.86
  18.0 2.2 %all-to-all-done.refs_1_ = f32[8,16,320]{2,1,0:T(8,128)S(1)} async-done(((f32[8,16,320]{2,1,0:T(8,128)}), f32[8,16,320]{2,1,0:T(8,128)S(1)}, u32[]{:S(2)}, u32[]{:S(2)}) %all-to-all-start) | async-done | bytes 163872 | tf_op jit(solution)/shard_map/all_to_all | solution.py:255
  20.1 0.0 slice-start
  20.1 0.0 slice-start.1
  20.2 8.9 %all_to_all.31.refs_2_ = f32[4,16,320]{2,1,0:T(8,128)S(1)} all-to-all(f32[4,16,320]{2,1,0:T(8,128)S(1)} %get-tuple-element.29), channel_id=1, replica_groups={{0,64,128,192},{8,72,136,200},{16,80,144,208},{24,88,152,216},{32,96,16..., dimensions={0} | all-to-all | bytes 163840 | tf_op jit(solution)/shard_map/all_to_all | solution.py:255
  29.1 0.0 slice-start.2
  29.1 1.0 %shard_map.89 = (f32[8,8,320]{2,1,0:T(8,128)S(1)}, bf16[256,1280]{1,0:T(8,128)(2,1)S(1)}, f32[2,8,320]{2,1,0:T(8,128)S(1)}, f32[2,8,320]{2,1,0:T(8,128)S(1)}) custom-call(f32[8,8,320]{2,1,0:T(8,128)S(1)} %get-tuple-element.27.refs_0_.source, f32[8,8,320]{2,1,0:T(8,128)S(1)} %get-tuple-element.28.refs_1_.decay, f32[4,16,320]{2,1,0:T(8,128)S(1)} %all_to_all.31.refs_2_, ...), custom_call_target="tpu_custom_call" | custom-call | flops 10000000000 | bytes 2000000 | tf_op jit(solution)/shard_map/pallas_call | solution.py:283
  30.1 5.2 %collective-permute-start = (f32[2,8,320]{2,1,0:T(8,128)S(1)}, f32[2,8,320]{2,1,0:T(8,128)S(1)}, u32[]{:S(2)}, u32[]{:S(2)}) collective-permute-start(f32[2,8,320]{2,1,0:T(8,128)S(1)} %get-tuple-element.35), channel_id=1, source_target_pairs={{0,1},{1,2},{2,3},{3,4},{4,5},{5,6},{6,7},{7,0},{8,9},{9,10},{10,1... | collective-permute-start | bytes 61448 | tf_op jit(solution)/shard_map/ppermute | solution.py:296
  35.2 0.0 collective-permute-start.1
  35.2 0.0 slice-done
  35.2 0.0 slice-done.1
  35.2 0.0 slice-done.2
  35.2 2.6 %shard_map.90.local = f32[8,8,320]{2,1,0:T(8,128)S(1)} custom-call(bf16[256,1280]{1,0:T(8,128)(2,1)S(1)} %get-tuple-element.33.refs_0_, bf16[7,16,128]{2,1,0:T(8,128)(2,1)S(1)} %get-tuple-element.34.refs_1_, bf16[7,1280,640]{2,1,0:T(8,128)(2,1)S(1)} %bitcast.18), custom_call_target="tpu_custom_call" | custom-call | flops 2936012800 | bytes 11468800 | tf_op jit(solution)/shard_map/pallas_call | solution.py:314
  37.9 0.0 collective-permute-done.below
  37.9 0.6 collective-permute-done.1.above
  38.5 0.1 shard_map.91
  38.5 10.5 %all_to_all.32.refs_2_ = f32[8,8,320]{2,1,0:T(8,128)S(1)} all-to-all(f32[8,8,320]{2,1,0:T(8,128)S(1)} %get-tuple-element.38), channel_id=1, replica_groups={{0,8,16,24,32,40,48,56},{64,72,80,88,96,104,112,120},{128,136,144,152,1..., dimensions={0} | all-to-all | bytes 163840 | tf_op jit(solution)/shard_map/all_to_all | solution.py:255
  49.1 6.7 %all_to_all.33.refs_4_ = f32[4,8,320]{2,1,0:T(8,128)S(1)} all-to-all(f32[4,8,320]{2,1,0:T(8,128)S(1)} %get-tuple-element.39), channel_id=1, replica_groups={{0,64,128,192},{8,72,136,200},{16,80,144,208},{24,88,152,216},{32,96,16..., dimensions={0} | all-to-all | bytes 81920 | tf_op jit(solution)/shard_map/all_to_all | solution.py:255
  55.8 1.0 %shard_map.93 = (f32[8,8,320]{2,1,0:T(8,128)S(1)}, bf16[256,1280]{1,0:T(8,128)(2,1)S(1)}, f32[2,8,320]{2,1,0:T(8,128)S(1)}, f32[2,8,320]{2,1,0:T(8,128)S(1)}) custom-call(f32[8,8,320]{2,1,0:T(8,128)S(1)} %get-tuple-element.37.refs_0_.image0, f32[8,8,320]{2,1,0:T(8,128)S(1)} %get-tuple-element.28.refs_1_.decay, f32[4,16,320]{2,1,0:T(8,128)S(1)} %all_to_all.31.refs_2_, ...), custom_call_target="tpu_custom_call" | custom-call | flops 10000000000 | bytes 2000000 | tf_op jit(solution)/shard_map/pallas_call | solution.py:283
  56.8 4.0 %collective-permute-start.2 = (f32[2,8,320]{2,1,0:T(8,128)S(1)}, f32[2,8,320]{2,1,0:T(8,128)S(1)}, u32[]{:S(2)}, u32[]{:S(2)}) collective-permute-start(f32[2,8,320]{2,1,0:T(8,128)S(1)} %get-tuple-element.42), channel_id=1, source_target_pairs={{0,1},{1,2},{2,3},{3,4},{4,5},{5,6},{6,7},{7,0},{8,9},{9,10},{10,1... | collective-permute-start | bytes 61448 | tf_op jit(solution)/shard_map/ppermute | solution.py:296
  60.8 0.0 collective-permute-start.3
  60.8 2.7 %shard_map.94.local = f32[8,8,320]{2,1,0:T(8,128)S(1)} custom-call(bf16[256,1280]{1,0:T(8,128)(2,1)S(1)} %get-tuple-element.41.refs_0_, bf16[7,16,128]{2,1,0:T(8,128)(2,1)S(1)} %get-tuple-element.34.refs_1_, bf16[7,1280,640]{2,1,0:T(8,128)(2,1)S(1)} %bitcast.19), custom_call_target="tpu_custom_call" | custom-call | flops 2936012800 | bytes 11468800 | tf_op jit(solution)/shard_map/pallas_call | solution.py:314
  63.5 0.0 collective-permute-done.2.below
  63.5 0.8 collective-permute-done.3.above
  64.3 0.3 shard_map.95
  64.7 19.7 %all_to_all.34 = f32[256,1,128]{2,1,0:T(1,128)S(1)} all-to-all(f32[256,1,128]{2,1,0:T(1,128)S(1)} %bitcast.25), channel_id=1, replica_groups=mesh['tm'=32,'space'=8] {'tm','space'}, dimensions={0} | all-to-all | bytes 262144 | tf_op jit(solution)/shard_map/all_to_all | solution.py:493
  84.3 1.0 %shard_map.96 = (f32[8,8,320]{2,1,0:T(8,128)}, f32[8,8,320]{2,1,0:T(8,128)}) custom-call(f32[256,128]{1,0:T(8,128)S(1)} %bitcast.20, f32[8,8,320]{2,1,0:T(8,128)S(1)} %get-tuple-element.27.refs_0_.source, f32[8,8,320]{2,1,0:T(8,128)S(1)} %get-tuple-element.45.first_chain, f32[8,8,320]{2,1,0:T(8,128)S(1)} %get-tuple-element.46.second_chain, ...), custom_call_target="tpu_custom_call" | custom-call | tf_op jit(solution)/shard_map/pallas_call | solution.py:494
  (3 shorter events, 0.0 us)
Async XLA Ops:
  2.3 17.8 %all-to-all-start = ((f32[8,16,320]{2,1,0:T(8,128)}), f32[8,16,320]{2,1,0:T(8,128)S(1)}, u32[]{:S(2)}, u32[]{:S(2)}) async-start(f32[8,16,320]{2,1,0:T(8,128)} %shard_map.87), calls=%async_computation | async-start | bytes 393216 | tf_op jit(solution)/shard_map/all_to_all | solution.py:255
  13.4 0.9 %copy-start = (f32[8,320,8]{1,2,0:T(8,128)S(1)}, f32[8,320,8]{1,2,0:T(8,128)}, u32[]{:S(2)}) copy-start(f32[8,320,8]{1,2,0:T(8,128)} %param.7) | copy-start | bytes 245764
  14.3 0.9 %copy-start.1 = (f32[8,320,8]{1,2,0:T(8,128)S(1)}, f32[8,320,8]{1,2,0:T(8,128)}, u32[]{:S(2)}) copy-start(f32[8,320,8]{1,2,0:T(8,128)} %param.8) | copy-start | bytes 245764
  15.2 0.7 copy-start.2
  15.9 0.7 copy-start.3
  16.6 0.7 copy-start.4
  20.1 15.1 %slice-start = ((s8[11468800]{0:T(1024)(128)(4,1)}), s8[4194304]{0:T(1024)(128)(4,1)S(1)}, s32[]{:S(2)}) async-start(s8[11468800]{0:T(1024)(128)(4,1)} %bitcast.16), calls=%async_computation.5 | async-start | bytes 8388608
  20.1 15.1 %slice-start.1 = ((s8[11468800]{0:T(1024)(128)(4,1)}), s8[4194304]{0:T(1024)(128)(4,1)S(1)}, s32[]{:S(2)}) async-start(s8[11468800]{0:T(1024)(128)(4,1)} %bitcast.16), calls=%async_computation.6 | async-start | bytes 8388608
  29.1 6.1 %slice-start.2 = ((s8[11468800]{0:T(1024)(128)(4,1)}), s8[3080192]{0:T(1024)(128)(4,1)S(1)}, s32[]{:S(2)}) async-start(s8[11468800]{0:T(1024)(128)(4,1)} %bitcast.16), calls=%async_computation.7 | async-start | bytes 6160384
  30.1 7.8 %collective-permute-start = (f32[2,8,320]{2,1,0:T(8,128)S(1)}, f32[2,8,320]{2,1,0:T(8,128)S(1)}, u32[]{:S(2)}, u32[]{:S(2)}) collective-permute-start(f32[2,8,320]{2,1,0:T(8,128)S(1)} %get-tuple-element.35), channel_id=1, source_target_pairs={{0,1},{1,2},{2,3},{3,4},{4,5},{5,6},{6,7},{7,0},{8,9},{9,10},{10,1... | collective-permute-start | bytes 61448 | tf_op jit(solution)/shard_map/ppermute | solution.py:296
  35.2 3.3 %collective-permute-start.1 = (f32[2,8,320]{2,1,0:T(8,128)S(1)}, f32[2,8,320]{2,1,0:T(8,128)S(1)}, u32[]{:S(2)}, u32[]{:S(2)}) collective-permute-start(f32[2,8,320]{2,1,0:T(8,128)S(1)} %get-tuple-element.36), channel_id=1, source_target_pairs={{1,0},{2,1},{3,2},{4,3},{5,4},{6,5},{7,6},{0,7},{9,8},{10,9},{11,1... | collective-permute-start | bytes 61448 | tf_op jit(solution)/shard_map/ppermute | solution.py:297
  56.8 6.7 %collective-permute-start.2 = (f32[2,8,320]{2,1,0:T(8,128)S(1)}, f32[2,8,320]{2,1,0:T(8,128)S(1)}, u32[]{:S(2)}, u32[]{:S(2)}) collective-permute-start(f32[2,8,320]{2,1,0:T(8,128)S(1)} %get-tuple-element.42), channel_id=1, source_target_pairs={{0,1},{1,2},{2,3},{3,4},{4,5},{5,6},{6,7},{7,0},{8,9},{9,10},{10,1... | collective-permute-start | bytes 61448 | tf_op jit(solution)/shard_map/ppermute | solution.py:296
  60.8 3.5 %collective-permute-start.3 = (f32[2,8,320]{2,1,0:T(8,128)S(1)}, f32[2,8,320]{2,1,0:T(8,128)S(1)}, u32[]{:S(2)}, u32[]{:S(2)}) collective-permute-start(f32[2,8,320]{2,1,0:T(8,128)S(1)} %get-tuple-element.43), channel_id=1, source_target_pairs={{1,0},{2,1},{3,2},{4,3},{5,4},{6,5},{7,6},{0,7},{9,8},{10,9},{11,1... | collective-permute-start | bytes 61448 | tf_op jit(solution)/shard_map/ppermute | solution.py:297

commit v3 on v2

--- a/solution.py
+++ b/solution.py
@@ -31,6 +31,8 @@
 SMEM = pl.BlockSpec(memory_space=pltpu.SMEM)
 HBM = pl.BlockSpec(memory_space=pltpu.HBM)
 
+HINT = pl.CostEstimate(flops=10 * 10**9, bytes_accessed=10**6, transcendentals=0)
+
 
 def iota(shape, dim):
     return lax.broadcasted_iota(jnp.int32, shape, dim)
@@ -96,7 +98,6 @@
         halo[2 + i] = chosen(at == owner[0, i])
     halo[4] = chosen(at * 0 == pairing[0, 0])
     halo[5] = (at * 0 + mine[0] % RING).astype(F32)
-    halo[6] = (at * 0 + mine[0] // RING).astype(F32)
 
     row = iota((4 * 2 * SLABS, 2 * ROWS), 0)
     col = iota((4 * 2 * SLABS, 2 * ROWS), 1)
@@ -140,37 +141,31 @@
     if first:
         later[0:ELEMENTS] = keep_product
         later[ELEMENTS:] = keep
-        for j in range(LINES):
-            out[j, 0:ELEMENTS] = product
-            out[j, ELEMENTS:] = offset
+        out[0:ELEMENTS] = product
+        out[ELEMENTS:] = offset
     else:
         later[...] = keep
-        for j in range(LINES):
-            out[j] = offset
+        out[...] = offset
 
 
 def chain_kernel(first, *refs):
+    field, decay = refs[:2]
+    later, *lines = refs[2 : 3 + LINES]
+    refs = refs[3 + LINES :]
     if first:
-        field, decay, lines, later = refs[:4]
-        refs = refs[4:]
-        offset_of = lambda j: lines[j, ELEMENTS:]
+        offsets = [line[ELEMENTS:] for line in lines]
         later_offset = later[ELEMENTS:]
     else:
-        field, decay, lines, later, line_offsets, later_offsets = refs[:6]
-        refs = refs[6:]
-        offset_of = lambda j: line_offsets[j]
-        later_offset = later_offsets[...]
+        later_offset, *offsets = [ref[...] for ref in refs[: 1 + LINES]]
+        refs = refs[1 + LINES :]
     pick, halo, couple, chained, spread, up, down = refs
 
-    product = jnp.ones((ELEMENTS, WIDTH), F32)
-    offset = jnp.zeros((ELEMENTS, WIDTH), F32)
-    for j in reversed(range(LINES)):
-        offset = offset_of(j) + lines[j, 0:ELEMENTS] * offset
-        product = product * lines[j, 0:ELEMENTS]
-    value = offset / (1.0 - product)
+    product = lines[0][0:ELEMENTS]
+    offset = offsets[0]
     for j in reversed(range(1, LINES)):
-        value = jnp.where(halo[6] < j, offset_of(j) + lines[j, 0:ELEMENTS] * value, value)
-    value = later_offset + later[0:ELEMENTS] * value
+        offset = offsets[j] + lines[j][0:ELEMENTS] * offset
+        product = product * lines[j][0:ELEMENTS]
+    value = later_offset + later[0:ELEMENTS] * (offset / (1.0 - product))
     for t in reversed(range(SLABS)):
         value = field[t] + decay[t] * value
         chained[t] = value
@@ -259,7 +254,6 @@
     faces, pick, halo = tables
     depth = 2 * ELEMENTS if first else ELEMENTS
     along_z = [[y * RING + z for z in range(RING)] for y in range(LINES)]
-    along_y = [[y * RING + z for y in range(LINES)] for z in range(RING)]
 
     def compose(*refs):
         line_kernel(first, *refs)
@@ -271,15 +265,19 @@
     own = (gathered,) if first else (known[0], gathered)
     line, later = pl.pallas_call(
         compose,
-        out_shape=(struct(LINES, depth, WIDTH), struct(depth, WIDTH)),
+        out_shape=(struct(depth, WIDTH), struct(depth, WIDTH)),
         in_specs=[VMEM] * (1 + len(own)),
         out_specs=(VMEM,) * 2,
         compiler_params=params(SMALL_MIB),
-        cost_estimate=pl.CostEstimate(flops=10 * 10**9, bytes_accessed=2 * 10**6, transcendentals=0),
+        cost_estimate=HINT,
     )(halo, *own)
-    lines = along(line, along_y)
+    count = RING * LINES
+    lines = [line] + [
+        lax.ppermute(line, "tm", [((i + k * RING) % count, i) for i in range(count)])
+        for k in range(1, LINES)
+    ]
     if first:
-        known = (gathered, lines, later)
+        known = (gathered, later, *lines)
     chained, spread, up, down = pl.pallas_call(
         chain,
         out_shape=(
@@ -288,11 +286,11 @@
             struct(2, SLABS, WIDTH),
             struct(2, SLABS, WIDTH),
         ),
-        in_specs=[VMEM] * (7 if first else 9),
+        in_specs=[VMEM] * ((1 if first else 2) * (1 + LINES) + 5),
         out_specs=(VMEM,) * 4,
         compiler_params=params(OPERATE_MIB),
-        cost_estimate=pl.CostEstimate(flops=10 * 10**9, bytes_accessed=2 * 10**6, transcendentals=0),
-    )(field, decay, *known[1:], *(() if first else (lines, later)), pick, halo, couple)
+        cost_estimate=HINT,
+    )(field, decay, *known[1:], *(() if first else (later, *lines)), pick, halo, couple)
     below = lax.ppermute(up, "space", [(i, (i + 1) % 8) for i in range(8)])
     above = lax.ppermute(down, "space", [((i + 1) % 8, i) for i in range(8)])
     resident = RESIDENT[0 if first else 1]
@@ -454,13 +452,14 @@
         scratch_shapes=[pltpu.VMEM((SLABS, ELEMENTS, WIDTH), F32)] * 2
         + [pltpu.SemaphoreType.DMA((2,))],
         compiler_params=params(WHOLE_MIB),
+        cost_estimate=HINT,
     )(source, decay)
     *tables, source, decay, couple = pl.pallas_call(
         prepare_kernel,
         out_shape=(
             jax.ShapeDtypeStruct((FACES, 2 * ELEMENTS, 128), BF16),
             jax.ShapeDtypeStruct((4 * 2 * SLABS, 2 * ROWS), BF16),
-            struct(7, ELEMENTS, WIDTH),
+            struct(6, ELEMENTS, WIDTH),
             field_shape,
             field_shape,
             jax.ShapeDtypeStruct((2, 2, WIDTH, WIDTH), BF16),

time: 85.8 us -> 82.9 us (0.966)
  blocking collectives: 45.8 us -> 29.4 us
  waiting for transfers between devices: 3.59 us -> 12.7 us
  starting transfers between devices: 18.2 us -> 27.3 us
  local copies, waits for them, and re-layouts: 5.89 us -> 1.17 us
    all_to_all x3 -> x1, blocking collectives: 26.2 us -> 9.97 us  [along(): return lax.all_to_all(x, 'tm', 0, 0, axis_index_groups=groups, tiled=True)]
    ppermute x0 -> x6, starting transfers between devices: none -> 8.6 us  [operate(): lax.ppermute(line, 'tm', [((i + k * RING) % count, i) for i in range(coun...]
    all_to_all x1, waiting for transfers between devices: 2.17 us -> 6.86 us  [along(): return lax.all_to_all(x, 'tm', 0, 0, axis_index_groups=groups, tiled=True)]
    ppermute x0 -> x6, waiting for transfers between devices: none -> 4.44 us  [operate(): lax.ppermute(line, 'tm', [((i + k * RING) % count, i) for i in range(coun...]
    unnamed x16 -> x18, local copies, waits for them, and re-layouts: 3.81 us -> 0.04 us
    reshape x1, local copies, waits for them, and re-layouts: 2.07 us -> 1.14 us  [shards(): couple = interface_jacobian_blocks.reshape(2, 2, WIDTH, WIDTH)]
  transfers between devices with their start and end apart: 5 -> 11, of which waited for: 3 -> 8; matrix products, arithmetic and copies ran while one was open for 2% -> 1% of each run, Pallas kernels for 7% -> 7%
where the time goes in v3:
time: 82.9 us; the launch traced here: 82.6 us
  blocking collectives  29.4 us (35%)
  starting transfers between devices  27.3 us (33%)
  waiting for transfers between devices  12.7 us (15%)
  Pallas kernels  11.2 us (14%)
  local copies, waits for them, and re-layouts  1.17 us (1%)
  between operations  0.84 us (1%)
    all_to_all x1, blocking collectives, shards(): gram = lax.all_to_all(gram, ('tm', 'space'), 0, 0, tiled=True)  19.4 us
    all_to_all x1, blocking collectives, along(): return lax.all_to_all(x, 'tm', 0, 0, axis_index_groups=groups, tiled=True)  9.97 us
    ppermute x2, starting transfers between devices, operate(): below = lax.ppermute(up, 'space', [(i, (i + 1) % 8) for i in range(8)])  9.67 us
    all_to_all x1, starting transfers between devices, along(): return lax.all_to_all(x, 'tm', 0, 0, axis_index_groups=groups, tiled=True)  9.03 us
    ppermute x6, starting transfers between devices, operate(): lax.ppermute(line, 'tm', [((i + k * RING) % count, i) for i in range(coun...  8.6 us
    all_to_all x1, waiting for transfers between devices, along(): return lax.all_to_all(x, 'tm', 0, 0, axis_index_groups=groups, tiled=True)  6.86 us
    pallas_call x2, Pallas kernels, operate(): pl.pallas_call(local_part, out_shape=struct(SLABS, ELEMENTS, WIDTH), in_s...  5.33 us
    ppermute x6, waiting for transfers between devices, operate(): lax.ppermute(line, 'tm', [((i + k * RING) % count, i) for i in range(coun...  4.44 us
  transfers between devices with their start and end apart: 11, of which 8 were waited for; matrix products, arithmetic and copies ran while one was open for 1% of the time, Pallas kernels for 7%

profile of v3, /device:TPU:1, one launch (start us, length us, event | category | flops | bytes accessed | tf_op | source)
XLA Modules:
  0.0 82.6 jit_solution(5636820022290898040)
XLA Ops:
  0.6 0.0 copy-start.5
  0.6 0.0 copy-start
  0.7 0.0 copy-start.1
  0.7 0.0 copy-start.2
  0.7 0.0 copy-start.3
  0.7 0.0 copy-start.4
  0.7 1.7 %shard_map.87 = f32[8,16,320]{2,1,0:T(8,128)} custom-call(f32[8,8,320]{2,1,0:T(8,128)} %bitcast.22, f32[8,8,320]{2,1,0:T(8,128)} %bitcast.24), custom_call_target="tpu_custom_call" | custom-call | flops 10000000000 | bytes 1000000 | tf_op jit(solution)/shard_map/pallas_call | solution.py:447
  2.4 9.0 %all-to-all-start = ((f32[8,16,320]{2,1,0:T(8,128)}), f32[8,16,320]{2,1,0:T(8,128)S(1)}, u32[]{:S(2)}, u32[]{:S(2)}) async-start(f32[8,16,320]{2,1,0:T(8,128)} %shard_map.87), calls=%async_computation | async-start | bytes 393216 | tf_op jit(solution)/shard_map/all_to_all | solution.py:250
  11.5 0.0 copy-done.5
  11.5 1.1 %reshape.19.couple = bf16[2,2,320,320]{3,2,1,0:T(8,128)(2,1)S(1)} reshape(bf16[2,2,102400]{2,1,0:T(2,128)(2,1)S(1)} %copy-done.5) | data formatting | bytes 1638400 | tf_op jit(solution)/shard_map/reshape | solution.py:444
  12.6 0.0 copy-done
  12.6 0.0 copy-done.1
  12.6 0.0 copy-done.2
  12.6 0.0 copy-done.3
  12.6 0.0 copy-done.4
  12.7 0.7 shard_map.86
  13.4 6.9 %all-to-all-done.refs_1_ = f32[8,16,320]{2,1,0:T(8,128)S(1)} async-done(((f32[8,16,320]{2,1,0:T(8,128)}), f32[8,16,320]{2,1,0:T(8,128)S(1)}, u32[]{:S(2)}, u32[]{:S(2)}) %all-to-all-start) | async-done | bytes 163872 | tf_op jit(solution)/shard_map/all_to_all | solution.py:250
  20.3 0.0 slice-start
  20.3 0.0 slice-start.1
  20.3 1.4 %collective-permute-start.2 = (f32[16,320]{1,0:T(8,128)S(1)}, f32[16,320]{1,0:T(8,128)S(1)}, u32[]{:S(2)}, u32[]{:S(2)}) collective-permute-start(f32[16,320]{1,0:T(8,128)S(1)} %get-tuple-element.30.refs_3_), channel_id=1, source_target_pairs={{192,0},{200,8},{208,16},{216,24},{224,32},{232,40},{240,48},{248,... | collective-permute-start | bytes 61448 | tf_op jit(solution)/shard_map/ppermute | solution.py:276
  21.7 2.6 %collective-permute-start.1 = (f32[16,320]{1,0:T(8,128)S(1)}, f32[16,320]{1,0:T(8,128)S(1)}, u32[]{:S(2)}, u32[]{:S(2)}) collective-permute-start(f32[16,320]{1,0:T(8,128)S(1)} %get-tuple-element.30.refs_3_), channel_id=1, source_target_pairs={{128,0},{136,8},{144,16},{152,24},{160,32},{168,40},{176,48},{184,... | collective-permute-start | bytes 61448 | tf_op jit(solution)/shard_map/ppermute | solution.py:276
  24.3 1.1 %collective-permute-start = (f32[16,320]{1,0:T(8,128)S(1)}, f32[16,320]{1,0:T(8,128)S(1)}, u32[]{:S(2)}, u32[]{:S(2)}) collective-permute-start(f32[16,320]{1,0:T(8,128)S(1)} %get-tuple-element.30.refs_3_), channel_id=1, source_target_pairs={{64,0},{72,8},{80,16},{88,24},{96,32},{104,40},{112,48},{120,56},{... | collective-permute-start | bytes 61448 | tf_op jit(solution)/shard_map/ppermute | solution.py:276
  25.4 0.0 collective-permute-done.2.refs_6_
  25.4 0.5 collective-permute-done.1.refs_5_
  25.9 1.4 %collective-permute-done.refs_4_ = f32[16,320]{1,0:T(8,128)S(1)} collective-permute-done((f32[16,320]{1,0:T(8,128)S(1)}, f32[16,320]{1,0:T(8,128)S(1)}, u32[]{:S(2)}, u32[]{:S(2)}) %collective-permute-start) | collective-permute-done | bytes 20512 | tf_op jit(solution)/shard_map/ppermute | solution.py:276
  27.3 0.0 slice-start.2
  27.3 1.0 %shard_map.89 = (f32[8,8,320]{2,1,0:T(8,128)S(1)}, bf16[256,1280]{1,0:T(8,128)(2,1)S(1)}, f32[2,8,320]{2,1,0:T(8,128)S(1)}, f32[2,8,320]{2,1,0:T(8,128)S(1)}) custom-call(f32[8,8,320]{2,1,0:T(8,128)S(1)} %get-tuple-element.27.refs_0_.source, f32[8,8,320]{2,1,0:T(8,128)S(1)} %get-tuple-element.28.refs_1_.decay, f32[16,320]{1,0:T(8,128)S(1)} %get-tuple-element.29.refs_2_, ...), custom_call_target="tpu_custom_call" | custom-call | flops 10000000000 | bytes 1000000 | tf_op jit(solution)/shard_map/pallas_call | solution.py:281
  28.2 5.1 %collective-permute-start.3 = (f32[2,8,320]{2,1,0:T(8,128)S(1)}, f32[2,8,320]{2,1,0:T(8,128)S(1)}, u32[]{:S(2)}, u32[]{:S(2)}) collective-permute-start(f32[2,8,320]{2,1,0:T(8,128)S(1)} %get-tuple-element.35), channel_id=1, source_target_pairs={{0,1},{1,2},{2,3},{3,4},{4,5},{5,6},{6,7},{7,0},{8,9},{9,10},{10,1... | collective-permute-start | bytes 61448 | tf_op jit(solution)/shard_map/ppermute | solution.py:294
  33.4 0.0 collective-permute-start.4
  33.4 0.0 slice-done
  33.4 0.0 slice-done.1
  33.4 0.0 slice-done.2
  33.4 2.6 %shard_map.90.local = f32[8,8,320]{2,1,0:T(8,128)S(1)} custom-call(bf16[256,1280]{1,0:T(8,128)(2,1)S(1)} %get-tuple-element.33.refs_0_, bf16[7,16,128]{2,1,0:T(8,128)(2,1)S(1)} %get-tuple-element.34.refs_1_, bf16[7,1280,640]{2,1,0:T(8,128)(2,1)S(1)} %bitcast.18), custom_call_target="tpu_custom_call" | custom-call | flops 2936012800 | bytes 11468800 | tf_op jit(solution)/shard_map/pallas_call | solution.py:312
  36.0 0.0 collective-permute-done.3.below
  36.1 0.6 collective-permute-done.4.above
  36.6 0.1 shard_map.91
  36.7 10.0 %all_to_all.21.refs_2_ = f32[8,8,320]{2,1,0:T(8,128)S(1)} all-to-all(f32[8,8,320]{2,1,0:T(8,128)S(1)} %get-tuple-element.38), channel_id=1, replica_groups={{0,8,16,24,32,40,48,56},{64,72,80,88,96,104,112,120},{128,136,144,152,1..., dimensions={0} | all-to-all | bytes 163840 | tf_op jit(solution)/shard_map/all_to_all | solution.py:250
  46.7 0.1 collective-permute-start.7
  46.8 3.5 %collective-permute-start.6 = (f32[8,320]{1,0:T(8,128)S(1)}, f32[8,320]{1,0:T(8,128)S(1)}, u32[]{:S(2)}, u32[]{:S(2)}) collective-permute-start(f32[8,320]{1,0:T(8,128)S(1)} %get-tuple-element.40.refs_8_), channel_id=1, source_target_pairs={{128,0},{136,8},{144,16},{152,24},{160,32},{168,40},{176,48},{184,... | collective-permute-start | bytes 30728 | tf_op jit(solution)/shard_map/ppermute | solution.py:276
  50.2 0.0 collective-permute-start.5
  50.2 0.3 collective-permute-done.7.refs_11_
  50.5 0.9 %collective-permute-done.6.refs_10_ = f32[8,320]{1,0:T(8,128)S(1)} collective-permute-done((f32[8,320]{1,0:T(8,128)S(1)}, f32[8,320]{1,0:T(8,128)S(1)}, u32[]{:S(2)}, u32[]{:S(2)}) %collective-permute-start.6) | collective-permute-done | bytes 10272 | tf_op jit(solution)/shard_map/ppermute | solution.py:276
  51.4 1.3 %collective-permute-done.5.refs_9_ = f32[8,320]{1,0:T(8,128)S(1)} collective-permute-done((f32[8,320]{1,0:T(8,128)S(1)}, f32[8,320]{1,0:T(8,128)S(1)}, u32[]{:S(2)}, u32[]{:S(2)}) %collective-permute-start.5) | collective-permute-done | bytes 10272 | tf_op jit(solution)/shard_map/ppermute | solution.py:276
  52.8 1.0 %shard_map.93 = (f32[8,8,320]{2,1,0:T(8,128)S(1)}, bf16[256,1280]{1,0:T(8,128)(2,1)S(1)}, f32[2,8,320]{2,1,0:T(8,128)S(1)}, f32[2,8,320]{2,1,0:T(8,128)S(1)}) custom-call(f32[8,8,320]{2,1,0:T(8,128)S(1)} %get-tuple-element.37.refs_0_.image0, f32[8,8,320]{2,1,0:T(8,128)S(1)} %get-tuple-element.28.refs_1_.decay, f32[16,320]{1,0:T(8,128)S(1)} %get-tuple-element.29.refs_2_, ...), custom_call_target="tpu_custom_call" | custom-call | flops 10000000000 | bytes 1000000 | tf_op jit(solution)/shard_map/pallas_call | solution.py:281
  53.8 4.5 %collective-permute-start.8 = (f32[2,8,320]{2,1,0:T(8,128)S(1)}, f32[2,8,320]{2,1,0:T(8,128)S(1)}, u32[]{:S(2)}, u32[]{:S(2)}) collective-permute-start(f32[2,8,320]{2,1,0:T(8,128)S(1)} %get-tuple-element.42), channel_id=1, source_target_pairs={{0,1},{1,2},{2,3},{3,4},{4,5},{5,6},{6,7},{7,0},{8,9},{9,10},{10,1... | collective-permute-start | bytes 61448 | tf_op jit(solution)/shard_map/ppermute | solution.py:294
  58.3 0.0 collective-permute-start.9
  58.3 2.7 %shard_map.94.local = f32[8,8,320]{2,1,0:T(8,128)S(1)} custom-call(bf16[256,1280]{1,0:T(8,128)(2,1)S(1)} %get-tuple-element.41.refs_0_, bf16[7,16,128]{2,1,0:T(8,128)(2,1)S(1)} %get-tuple-element.34.refs_1_, bf16[7,1280,640]{2,1,0:T(8,128)(2,1)S(1)} %bitcast.19), custom_call_target="tpu_custom_call" | custom-call | flops 2936012800 | bytes 11468800 | tf_op jit(solution)/shard_map/pallas_call | solution.py:312
  61.0 0.0 collective-permute-done.8.below
  61.0 0.8 %collective-permute-done.9.above = f32[2,8,320]{2,1,0:T(8,128)S(1)} collective-permute-done((f32[2,8,320]{2,1,0:T(8,128)S(1)}, f32[2,8,320]{2,1,0:T(8,128)S(1)}, u32[]{:S(2)}, u32[]{:S(2)}) %collective-permute-start.9) | collective-permute-done | bytes 20512 | tf_op jit(solution)/shard_map/ppermute | solution.py:295
  61.9 0.3 shard_map.95
  62.2 19.4 %all_to_all.22 = f32[256,1,128]{2,1,0:T(1,128)S(1)} all-to-all(f32[256,1,128]{2,1,0:T(1,128)S(1)} %bitcast.21), channel_id=1, replica_groups=mesh['tm'=32,'space'=8] {'tm','space'}, dimensions={0} | all-to-all | bytes 262144 | tf_op jit(solution)/shard_map/all_to_all | solution.py:492
  81.6 1.0 %shard_map.96 = (f32[8,8,320]{2,1,0:T(8,128)}, f32[8,8,320]{2,1,0:T(8,128)}) custom-call(f32[256,128]{1,0:T(8,128)S(1)} %bitcast.20, f32[8,8,320]{2,1,0:T(8,128)S(1)} %get-tuple-element.27.refs_0_.source, f32[8,8,320]{2,1,0:T(8,128)S(1)} %get-tuple-element.45.first_chain, f32[8,8,320]{2,1,0:T(8,128)S(1)} %get-tuple-element.46.second_chain, ...), custom_call_target="tpu_custom_call" | custom-call | tf_op jit(solution)/shard_map/pallas_call | solution.py:493
  (3 shorter events, 0.1 us)
Async XLA Ops:
  0.6 10.8 %copy-start.5 = (bf16[2,2,102400]{2,1,0:T(2,128)(2,1)S(1)}, bf16[2,2,102400]{2,1,0:T(2,128)(2,1)}, u32[]{:S(2)}) copy-start(bf16[2,2,102400]{2,1,0:T(2,128)(2,1)} %param.11) | copy-start | bytes 2457604
  0.6 12.0 %copy-start = (f32[8,320,8]{1,2,0:T(8,128)S(1)}, f32[8,320,8]{1,2,0:T(8,128)}, u32[]{:S(2)}) copy-start(f32[8,320,8]{1,2,0:T(8,128)} %param.7) | copy-start | bytes 245764
  0.7 12.0 %copy-start.1 = (f32[8,320,8]{1,2,0:T(8,128)S(1)}, f32[8,320,8]{1,2,0:T(8,128)}, u32[]{:S(2)}) copy-start(f32[8,320,8]{1,2,0:T(8,128)} %param.8) | copy-start | bytes 245764
  0.7 12.0 %copy-start.2 = (s32[6,8]{1,0:T(8,128)S(1)}, s32[6,8]{1,0:T(8,128)}, u32[]{:S(2)}) copy-start(s32[6,8]{1,0:T(8,128)} %neighbours.1) | copy-start | bytes 580
  0.7 12.0 %copy-start.3 = (s32[2,2]{1,0:T(2,128)S(1)}, s32[2,2]{1,0:T(2,128)}, u32[]{:S(2)}) copy-start(s32[2,2]{1,0:T(2,128)} %owner.1) | copy-start | bytes 52
  0.7 12.0 %copy-start.4 = (s32[1,2]{1,0:T(1,128)S(1)}, s32[1,2]{1,0:T(1,128)}, u32[]{:S(2)}) copy-start(s32[1,2]{1,0:T(1,128)} %pairing.1) | copy-start | bytes 28
  2.4 17.8 %all-to-all-start = ((f32[8,16,320]{2,1,0:T(8,128)}), f32[8,16,320]{2,1,0:T(8,128)S(1)}, u32[]{:S(2)}, u32[]{:S(2)}) async-start(f32[8,16,320]{2,1,0:T(8,128)} %shard_map.87), calls=%async_computation | async-start | bytes 393216 | tf_op jit(solution)/shard_map/all_to_all | solution.py:250
  20.3 13.1 %slice-start = ((s8[11468800]{0:T(1024)(128)(4,1)}), s8[4194304]{0:T(1024)(128)(4,1)S(1)}, s32[]{:S(2)}) async-start(s8[11468800]{0:T(1024)(128)(4,1)} %bitcast.16), calls=%async_computation.3 | async-start | bytes 8388608
  20.3 13.1 %slice-start.1 = ((s8[11468800]{0:T(1024)(128)(4,1)}), s8[4194304]{0:T(1024)(128)(4,1)S(1)}, s32[]{:S(2)}) async-start(s8[11468800]{0:T(1024)(128)(4,1)} %bitcast.16), calls=%async_computation.4 | async-start | bytes 8388608
  20.3 5.1 %collective-permute-start.2 = (f32[16,320]{1,0:T(8,128)S(1)}, f32[16,320]{1,0:T(8,128)S(1)}, u32[]{:S(2)}, u32[]{:S(2)}) collective-permute-start(f32[16,320]{1,0:T(8,128)S(1)} %get-tuple-element.30.refs_3_), channel_id=1, source_target_pairs={{192,0},{200,8},{208,16},{216,24},{224,32},{232,40},{240,48},{248,... | collective-permute-start | bytes 61448 | tf_op jit(solution)/shard_map/ppermute | solution.py:276
  21.7 4.2 %collective-permute-start.1 = (f32[16,320]{1,0:T(8,128)S(1)}, f32[16,320]{1,0:T(8,128)S(1)}, u32[]{:S(2)}, u32[]{:S(2)}) collective-permute-start(f32[16,320]{1,0:T(8,128)S(1)} %get-tuple-element.30.refs_3_), channel_id=1, source_target_pairs={{128,0},{136,8},{144,16},{152,24},{160,32},{168,40},{176,48},{184,... | collective-permute-start | bytes 61448 | tf_op jit(solution)/shard_map/ppermute | solution.py:276
  24.3 3.0 %collective-permute-start = (f32[16,320]{1,0:T(8,128)S(1)}, f32[16,320]{1,0:T(8,128)S(1)}, u32[]{:S(2)}, u32[]{:S(2)}) collective-permute-start(f32[16,320]{1,0:T(8,128)S(1)} %get-tuple-element.30.refs_3_), channel_id=1, source_target_pairs={{64,0},{72,8},{80,16},{88,24},{96,32},{104,40},{112,48},{120,56},{... | collective-permute-start | bytes 61448 | tf_op jit(solution)/shard_map/ppermute | solution.py:276
  27.3 6.1 %slice-start.2 = ((s8[11468800]{0:T(1024)(128)(4,1)}), s8[3080192]{0:T(1024)(128)(4,1)S(1)}, s32[]{:S(2)}) async-start(s8[11468800]{0:T(1024)(128)(4,1)} %bitcast.16), calls=%async_computation.5 | async-start | bytes 6160384
  28.2 7.8 %collective-permute-start.3 = (f32[2,8,320]{2,1,0:T(8,128)S(1)}, f32[2,8,320]{2,1,0:T(8,128)S(1)}, u32[]{:S(2)}, u32[]{:S(2)}) collective-permute-start(f32[2,8,320]{2,1,0:T(8,128)S(1)} %get-tuple-element.35), channel_id=1, source_target_pairs={{0,1},{1,2},{2,3},{3,4},{4,5},{5,6},{6,7},{7,0},{8,9},{9,10},{10,1... | collective-permute-start | bytes 61448 | tf_op jit(solution)/shard_map/ppermute | solution.py:294
  33.4 3.3 %collective-permute-start.4 = (f32[2,8,320]{2,1,0:T(8,128)S(1)}, f32[2,8,320]{2,1,0:T(8,128)S(1)}, u32[]{:S(2)}, u32[]{:S(2)}) collective-permute-start(f32[2,8,320]{2,1,0:T(8,128)S(1)} %get-tuple-element.36), channel_id=1, source_target_pairs={{1,0},{2,1},{3,2},{4,3},{5,4},{6,5},{7,6},{0,7},{9,8},{10,9},{11,1... | collective-permute-start | bytes 61448 | tf_op jit(solution)/shard_map/ppermute | solution.py:295
  46.7 3.8 %collective-permute-start.7 = (f32[8,320]{1,0:T(8,128)S(1)}, f32[8,320]{1,0:T(8,128)S(1)}, u32[]{:S(2)}, u32[]{:S(2)}) collective-permute-start(f32[8,320]{1,0:T(8,128)S(1)} %get-tuple-element.40.refs_8_), channel_id=1, source_target_pairs={{192,0},{200,8},{208,16},{216,24},{224,32},{232,40},{240,48},{248,... | collective-permute-start | bytes 30728 | tf_op jit(solution)/shard_map/ppermute | solution.py:276
  46.8 4.7 %collective-permute-start.6 = (f32[8,320]{1,0:T(8,128)S(1)}, f32[8,320]{1,0:T(8,128)S(1)}, u32[]{:S(2)}, u32[]{:S(2)}) collective-permute-start(f32[8,320]{1,0:T(8,128)S(1)} %get-tuple-element.40.refs_8_), channel_id=1, source_target_pairs={{128,0},{136,8},{144,16},{152,24},{160,32},{168,40},{176,48},{184,... | collective-permute-start | bytes 30728 | tf_op jit(solution)/shard_map/ppermute | solution.py:276
  50.2 2.5 %collective-permute-start.5 = (f32[8,320]{1,0:T(8,128)S(1)}, f32[8,320]{1,0:T(8,128)S(1)}, u32[]{:S(2)}, u32[]{:S(2)}) collective-permute-start(f32[8,320]{1,0:T(8,128)S(1)} %get-tuple-element.40.refs_8_), channel_id=1, source_target_pairs={{64,0},{72,8},{80,16},{88,24},{96,32},{104,40},{112,48},{120,56},{... | collective-permute-start | bytes 30728 | tf_op jit(solution)/shard_map/ppermute | solution.py:276
  53.8 7.3 %collective-permute-start.8 = (f32[2,8,320]{2,1,0:T(8,128)S(1)}, f32[2,8,320]{2,1,0:T(8,128)S(1)}, u32[]{:S(2)}, u32[]{:S(2)}) collective-permute-start(f32[2,8,320]{2,1,0:T(8,128)S(1)} %get-tuple-element.42), channel_id=1, source_target_pairs={{0,1},{1,2},{2,3},{3,4},{4,5},{5,6},{6,7},{7,0},{8,9},{9,10},{10,1... | collective-permute-start | bytes 61448 | tf_op jit(solution)/shard_map/ppermute | solution.py:294
  58.3 3.5 %collective-permute-start.9 = (f32[2,8,320]{2,1,0:T(8,128)S(1)}, f32[2,8,320]{2,1,0:T(8,128)S(1)}, u32[]{:S(2)}, u32[]{:S(2)}) collective-permute-start(f32[2,8,320]{2,1,0:T(8,128)S(1)} %get-tuple-element.43), channel_id=1, source_target_pairs={{1,0},{2,1},{3,2},{4,3},{5,4},{6,5},{7,6},{0,7},{9,8},{10,9},{11,1... | collective-permute-start | bytes 61448 | tf_op jit(solution)/shard_map/ppermute | solution.py:295

commit v4 on v3

--- a/solution.py
+++ b/solution.py
@@ -23,8 +23,6 @@
 SPAN = 1024
 SMALL_MIB = 4
 OPERATE_MIB = 8
-WIDE_MIB = 46
-RESIDENT = (True, True)
 WHOLE_MIB = 54
 
 VMEM = pl.BlockSpec(memory_space=pltpu.VMEM)
@@ -109,14 +107,15 @@
     )
     pick[...] = chosen((row % (2 * SLABS)) * ELEMENTS + element == col).astype(BF16)
 
-    e = iota((2 * ELEMENTS, 128), 1) % ELEMENTS
-    d = iota((2 * ELEMENTS, 128), 0) % ELEMENTS
-    for f in range(FACES):
-        to = e
-        if f > 0:
-            for k in range(ELEMENTS):
-                to = jnp.where(e == k, neighbours[f - 1, k], to)
-        faces[f] = chosen(to == d).astype(BF16)
+    shape = (ROWS, (FACES - 1) * ROWS)
+    row, col = iota(shape, 0), iota(shape, 1)
+    face, e = col // ROWS, col % ELEMENTS
+    to = e
+    for f in range(FACES - 1):
+        for k in range(ELEMENTS):
+            to = jnp.where((face == f) & (e == k), neighbours[f, k], to)
+    lands = (col % ROWS) // ELEMENTS * ELEMENTS + to == row
+    faces[...] = chosen(lands).astype(BF16)
 
 
 def line_kernel(first, *refs):
@@ -189,7 +188,6 @@
     down[0] = jnp.where(straight, products[2], products[3])
     down[1] = jnp.where(straight, products[3], products[2])
 
-    same = jnp.where(iota((128, 128), 0) // 8 == iota((128, 128), 1) // 8, 1.0, 0.0).astype(BF16)
     own = iota((2 * ROWS, DEPTH), 0) % ELEMENTS == iota((2 * ROWS, DEPTH), 1) % ELEMENTS
     n = iota((256, SPAN), 0)
     lane = iota((256, SPAN), 1)
@@ -202,47 +200,43 @@
             ],
             axis=1,
         )
-        wide = jnp.where(own, wide, 0.0).astype(BF16)
-        spread[b * 2 * ROWS : (b + 1) * 2 * ROWS] = jnp.dot(
-            same, wide, preferred_element_type=F32
-        ).astype(BF16)
-
-
-def local_kernel(resident, *refs):
-    if resident:
-        spread, faces, weights, local, low, middle, high = refs
-    else:
-        spread, faces, stored, local, weights, low, middle, high, sems = refs
-        copies = [
-            pltpu.make_async_copy(stored.at[f], weights.at[f], sems.at[f]) for f in range(FACES)
-        ]
-        for copy in copies:
-            copy.start()
+        spread[b * 2 * ROWS : (b + 1) * 2 * ROWS] = jnp.where(own, wide, 0.0).astype(BF16)
+
+
+def local_kernel(spread, faces, weights, local):
     half = 2 * ROWS
-    for f in range(FACES):
-        mask = jnp.concatenate([faces[f]] * (DEPTH // 128), axis=1)
-        mask = jnp.concatenate([mask] * (4 * ROWS // 16), axis=0)
-        left = spread[...] * mask
-        if not resident:
-            copies[f].wait()
-        parts = (
-            (low, left[:half], slice(0, 256)),
-            (middle, left, slice(256, 384)),
-            (high, left[half:], slice(384, LANES)),
+
+    def paired(x):
+        return x[:ROWS] + x[ROWS:]
+
+    def products(some):
+        both = jnp.dot(
+            spread[...],
+            jnp.concatenate([weights[f, :, 256:384] for f in some], axis=1),
+            preferred_element_type=F32,
         )
-        for sums, rows, lanes in parts:
-            part = jnp.dot(rows, weights[f, :, lanes], preferred_element_type=F32)
-            if f == 0:
-                sums[...] = part
-            else:
-                sums[...] += part
-    even = low[:ROWS] + low[ROWS:]
-    even_end = middle[:ROWS] + middle[ROWS:half]
-    odd_start = middle[half : half + ROWS] + middle[half + ROWS :]
-    odd = high[:ROWS] + high[ROWS:]
-    result = jnp.concatenate([even, even_end[:, :64]], axis=1) + jnp.concatenate(
-        [odd_start[:, 64:], odd], axis=1
-    )
+        results = []
+        for i, f in enumerate(some):
+            low = jnp.dot(spread[:half], weights[f, :, :256], preferred_element_type=F32)
+            high = jnp.dot(spread[half:], weights[f, :, 384:], preferred_element_type=F32)
+            even = paired(both[:half, i * 128 : i * 128 + 64])
+            odd = paired(both[half:, i * 128 + 64 : (i + 1) * 128])
+            results.append(
+                jnp.concatenate([paired(low), even], axis=1)
+                + jnp.concatenate([odd, paired(high)], axis=1)
+            )
+        return results
+
+    result = jnp.zeros((ROWS, WIDTH), F32)
+    placed = []
+    for some in ((1, 2), (3, 4), (5, 6)):
+        placed += products(some)
+    placed = jnp.concatenate(placed, axis=0)
+    high = placed.astype(BF16)
+    low = (placed - high.astype(F32)).astype(BF16)
+    for part in (high, low):
+        result = result + jnp.dot(faces[...], part, preferred_element_type=F32)
+    result = result + products((0,))[0]
     local[...] = result.reshape(SLABS, ELEMENTS, WIDTH)
 
 
@@ -293,29 +287,12 @@
     )(field, decay, *known[1:], *(() if first else (later, *lines)), pick, halo, couple)
     below = lax.ppermute(up, "space", [(i, (i + 1) % 8) for i in range(8)])
     above = lax.ppermute(down, "space", [((i + 1) % 8, i) for i in range(8)])
-    resident = RESIDENT[0 if first else 1]
-
-    def local_part(*refs):
-        local_kernel(resident, *refs)
-
-    scratch = [
-        pltpu.VMEM((2 * ROWS, 256), F32),
-        pltpu.VMEM((4 * ROWS, 128), F32),
-        pltpu.VMEM((2 * ROWS, 256), F32),
-    ]
-    if not resident:
-        scratch = [
-            pltpu.VMEM((FACES, DEPTH, LANES), BF16),
-            *scratch,
-            pltpu.SemaphoreType.DMA((FACES,)),
-        ]
     local = pl.pallas_call(
-        local_part,
+        local_kernel,
         out_shape=struct(SLABS, ELEMENTS, WIDTH),
-        in_specs=[VMEM] * 2 + [VMEM if resident else HBM],
+        in_specs=[VMEM] * 3,
         out_specs=VMEM,
-        scratch_shapes=scratch,
-        compiler_params=params(OPERATE_MIB if resident else WIDE_MIB),
+        compiler_params=params(OPERATE_MIB),
         cost_estimate=pl.CostEstimate(
             flops=2 * FACES * 4 * ROWS * DEPTH * LANES,
             bytes_accessed=2 * FACES * DEPTH * LANES,
@@ -457,7 +434,7 @@
     *tables, source, decay, couple = pl.pallas_call(
         prepare_kernel,
         out_shape=(
-            jax.ShapeDtypeStruct((FACES, 2 * ELEMENTS, 128), BF16),
+            jax.ShapeDtypeStruct((ROWS, (FACES - 1) * ROWS), BF16),
             jax.ShapeDtypeStruct((4 * 2 * SLABS, 2 * ROWS), BF16),
             struct(6, ELEMENTS, WIDTH),
             field_shape,

time: 82.9 us -> 81.9 us (0.988)
  Pallas kernels: 11.2 us -> 10.3 us
where the time goes in v4:
time: 81.9 us; the launch traced here: 81.7 us
  blocking collectives  29.3 us (36%)
  starting transfers between devices  26.9 us (33%)
  waiting for transfers between devices  13.1 us (16%)
  Pallas kernels  10.3 us (13%)
  local copies, waits for them, and re-layouts  1.17 us (1%)
  between operations  0.84 us (1%)
    all_to_all x1, blocking collectives, shards(): gram = lax.all_to_all(gram, ('tm', 'space'), 0, 0, tiled=True)  19.2 us
    all_to_all x1, blocking collectives, along(): return lax.all_to_all(x, 'tm', 0, 0, axis_index_groups=groups, tiled=True)  10.1 us
    ppermute x2, starting transfers between devices, operate(): below = lax.ppermute(up, 'space', [(i, (i + 1) % 8) for i in range(8)])  9.3 us
    all_to_all x1, starting transfers between devices, along(): return lax.all_to_all(x, 'tm', 0, 0, axis_index_groups=groups, tiled=True)  9.03 us
    ppermute x6, starting transfers between devices, operate(): lax.ppermute(line, 'tm', [((i + k * RING) % count, i) for i in range(coun...  8.6 us
    all_to_all x1, waiting for transfers between devices, along(): return lax.all_to_all(x, 'tm', 0, 0, axis_index_groups=groups, tiled=True)  6.84 us
    pallas_call x2, Pallas kernels, operate(): pl.pallas_call(local_kernel, out_shape=struct(SLABS, ELEMENTS, WIDTH), in...  5.03 us
    ppermute x6, waiting for transfers between devices, operate(): lax.ppermute(line, 'tm', [((i + k * RING) % count, i) for i in range(coun...  4.74 us
  transfers between devices with their start and end apart: 11, of which 8 were waited for; matrix products, arithmetic and copies ran while one was open for 1% of the time, Pallas kernels for 7%

profile of v4, /device:TPU:1, one launch (start us, length us, event | category | flops | bytes accessed | tf_op | source)
XLA Modules:
  0.0 81.7 jit_solution(2855178636913706663)
XLA Ops:
  0.6 0.0 copy-start.5
  0.6 0.0 copy-start
  0.7 0.0 copy-start.1
  0.7 0.0 copy-start.2
  0.7 0.0 copy-start.3
  0.7 0.0 copy-start.4
  0.7 1.7 %shard_map.87 = f32[8,16,320]{2,1,0:T(8,128)} custom-call(f32[8,8,320]{2,1,0:T(8,128)} %bitcast.22, f32[8,8,320]{2,1,0:T(8,128)} %bitcast.24), custom_call_target="tpu_custom_call" | custom-call | flops 10000000000 | bytes 1000000 | tf_op jit(solution)/shard_map/pallas_call | solution.py:424
  2.4 9.0 %all-to-all-start = ((f32[8,16,320]{2,1,0:T(8,128)}), f32[8,16,320]{2,1,0:T(8,128)S(1)}, u32[]{:S(2)}, u32[]{:S(2)}) async-start(f32[8,16,320]{2,1,0:T(8,128)} %shard_map.87), calls=%async_computation | async-start | bytes 393216 | tf_op jit(solution)/shard_map/all_to_all | solution.py:244
  11.5 0.0 copy-done.5
  11.5 1.1 %reshape.19.couple = bf16[2,2,320,320]{3,2,1,0:T(8,128)(2,1)S(1)} reshape(bf16[2,2,102400]{2,1,0:T(2,128)(2,1)S(1)} %copy-done.5) | data formatting | bytes 1638400 | tf_op jit(solution)/shard_map/reshape | solution.py:421
  12.6 0.0 copy-done
  12.6 0.0 copy-done.1
  12.6 0.0 copy-done.2
  12.6 0.0 copy-done.3
  12.6 0.0 copy-done.4
  12.7 0.8 shard_map.86
  13.4 6.8 %all-to-all-done.refs_1_ = f32[8,16,320]{2,1,0:T(8,128)S(1)} async-done(((f32[8,16,320]{2,1,0:T(8,128)}), f32[8,16,320]{2,1,0:T(8,128)S(1)}, u32[]{:S(2)}, u32[]{:S(2)}) %all-to-all-start) | async-done | bytes 163872 | tf_op jit(solution)/shard_map/all_to_all | solution.py:244
  20.3 0.0 slice-start
  20.3 0.0 slice-start.1
  20.3 1.4 %collective-permute-start.2 = (f32[16,320]{1,0:T(8,128)S(1)}, f32[16,320]{1,0:T(8,128)S(1)}, u32[]{:S(2)}, u32[]{:S(2)}) collective-permute-start(f32[16,320]{1,0:T(8,128)S(1)} %get-tuple-element.30.refs_3_), channel_id=1, source_target_pairs={{192,0},{200,8},{208,16},{216,24},{224,32},{232,40},{240,48},{248,... | collective-permute-start | bytes 61448 | tf_op jit(solution)/shard_map/ppermute | solution.py:270
  21.7 2.6 %collective-permute-start.1 = (f32[16,320]{1,0:T(8,128)S(1)}, f32[16,320]{1,0:T(8,128)S(1)}, u32[]{:S(2)}, u32[]{:S(2)}) collective-permute-start(f32[16,320]{1,0:T(8,128)S(1)} %get-tuple-element.30.refs_3_), channel_id=1, source_target_pairs={{128,0},{136,8},{144,16},{152,24},{160,32},{168,40},{176,48},{184,... | collective-permute-start | bytes 61448 | tf_op jit(solution)/shard_map/ppermute | solution.py:270
  24.3 1.1 %collective-permute-start = (f32[16,320]{1,0:T(8,128)S(1)}, f32[16,320]{1,0:T(8,128)S(1)}, u32[]{:S(2)}, u32[]{:S(2)}) collective-permute-start(f32[16,320]{1,0:T(8,128)S(1)} %get-tuple-element.30.refs_3_), channel_id=1, source_target_pairs={{64,0},{72,8},{80,16},{88,24},{96,32},{104,40},{112,48},{120,56},{... | collective-permute-start | bytes 61448 | tf_op jit(solution)/shard_map/ppermute | solution.py:270
  25.4 0.0 collective-permute-done.2.refs_6_
  25.4 0.5 collective-permute-done.1.refs_5_
  25.9 1.4 %collective-permute-done.refs_4_ = f32[16,320]{1,0:T(8,128)S(1)} collective-permute-done((f32[16,320]{1,0:T(8,128)S(1)}, f32[16,320]{1,0:T(8,128)S(1)}, u32[]{:S(2)}, u32[]{:S(2)}) %collective-permute-start) | collective-permute-done | bytes 20512 | tf_op jit(solution)/shard_map/ppermute | solution.py:270
  27.3 0.0 slice-start.2
  27.3 0.6 shard_map.89
  27.9 5.1 %collective-permute-start.3 = (f32[2,8,320]{2,1,0:T(8,128)S(1)}, f32[2,8,320]{2,1,0:T(8,128)S(1)}, u32[]{:S(2)}, u32[]{:S(2)}) collective-permute-start(f32[2,8,320]{2,1,0:T(8,128)S(1)} %get-tuple-element.35), channel_id=1, source_target_pairs={{0,1},{1,2},{2,3},{3,4},{4,5},{5,6},{6,7},{7,0},{8,9},{9,10},{10,1... | collective-permute-start | bytes 61448 | tf_op jit(solution)/shard_map/ppermute | solution.py:288
  33.1 0.0 collective-permute-start.4
  33.1 0.0 slice-done
  33.1 0.0 slice-done.1
  33.1 0.0 slice-done.2
  33.1 2.4 %shard_map.90.local = f32[8,8,320]{2,1,0:T(8,128)S(1)} custom-call(bf16[256,1280]{1,0:T(8,128)(2,1)S(1)} %get-tuple-element.33.spread, bf16[64,384]{1,0:T(8,128)(2,1)S(1)} %get-tuple-element.34.faces, bf16[7,1280,640]{2,1,0:T(8,128)(2,1)S(1)} %bitcast.18), custom_call_target="tpu_custom_call" | custom-call | flops 2936012800 | bytes 11468800 | tf_op jit(solution)/shard_map/pallas_call | solution.py:290
  35.5 0.0 collective-permute-done.3.below
  35.5 0.8 %collective-permute-done.4.above = f32[2,8,320]{2,1,0:T(8,128)S(1)} collective-permute-done((f32[2,8,320]{2,1,0:T(8,128)S(1)}, f32[2,8,320]{2,1,0:T(8,128)S(1)}, u32[]{:S(2)}, u32[]{:S(2)}) %collective-permute-start.4) | collective-permute-done | bytes 20512 | tf_op jit(solution)/shard_map/ppermute | solution.py:289
  36.3 0.1 shard_map.91
  36.4 10.1 %all_to_all.21.refs_2_ = f32[8,8,320]{2,1,0:T(8,128)S(1)} all-to-all(f32[8,8,320]{2,1,0:T(8,128)S(1)} %get-tuple-element.38), channel_id=1, replica_groups={{0,8,16,24,32,40,48,56},{64,72,80,88,96,104,112,120},{128,136,144,152,1..., dimensions={0} | all-to-all | bytes 163840 | tf_op jit(solution)/shard_map/all_to_all | solution.py:244
  46.5 0.1 collective-permute-start.7
  46.6 3.5 %collective-permute-start.6 = (f32[8,320]{1,0:T(8,128)S(1)}, f32[8,320]{1,0:T(8,128)S(1)}, u32[]{:S(2)}, u32[]{:S(2)}) collective-permute-start(f32[8,320]{1,0:T(8,128)S(1)} %get-tuple-element.40.refs_8_), channel_id=1, source_target_pairs={{128,0},{136,8},{144,16},{152,24},{160,32},{168,40},{176,48},{184,... | collective-permute-start | bytes 30728 | tf_op jit(solution)/shard_map/ppermute | solution.py:270
  50.0 0.0 collective-permute-start.5
  50.0 0.3 collective-permute-done.7.refs_11_
  50.3 0.9 %collective-permute-done.6.refs_10_ = f32[8,320]{1,0:T(8,128)S(1)} collective-permute-done((f32[8,320]{1,0:T(8,128)S(1)}, f32[8,320]{1,0:T(8,128)S(1)}, u32[]{:S(2)}, u32[]{:S(2)}) %collective-permute-start.6) | collective-permute-done | bytes 10272 | tf_op jit(solution)/shard_map/ppermute | solution.py:270
  51.2 1.6 %collective-permute-done.5.refs_9_ = f32[8,320]{1,0:T(8,128)S(1)} collective-permute-done((f32[8,320]{1,0:T(8,128)S(1)}, f32[8,320]{1,0:T(8,128)S(1)}, u32[]{:S(2)}, u32[]{:S(2)}) %collective-permute-start.5) | collective-permute-done | bytes 10272 | tf_op jit(solution)/shard_map/ppermute | solution.py:270
  52.8 0.6 shard_map.93
  53.5 4.2 %collective-permute-start.8 = (f32[2,8,320]{2,1,0:T(8,128)S(1)}, f32[2,8,320]{2,1,0:T(8,128)S(1)}, u32[]{:S(2)}, u32[]{:S(2)}) collective-permute-start(f32[2,8,320]{2,1,0:T(8,128)S(1)} %get-tuple-element.42), channel_id=1, source_target_pairs={{0,1},{1,2},{2,3},{3,4},{4,5},{5,6},{6,7},{7,0},{8,9},{9,10},{10,1... | collective-permute-start | bytes 61448 | tf_op jit(solution)/shard_map/ppermute | solution.py:288
  57.7 0.0 collective-permute-start.9
  57.7 2.6 %shard_map.94.local = f32[8,8,320]{2,1,0:T(8,128)S(1)} custom-call(bf16[256,1280]{1,0:T(8,128)(2,1)S(1)} %get-tuple-element.41.spread, bf16[64,384]{1,0:T(8,128)(2,1)S(1)} %get-tuple-element.34.faces, bf16[7,1280,640]{2,1,0:T(8,128)(2,1)S(1)} %bitcast.19), custom_call_target="tpu_custom_call" | custom-call | flops 2936012800 | bytes 11468800 | tf_op jit(solution)/shard_map/pallas_call | solution.py:290
  60.3 0.0 collective-permute-done.8.below
  60.3 0.7 collective-permute-done.9.above
  61.1 0.3 shard_map.95
  61.4 19.2 %all_to_all.22 = f32[256,1,128]{2,1,0:T(1,128)S(1)} all-to-all(f32[256,1,128]{2,1,0:T(1,128)S(1)} %bitcast.21), channel_id=1, replica_groups=mesh['tm'=32,'space'=8] {'tm','space'}, dimensions={0} | all-to-all | bytes 262144 | tf_op jit(solution)/shard_map/all_to_all | solution.py:469
  80.6 1.0 %shard_map.96 = (f32[8,8,320]{2,1,0:T(8,128)}, f32[8,8,320]{2,1,0:T(8,128)}) custom-call(f32[256,128]{1,0:T(8,128)S(1)} %bitcast.20, f32[8,8,320]{2,1,0:T(8,128)S(1)} %get-tuple-element.27.refs_0_.source, f32[8,8,320]{2,1,0:T(8,128)S(1)} %get-tuple-element.45.first_chain, f32[8,8,320]{2,1,0:T(8,128)S(1)} %get-tuple-element.46.second_chain, ...), custom_call_target="tpu_custom_call" | custom-call | tf_op jit(solution)/shard_map/pallas_call | solution.py:470
  (3 shorter events, 0.1 us)
Async XLA Ops:
  0.6 10.8 %copy-start.5 = (bf16[2,2,102400]{2,1,0:T(2,128)(2,1)S(1)}, bf16[2,2,102400]{2,1,0:T(2,128)(2,1)}, u32[]{:S(2)}) copy-start(bf16[2,2,102400]{2,1,0:T(2,128)(2,1)} %param.11) | copy-start | bytes 2457604
  0.6 12.0 %copy-start = (f32[8,320,8]{1,2,0:T(8,128)S(1)}, f32[8,320,8]{1,2,0:T(8,128)}, u32[]{:S(2)}) copy-start(f32[8,320,8]{1,2,0:T(8,128)} %param.7) | copy-start | bytes 245764
  0.7 12.0 %copy-start.1 = (f32[8,320,8]{1,2,0:T(8,128)S(1)}, f32[8,320,8]{1,2,0:T(8,128)}, u32[]{:S(2)}) copy-start(f32[8,320,8]{1,2,0:T(8,128)} %param.8) | copy-start | bytes 245764
  0.7 12.0 %copy-start.2 = (s32[6,8]{1,0:T(8,128)S(1)}, s32[6,8]{1,0:T(8,128)}, u32[]{:S(2)}) copy-start(s32[6,8]{1,0:T(8,128)} %neighbours.1) | copy-start | bytes 580
  0.7 12.0 %copy-start.3 = (s32[2,2]{1,0:T(2,128)S(1)}, s32[2,2]{1,0:T(2,128)}, u32[]{:S(2)}) copy-start(s32[2,2]{1,0:T(2,128)} %owner.1) | copy-start | bytes 52
  0.7 12.0 %copy-start.4 = (s32[1,2]{1,0:T(1,128)S(1)}, s32[1,2]{1,0:T(1,128)}, u32[]{:S(2)}) copy-start(s32[1,2]{1,0:T(1,128)} %pairing.1) | copy-start | bytes 28
  2.4 17.8 %all-to-all-start = ((f32[8,16,320]{2,1,0:T(8,128)}), f32[8,16,320]{2,1,0:T(8,128)S(1)}, u32[]{:S(2)}, u32[]{:S(2)}) async-start(f32[8,16,320]{2,1,0:T(8,128)} %shard_map.87), calls=%async_computation | async-start | bytes 393216 | tf_op jit(solution)/shard_map/all_to_all | solution.py:244
  20.3 12.8 %slice-start = ((s8[11468800]{0:T(1024)(128)(4,1)}), s8[4194304]{0:T(1024)(128)(4,1)S(1)}, s32[]{:S(2)}) async-start(s8[11468800]{0:T(1024)(128)(4,1)} %bitcast.16), calls=%async_computation.3 | async-start | bytes 8388608
  20.3 12.8 %slice-start.1 = ((s8[11468800]{0:T(1024)(128)(4,1)}), s8[4194304]{0:T(1024)(128)(4,1)S(1)}, s32[]{:S(2)}) async-start(s8[11468800]{0:T(1024)(128)(4,1)} %bitcast.16), calls=%async_computation.4 | async-start | bytes 8388608
  20.3 5.1 %collective-permute-start.2 = (f32[16,320]{1,0:T(8,128)S(1)}, f32[16,320]{1,0:T(8,128)S(1)}, u32[]{:S(2)}, u32[]{:S(2)}) collective-permute-start(f32[16,320]{1,0:T(8,128)S(1)} %get-tuple-element.30.refs_3_), channel_id=1, source_target_pairs={{192,0},{200,8},{208,16},{216,24},{224,32},{232,40},{240,48},{248,... | collective-permute-start | bytes 61448 | tf_op jit(solution)/shard_map/ppermute | solution.py:270
  21.7 4.2 %collective-permute-start.1 = (f32[16,320]{1,0:T(8,128)S(1)}, f32[16,320]{1,0:T(8,128)S(1)}, u32[]{:S(2)}, u32[]{:S(2)}) collective-permute-start(f32[16,320]{1,0:T(8,128)S(1)} %get-tuple-element.30.refs_3_), channel_id=1, source_target_pairs={{128,0},{136,8},{144,16},{152,24},{160,32},{168,40},{176,48},{184,... | collective-permute-start | bytes 61448 | tf_op jit(solution)/shard_map/ppermute | solution.py:270
  24.3 3.0 %collective-permute-start = (f32[16,320]{1,0:T(8,128)S(1)}, f32[16,320]{1,0:T(8,128)S(1)}, u32[]{:S(2)}, u32[]{:S(2)}) collective-permute-start(f32[16,320]{1,0:T(8,128)S(1)} %get-tuple-element.30.refs_3_), channel_id=1, source_target_pairs={{64,0},{72,8},{80,16},{88,24},{96,32},{104,40},{112,48},{120,56},{... | collective-permute-start | bytes 61448 | tf_op jit(solution)/shard_map/ppermute | solution.py:270
  27.3 5.8 %slice-start.2 = ((s8[11468800]{0:T(1024)(128)(4,1)}), s8[3080192]{0:T(1024)(128)(4,1)S(1)}, s32[]{:S(2)}) async-start(s8[11468800]{0:T(1024)(128)(4,1)} %bitcast.16), calls=%async_computation.5 | async-start | bytes 6160384
  27.9 7.6 %collective-permute-start.3 = (f32[2,8,320]{2,1,0:T(8,128)S(1)}, f32[2,8,320]{2,1,0:T(8,128)S(1)}, u32[]{:S(2)}, u32[]{:S(2)}) collective-permute-start(f32[2,8,320]{2,1,0:T(8,128)S(1)} %get-tuple-element.35), channel_id=1, source_target_pairs={{0,1},{1,2},{2,3},{3,4},{4,5},{5,6},{6,7},{7,0},{8,9},{9,10},{10,1... | collective-permute-start | bytes 61448 | tf_op jit(solution)/shard_map/ppermute | solution.py:288
  33.1 3.3 %collective-permute-start.4 = (f32[2,8,320]{2,1,0:T(8,128)S(1)}, f32[2,8,320]{2,1,0:T(8,128)S(1)}, u32[]{:S(2)}, u32[]{:S(2)}) collective-permute-start(f32[2,8,320]{2,1,0:T(8,128)S(1)} %get-tuple-element.36), channel_id=1, source_target_pairs={{1,0},{2,1},{3,2},{4,3},{5,4},{6,5},{7,6},{0,7},{9,8},{10,9},{11,1... | collective-permute-start | bytes 61448 | tf_op jit(solution)/shard_map/ppermute | solution.py:289
  46.5 3.8 %collective-permute-start.7 = (f32[8,320]{1,0:T(8,128)S(1)}, f32[8,320]{1,0:T(8,128)S(1)}, u32[]{:S(2)}, u32[]{:S(2)}) collective-permute-start(f32[8,320]{1,0:T(8,128)S(1)} %get-tuple-element.40.refs_8_), channel_id=1, source_target_pairs={{192,0},{200,8},{208,16},{216,24},{224,32},{232,40},{240,48},{248,... | collective-permute-start | bytes 30728 | tf_op jit(solution)/shard_map/ppermute | solution.py:270
  46.6 4.7 %collective-permute-start.6 = (f32[8,320]{1,0:T(8,128)S(1)}, f32[8,320]{1,0:T(8,128)S(1)}, u32[]{:S(2)}, u32[]{:S(2)}) collective-permute-start(f32[8,320]{1,0:T(8,128)S(1)} %get-tuple-element.40.refs_8_), channel_id=1, source_target_pairs={{128,0},{136,8},{144,16},{152,24},{160,32},{168,40},{176,48},{184,... | collective-permute-start | bytes 30728 | tf_op jit(solution)/shard_map/ppermute | solution.py:270
  50.0 2.8 %collective-permute-start.5 = (f32[8,320]{1,0:T(8,128)S(1)}, f32[8,320]{1,0:T(8,128)S(1)}, u32[]{:S(2)}, u32[]{:S(2)}) collective-permute-start(f32[8,320]{1,0:T(8,128)S(1)} %get-tuple-element.40.refs_8_), channel_id=1, source_target_pairs={{64,0},{72,8},{80,16},{88,24},{96,32},{104,40},{112,48},{120,56},{... | collective-permute-start | bytes 30728 | tf_op jit(solution)/shard_map/ppermute | solution.py:270
  53.5 6.8 %collective-permute-start.8 = (f32[2,8,320]{2,1,0:T(8,128)S(1)}, f32[2,8,320]{2,1,0:T(8,128)S(1)}, u32[]{:S(2)}, u32[]{:S(2)}) collective-permute-start(f32[2,8,320]{2,1,0:T(8,128)S(1)} %get-tuple-element.42), channel_id=1, source_target_pairs={{0,1},{1,2},{2,3},{3,4},{4,5},{5,6},{6,7},{7,0},{8,9},{9,10},{10,1... | collective-permute-start | bytes 61448 | tf_op jit(solution)/shard_map/ppermute | solution.py:288
  57.7 3.4 %collective-permute-start.9 = (f32[2,8,320]{2,1,0:T(8,128)S(1)}, f32[2,8,320]{2,1,0:T(8,128)S(1)}, u32[]{:S(2)}, u32[]{:S(2)}) collective-permute-start(f32[2,8,320]{2,1,0:T(8,128)S(1)} %get-tuple-element.43), channel_id=1, source_target_pairs={{1,0},{2,1},{3,2},{4,3},{5,4},{6,5},{7,6},{0,7},{9,8},{10,9},{11,1... | collective-permute-start | bytes 61448 | tf_op jit(solution)/shard_map/ppermute | solution.py:289

commit v5 on v4

--- a/solution.py
+++ b/solution.py
@@ -80,26 +80,32 @@
 ):
     source_out[...] = source[...]
     decay_out[...] = decay[...]
-    couple_out[...] = couple[...]
     at = iota((ELEMENTS, WIDTH), 0)
 
     def chosen(condition):
         return jnp.where(condition, 1.0, 0.0)
 
+    odd = lax.rem(mine[1], 2)
     for i in range(2):
         below = jnp.zeros((ELEMENTS, WIDTH), F32)
         for k in range(2):
             below = below + jnp.where(
                 (at == owner[1, k]) & (pairing[0, k] == i), 1.0, 0.0
             )
-        halo[i] = below
-        halo[2 + i] = chosen(at == owner[0, i])
-    halo[4] = chosen(at * 0 == pairing[0, 0])
-    halo[5] = (at * 0 + mine[0] % RING).astype(F32)
+        above = chosen(at == owner[0, i])
+        halo[i] = jnp.where(at * 0 == odd, above, below)
+        halo[2 + i] = jnp.where(at * 0 == odd, below, above)
+        couple_out[i] = couple[jnp.bitwise_xor(i, odd)]
+    straight = at * 0 == pairing[0, 0]
+    halo[4] = chosen(straight | (at * 0 == odd))
+    halo[5] = chosen(straight | (at * 0 + 1 == odd))
+    halo[6] = (at * 0 + lax.rem(mine[0], RING)).astype(F32)
+    halo[7] = (at * 0 + lax.rem(mine[0] // RING, 2)).astype(F32)
 
     row = iota((4 * 2 * SLABS, 2 * ROWS), 0)
     col = iota((4 * 2 * SLABS, 2 * ROWS), 1)
     slot = row // (2 * SLABS)
+    slot = jnp.bitwise_xor(slot, 2 * odd)
     element = jnp.where(
         slot < 2,
         jnp.where(slot == 0, owner[0, 0], owner[0, 1]),
@@ -125,7 +131,7 @@
     else:
         halo, maps, offsets, out, later = refs
         offset_of = lambda j: offsets[j]
-    mine = halo[5]
+    mine = halo[6]
     product = jnp.ones((ELEMENTS, WIDTH), F32)
     offset = jnp.zeros((ELEMENTS, WIDTH), F32)
     for j in reversed(range(RING)):
@@ -157,13 +163,20 @@
     else:
         later_offset, *offsets = [ref[...] for ref in refs[: 1 + LINES]]
         refs = refs[1 + LINES :]
-    pick, halo, couple, chained, spread, up, down = refs
-
-    product = lines[0][0:ELEMENTS]
+    pick, halo, couple, chained, spread, mate, other = refs
+
+    turned = halo[7] > 0.5
+    products = [line[0:ELEMENTS] for line in lines]
+    for part in (products, offsets):
+        part[1], part[3] = (
+            jnp.where(turned, part[3], part[1]),
+            jnp.where(turned, part[1], part[3]),
+        )
+    product = products[0]
     offset = offsets[0]
     for j in reversed(range(1, LINES)):
-        offset = offsets[j] + lines[j][0:ELEMENTS] * offset
-        product = product * lines[j][0:ELEMENTS]
+        offset = offsets[j] + products[j] * offset
+        product = product * products[j]
     value = later_offset + later[0:ELEMENTS] * (offset / (1.0 - product))
     for t in reversed(range(SLABS)):
         value = field[t] + decay[t] * value
@@ -182,11 +195,10 @@
             preferred_element_type=F32,
         )
         products.append(both[:SLABS] + both[SLABS:])
-    up[0] = products[0]
-    up[1] = products[1]
-    straight = halo[4] > 0.5
-    down[0] = jnp.where(straight, products[2], products[3])
-    down[1] = jnp.where(straight, products[3], products[2])
+    for k, out in enumerate((mate, other)):
+        straight = halo[4 + k] > 0.5
+        out[0] = jnp.where(straight, products[2 * k], products[2 * k + 1])
+        out[1] = jnp.where(straight, products[2 * k + 1], products[2 * k])
 
     own = iota((2 * ROWS, DEPTH), 0) % ELEMENTS == iota((2 * ROWS, DEPTH), 1) % ELEMENTS
     n = iota((256, SPAN), 0)
@@ -267,12 +279,12 @@
     )(halo, *own)
     count = RING * LINES
     lines = [line] + [
-        lax.ppermute(line, "tm", [((i + k * RING) % count, i) for i in range(count)])
+        lax.ppermute(line, "tm", [(i ^ (k * RING), i) for i in range(count)])
         for k in range(1, LINES)
     ]
     if first:
         known = (gathered, later, *lines)
-    chained, spread, up, down = pl.pallas_call(
+    chained, spread, mate, other = pl.pallas_call(
         chain,
         out_shape=(
             struct(SLABS, ELEMENTS, WIDTH),
@@ -285,8 +297,10 @@
         compiler_params=params(OPERATE_MIB),
         cost_estimate=HINT,
     )(field, decay, *known[1:], *(() if first else (later, *lines)), pick, halo, couple)
-    below = lax.ppermute(up, "space", [(i, (i + 1) % 8) for i in range(8)])
-    above = lax.ppermute(down, "space", [((i + 1) % 8, i) for i in range(8)])
+    pairs = [(i, i ^ 1) for i in range(8)]
+    across = [(i, (i + 1 if i % 2 else i - 1) % 8) for i in range(8)]
+    mate = lax.ppermute(mate, "space", pairs)
+    other = lax.ppermute(other, "space", across)
     local = pl.pallas_call(
         local_kernel,
         out_shape=struct(SLABS, ELEMENTS, WIDTH),
@@ -299,20 +313,20 @@
             transcendentals=0,
         ),
     )(spread, faces, weights)
-    return chained, local, below, above, known
-
-
-def add_halo(halo, local, below, above, out):
+    return chained, local, mate, other, known
+
+
+def add_halo(halo, local, mate, other, out):
     for t in range(SLABS):
         value = local[t]
         for k in range(2):
-            value = value + halo[k] * below[k, t : t + 1]
-            value = value + halo[2 + k] * above[k, t : t + 1]
+            value = value + halo[k] * mate[k, t : t + 1]
+            value = value + halo[2 + k] * other[k, t : t + 1]
         out[t] = value
 
 
-def middle_kernel(halo, local, below, above, decay, image, out):
-    add_halo(halo, local, below, above, image)
+def middle_kernel(halo, local, mate, other, decay, image, out):
+    add_halo(halo, local, mate, other, image)
     offset = jnp.zeros((ELEMENTS, WIDTH), F32)
     for t in reversed(range(SLABS)):
         offset = image[t] + decay[t] * offset
@@ -324,8 +338,8 @@
     return jnp.sum(jnp.sum(x, axis=0), keepdims=True)
 
 
-def gram_kernel(halo, local, below, above, source, image0, image1, out):
-    add_halo(halo, local, below, above, image1)
+def gram_kernel(halo, local, mate, other, source, image0, image1, out):
+    add_halo(halo, local, mate, other, image1)
     s = source[...]
     largest = [
         jnp.maximum(jnp.max(jnp.max(jnp.abs(image[...]), axis=0), keepdims=True), TINY)
@@ -419,7 +433,7 @@
     weights = jnp.transpose(blocks, (1, 0, 2)).reshape(FACES, ELEMENTS, PAIRS, LANES)
     weights = jnp.transpose(weights, (0, 2, 1, 3)).reshape(FACES, DEPTH, LANES)
     couple = interface_jacobian_blocks.reshape(2, 2, WIDTH, WIDTH)
-    mine = lax.axis_index("tm").astype(jnp.int32).reshape(1)
+    mine = jnp.stack([lax.axis_index("tm"), lax.axis_index("space")]).astype(jnp.int32)
     field_shape = struct(SLABS, ELEMENTS, WIDTH)
     maps = pl.pallas_call(
         maps_kernel,
@@ -436,7 +450,7 @@
         out_shape=(
             jax.ShapeDtypeStruct((ROWS, (FACES - 1) * ROWS), BF16),
             jax.ShapeDtypeStruct((4 * 2 * SLABS, 2 * ROWS), BF16),
-            struct(6, ELEMENTS, WIDTH),
+            struct(8, ELEMENTS, WIDTH),
             field_shape,
             field_shape,
             jax.ShapeDtypeStruct((2, 2, WIDTH, WIDTH), BF16),
@@ -446,7 +460,7 @@
         compiler_params=params(SMALL_MIB),
     )(mine, neighbours, face_element_owner, pairing, source, decay, couple)
     halo = tables[2]
-    chain0, local, below, above, known = operate(
+    chain0, local, mate, other, known = operate(
         True, source, decay, maps, None, tables, weights, couple
     )
     image0, offsets = pl.pallas_call(
@@ -455,8 +469,8 @@
         in_specs=[VMEM] * 5,
         out_specs=(VMEM,) * 2,
         compiler_params=params(SMALL_MIB),
-    )(halo, local, below, above, decay)
-    chain1, local, below, above, known = operate(
+    )(halo, local, mate, other, decay)
+    chain1, local, mate, other, known = operate(
         False, image0, decay, offsets, known, tables, weights, couple
     )
     image1, gram = pl.pallas_call(
@@ -465,7 +479,7 @@
         in_specs=[VMEM] * 6,
         out_specs=(VMEM,) * 2,
         compiler_params=params(SMALL_MIB),
-    )(halo, local, below, above, source, image0)
+    )(halo, local, mate, other, source, image0)
     gram = lax.all_to_all(gram, ("tm", "space"), 0, 0, tiled=True)
     adjoint, residual = pl.pallas_call(
         last_kernel,

time: 81.9 us -> 80.4 us (0.982)
  starting transfers between devices: 26.9 us -> 25.8 us
    ppermute x10, starting transfers between devices: 17.9 us -> 16.8 us  [the longest x2 8.46 us: operate(): mate = lax.ppermute(mate, 'space', pairs)]
  transfers between devices with their start and end apart: 11 -> 11, of which waited for: 8 -> 6; matrix products, arithmetic and copies ran while one was open for 1% -> 2% of each run, Pallas kernels for 7% -> 7%
where the time goes in v5:
time: 80.4 us; the launch traced here: 80.1 us
  blocking collectives  29.2 us (36%)
  starting transfers between devices  25.8 us (32%)
  waiting for transfers between devices  12.5 us (16%)
  Pallas kernels  10.5 us (13%)
  local copies, waits for them, and re-layouts  1.19 us (1%)
    all_to_all x1, blocking collectives, shards(): gram = lax.all_to_all(gram, ('tm', 'space'), 0, 0, tiled=True)  19.3 us
    all_to_all x1, blocking collectives, along(): return lax.all_to_all(x, 'tm', 0, 0, axis_index_groups=groups, tiled=True)  9.95 us
    all_to_all x1, starting transfers between devices, along(): return lax.all_to_all(x, 'tm', 0, 0, axis_index_groups=groups, tiled=True)  9.03 us
    ppermute x2, starting transfers between devices, operate(): mate = lax.ppermute(mate, 'space', pairs)  8.46 us
    ppermute x6, starting transfers between devices, operate(): lax.ppermute(line, 'tm', [(i ^ k * RING, i) for i in range(count)])  6.84 us
    all_to_all x1, waiting for transfers between devices, along(): return lax.all_to_all(x, 'tm', 0, 0, axis_index_groups=groups, tiled=True)  6.75 us
    ppermute x6, waiting for transfers between devices, operate(): lax.ppermute(line, 'tm', [(i ^ k * RING, i) for i in range(count)])  5.34 us
    pallas_call x2, Pallas kernels, operate(): pl.pallas_call(local_kernel, out_shape=struct(SLABS, ELEMENTS, WIDTH), in...  5.15 us
  transfers between devices with their start and end apart: 11, of which 6 were waited for; matrix products, arithmetic and copies ran while one was open for 2% of the time, Pallas kernels for 7%

profile of v5, /device:TPU:1, one launch (start us, length us, event | category | flops | bytes accessed | tf_op | source)
XLA Modules:
  0.0 80.1 jit_solution(251536007339196938)
XLA Ops:
  0.6 0.0 copy-start.5
  0.6 0.0 copy-start
  0.7 0.0 copy-start.1
  0.7 0.0 copy-start.2
  0.7 0.0 copy-start.3
  0.7 0.0 copy-start.4
  0.7 1.7 %shard_map.87 = f32[8,16,320]{2,1,0:T(8,128)} custom-call(f32[8,8,320]{2,1,0:T(8,128)} %bitcast.23, f32[8,8,320]{2,1,0:T(8,128)} %bitcast.25), custom_call_target="tpu_custom_call" | custom-call | flops 10000000000 | bytes 1000000 | tf_op jit(solution)/shard_map/pallas_call | solution.py:438
  2.4 9.0 %all-to-all-start = ((f32[8,16,320]{2,1,0:T(8,128)}), f32[8,16,320]{2,1,0:T(8,128)S(1)}, u32[]{:S(2)}, u32[]{:S(2)}) async-start(f32[8,16,320]{2,1,0:T(8,128)} %shard_map.87), calls=%async_computation | async-start | bytes 393216 | tf_op jit(solution)/shard_map/all_to_all | solution.py:256
  11.5 0.0 copy-done.5
  11.5 1.1 %reshape.15.couple = bf16[2,2,320,320]{3,2,1,0:T(8,128)(2,1)S(1)} reshape(bf16[2,2,102400]{2,1,0:T(2,128)(2,1)S(1)} %copy-done.5) | data formatting | bytes 1638400 | tf_op jit(solution)/shard_map/reshape | solution.py:435
  12.6 0.1 pad_add_fusion.mine
  12.7 0.0 copy-done
  12.7 0.0 copy-done.1
  12.7 0.0 copy-done.2
  12.7 0.0 copy-done.3
  12.7 0.0 copy-done.4
  12.7 0.8 shard_map.86
  13.5 6.8 %all-to-all-done.refs_1_ = f32[8,16,320]{2,1,0:T(8,128)S(1)} async-done(((f32[8,16,320]{2,1,0:T(8,128)}), f32[8,16,320]{2,1,0:T(8,128)S(1)}, u32[]{:S(2)}, u32[]{:S(2)}) %all-to-all-start) | async-done | bytes 163872 | tf_op jit(solution)/shard_map/all_to_all | solution.py:256
  20.3 0.0 slice-start
  20.3 0.0 slice-start.1
  20.3 2.8 %collective-permute-start.2 = (f32[16,320]{1,0:T(8,128)S(1)}, f32[16,320]{1,0:T(8,128)S(1)}, u32[]{:S(2)}, u32[]{:S(2)}) collective-permute-start(f32[16,320]{1,0:T(8,128)S(1)} %get-tuple-element.30.refs_3_), channel_id=1, source_target_pairs={{192,0},{200,8},{208,16},{216,24},{224,32},{232,40},{240,48},{248,... | collective-permute-start | bytes 61448 | tf_op jit(solution)/shard_map/ppermute | solution.py:282
  23.1 0.3 collective-permute-start.1
  23.5 0.3 collective-permute-start
  23.8 0.5 collective-permute-done.2.refs_6_
  24.3 3.0 %collective-permute-done.1.refs_5_ = f32[16,320]{1,0:T(8,128)S(1)} collective-permute-done((f32[16,320]{1,0:T(8,128)S(1)}, f32[16,320]{1,0:T(8,128)S(1)}, u32[]{:S(2)}, u32[]{:S(2)}) %collective-permute-start.1) | collective-permute-done | bytes 20512 | tf_op jit(solution)/shard_map/ppermute | solution.py:282
  27.3 0.0 collective-permute-done.refs_4_
  27.3 0.0 slice-start.2
  27.3 0.7 shard_map.89
  28.0 4.1 %collective-permute-start.3 = (f32[2,8,320]{2,1,0:T(8,128)S(1)}, f32[2,8,320]{2,1,0:T(8,128)S(1)}, u32[]{:S(2)}, u32[]{:S(2)}) collective-permute-start(f32[2,8,320]{2,1,0:T(8,128)S(1)} %get-tuple-element.35), channel_id=1, source_target_pairs={{0,1},{1,0},{2,3},{3,2},{4,5},{5,4},{6,7},{7,6},{8,9},{9,8},{10,11... | collective-permute-start | bytes 61448 | tf_op jit(solution)/shard_map/ppermute | solution.py:302
  32.1 1.2 %collective-permute-start.4 = (f32[2,8,320]{2,1,0:T(8,128)S(1)}, f32[2,8,320]{2,1,0:T(8,128)S(1)}, u32[]{:S(2)}, u32[]{:S(2)}) collective-permute-start(f32[2,8,320]{2,1,0:T(8,128)S(1)} %get-tuple-element.36), channel_id=1, source_target_pairs={{0,7},{1,2},{2,1},{3,4},{4,3},{5,6},{6,5},{7,0},{8,15},{9,10},{10,... | collective-permute-start | bytes 61448 | tf_op jit(solution)/shard_map/ppermute | solution.py:303
  33.3 0.0 slice-done
  33.3 0.0 slice-done.1
  33.3 0.0 slice-done.2
  33.3 2.6 %shard_map.90.local = f32[8,8,320]{2,1,0:T(8,128)S(1)} custom-call(bf16[256,1280]{1,0:T(8,128)(2,1)S(1)} %get-tuple-element.33.spread, bf16[64,384]{1,0:T(8,128)(2,1)S(1)} %get-tuple-element.34.faces, bf16[7,1280,640]{2,1,0:T(8,128)(2,1)S(1)} %bitcast.19), custom_call_target="tpu_custom_call" | custom-call | flops 2936012800 | bytes 11468800 | tf_op jit(solution)/shard_map/pallas_call | solution.py:304
  36.0 0.0 collective-permute-done.3.mate
  36.0 0.0 collective-permute-done.4.other
  36.0 0.1 shard_map.91
  36.1 10.0 %all_to_all.21.refs_2_ = f32[8,8,320]{2,1,0:T(8,128)S(1)} all-to-all(f32[8,8,320]{2,1,0:T(8,128)S(1)} %get-tuple-element.38), channel_id=1, replica_groups={{0,8,16,24,32,40,48,56},{64,72,80,88,96,104,112,120},{128,136,144,152,1..., dimensions={0} | all-to-all | bytes 163840 | tf_op jit(solution)/shard_map/all_to_all | solution.py:256
  46.0 1.1 %collective-permute-start.7 = (f32[8,320]{1,0:T(8,128)S(1)}, f32[8,320]{1,0:T(8,128)S(1)}, u32[]{:S(2)}, u32[]{:S(2)}) collective-permute-start(f32[8,320]{1,0:T(8,128)S(1)} %get-tuple-element.40.refs_8_), channel_id=1, source_target_pairs={{192,0},{200,8},{208,16},{216,24},{224,32},{232,40},{240,48},{248,... | collective-permute-start | bytes 30728 | tf_op jit(solution)/shard_map/ppermute | solution.py:282
  47.1 0.8 %collective-permute-start.6 = (f32[8,320]{1,0:T(8,128)S(1)}, f32[8,320]{1,0:T(8,128)S(1)}, u32[]{:S(2)}, u32[]{:S(2)}) collective-permute-start(f32[8,320]{1,0:T(8,128)S(1)} %get-tuple-element.40.refs_8_), channel_id=1, source_target_pairs={{128,0},{136,8},{144,16},{152,24},{160,32},{168,40},{176,48},{184,... | collective-permute-start | bytes 30728 | tf_op jit(solution)/shard_map/ppermute | solution.py:282
  48.0 1.4 %collective-permute-start.5 = (f32[8,320]{1,0:T(8,128)S(1)}, f32[8,320]{1,0:T(8,128)S(1)}, u32[]{:S(2)}, u32[]{:S(2)}) collective-permute-start(f32[8,320]{1,0:T(8,128)S(1)} %get-tuple-element.40.refs_8_), channel_id=1, source_target_pairs={{64,0},{72,8},{80,16},{88,24},{96,32},{104,40},{112,48},{120,56},{... | collective-permute-start | bytes 30728 | tf_op jit(solution)/shard_map/ppermute | solution.py:282
  49.4 0.5 collective-permute-done.7.refs_11_
  49.9 1.3 %collective-permute-done.6.refs_10_ = f32[8,320]{1,0:T(8,128)S(1)} collective-permute-done((f32[8,320]{1,0:T(8,128)S(1)}, f32[8,320]{1,0:T(8,128)S(1)}, u32[]{:S(2)}, u32[]{:S(2)}) %collective-permute-start.6) | collective-permute-done | bytes 10272 | tf_op jit(solution)/shard_map/ppermute | solution.py:282
  51.2 0.0 collective-permute-done.5.refs_9_
  51.2 0.7 shard_map.93
  51.9 4.4 %collective-permute-start.8 = (f32[2,8,320]{2,1,0:T(8,128)S(1)}, f32[2,8,320]{2,1,0:T(8,128)S(1)}, u32[]{:S(2)}, u32[]{:S(2)}) collective-permute-start(f32[2,8,320]{2,1,0:T(8,128)S(1)} %get-tuple-element.42), channel_id=1, source_target_pairs={{0,1},{1,0},{2,3},{3,2},{4,5},{5,4},{6,7},{7,6},{8,9},{9,8},{10,11... | collective-permute-start | bytes 61448 | tf_op jit(solution)/shard_map/ppermute | solution.py:302
  56.2 0.3 collective-permute-start.9
  56.5 2.5 %shard_map.94.local = f32[8,8,320]{2,1,0:T(8,128)S(1)} custom-call(bf16[256,1280]{1,0:T(8,128)(2,1)S(1)} %get-tuple-element.41.spread, bf16[64,384]{1,0:T(8,128)(2,1)S(1)} %get-tuple-element.34.faces, bf16[7,1280,640]{2,1,0:T(8,128)(2,1)S(1)} %bitcast.20), custom_call_target="tpu_custom_call" | custom-call | flops 2936012800 | bytes 11468800 | tf_op jit(solution)/shard_map/pallas_call | solution.py:304
  59.0 0.0 collective-permute-done.8.mate
  59.0 0.4 collective-permute-done.9.other
  59.5 0.3 shard_map.95
  59.8 19.3 %all_to_all.22 = f32[256,1,128]{2,1,0:T(1,128)S(1)} all-to-all(f32[256,1,128]{2,1,0:T(1,128)S(1)} %bitcast.22), channel_id=1, replica_groups=mesh['tm'=32,'space'=8] {'tm','space'}, dimensions={0} | all-to-all | bytes 262144 | tf_op jit(solution)/shard_map/all_to_all | solution.py:483
  79.1 1.0 %shard_map.96 = (f32[8,8,320]{2,1,0:T(8,128)}, f32[8,8,320]{2,1,0:T(8,128)}) custom-call(f32[256,128]{1,0:T(8,128)S(1)} %bitcast.21, f32[8,8,320]{2,1,0:T(8,128)S(1)} %get-tuple-element.27.refs_0_.source, f32[8,8,320]{2,1,0:T(8,128)S(1)} %get-tuple-element.45.first_chain, f32[8,8,320]{2,1,0:T(8,128)S(1)} %get-tuple-element.46.second_chain, ...), custom_call_target="tpu_custom_call" | custom-call | tf_op jit(solution)/shard_map/pallas_call | solution.py:484
  (3 shorter events, 0.0 us)
Async XLA Ops:
  0.6 10.8 %copy-start.5 = (bf16[2,2,102400]{2,1,0:T(2,128)(2,1)S(1)}, bf16[2,2,102400]{2,1,0:T(2,128)(2,1)}, u32[]{:S(2)}) copy-start(bf16[2,2,102400]{2,1,0:T(2,128)(2,1)} %param.11) | copy-start | bytes 2457604
  0.6 12.1 %copy-start = (f32[8,320,8]{1,2,0:T(8,128)S(1)}, f32[8,320,8]{1,2,0:T(8,128)}, u32[]{:S(2)}) copy-start(f32[8,320,8]{1,2,0:T(8,128)} %param.7) | copy-start | bytes 245764
  0.7 12.1 %copy-start.1 = (f32[8,320,8]{1,2,0:T(8,128)S(1)}, f32[8,320,8]{1,2,0:T(8,128)}, u32[]{:S(2)}) copy-start(f32[8,320,8]{1,2,0:T(8,128)} %param.8) | copy-start | bytes 245764
  0.7 12.0 %copy-start.2 = (s32[6,8]{1,0:T(8,128)S(1)}, s32[6,8]{1,0:T(8,128)}, u32[]{:S(2)}) copy-start(s32[6,8]{1,0:T(8,128)} %neighbours.1) | copy-start | bytes 580
  0.7 12.0 %copy-start.3 = (s32[2,2]{1,0:T(2,128)S(1)}, s32[2,2]{1,0:T(2,128)}, u32[]{:S(2)}) copy-start(s32[2,2]{1,0:T(2,128)} %owner.1) | copy-start | bytes 52
  0.7 12.0 %copy-start.4 = (s32[1,2]{1,0:T(1,128)S(1)}, s32[1,2]{1,0:T(1,128)}, u32[]{:S(2)}) copy-start(s32[1,2]{1,0:T(1,128)} %pairing.1) | copy-start | bytes 28
  2.4 17.8 %all-to-all-start = ((f32[8,16,320]{2,1,0:T(8,128)}), f32[8,16,320]{2,1,0:T(8,128)S(1)}, u32[]{:S(2)}, u32[]{:S(2)}) async-start(f32[8,16,320]{2,1,0:T(8,128)} %shard_map.87), calls=%async_computation | async-start | bytes 393216 | tf_op jit(solution)/shard_map/all_to_all | solution.py:256
  20.3 13.0 %slice-start = ((s8[11468800]{0:T(1024)(128)(4,1)}), s8[4194304]{0:T(1024)(128)(4,1)S(1)}, s32[]{:S(2)}) async-start(s8[11468800]{0:T(1024)(128)(4,1)} %bitcast.17), calls=%async_computation.3 | async-start | bytes 8388608
  20.3 13.0 %slice-start.1 = ((s8[11468800]{0:T(1024)(128)(4,1)}), s8[4194304]{0:T(1024)(128)(4,1)S(1)}, s32[]{:S(2)}) async-start(s8[11468800]{0:T(1024)(128)(4,1)} %bitcast.17), calls=%async_computation.4 | async-start | bytes 8388608
  20.3 4.0 %collective-permute-start.2 = (f32[16,320]{1,0:T(8,128)S(1)}, f32[16,320]{1,0:T(8,128)S(1)}, u32[]{:S(2)}, u32[]{:S(2)}) collective-permute-start(f32[16,320]{1,0:T(8,128)S(1)} %get-tuple-element.30.refs_3_), channel_id=1, source_target_pairs={{192,0},{200,8},{208,16},{216,24},{224,32},{232,40},{240,48},{248,... | collective-permute-start | bytes 61448 | tf_op jit(solution)/shard_map/ppermute | solution.py:282
  23.1 4.2 %collective-permute-start.1 = (f32[16,320]{1,0:T(8,128)S(1)}, f32[16,320]{1,0:T(8,128)S(1)}, u32[]{:S(2)}, u32[]{:S(2)}) collective-permute-start(f32[16,320]{1,0:T(8,128)S(1)} %get-tuple-element.30.refs_3_), channel_id=1, source_target_pairs={{128,0},{136,8},{144,16},{152,24},{160,32},{168,40},{176,48},{184,... | collective-permute-start | bytes 61448 | tf_op jit(solution)/shard_map/ppermute | solution.py:282
  23.5 3.9 %collective-permute-start = (f32[16,320]{1,0:T(8,128)S(1)}, f32[16,320]{1,0:T(8,128)S(1)}, u32[]{:S(2)}, u32[]{:S(2)}) collective-permute-start(f32[16,320]{1,0:T(8,128)S(1)} %get-tuple-element.30.refs_3_), channel_id=1, source_target_pairs={{64,0},{72,8},{80,16},{88,24},{96,32},{104,40},{112,48},{120,56},{... | collective-permute-start | bytes 61448 | tf_op jit(solution)/shard_map/ppermute | solution.py:282
  27.3 6.0 %slice-start.2 = ((s8[11468800]{0:T(1024)(128)(4,1)}), s8[3080192]{0:T(1024)(128)(4,1)S(1)}, s32[]{:S(2)}) async-start(s8[11468800]{0:T(1024)(128)(4,1)} %bitcast.17), calls=%async_computation.5 | async-start | bytes 6160384
  28.0 8.0 %collective-permute-start.3 = (f32[2,8,320]{2,1,0:T(8,128)S(1)}, f32[2,8,320]{2,1,0:T(8,128)S(1)}, u32[]{:S(2)}, u32[]{:S(2)}) collective-permute-start(f32[2,8,320]{2,1,0:T(8,128)S(1)} %get-tuple-element.35), channel_id=1, source_target_pairs={{0,1},{1,0},{2,3},{3,2},{4,5},{5,4},{6,7},{7,6},{8,9},{9,8},{10,11... | collective-permute-start | bytes 61448 | tf_op jit(solution)/shard_map/ppermute | solution.py:302
  32.1 3.9 %collective-permute-start.4 = (f32[2,8,320]{2,1,0:T(8,128)S(1)}, f32[2,8,320]{2,1,0:T(8,128)S(1)}, u32[]{:S(2)}, u32[]{:S(2)}) collective-permute-start(f32[2,8,320]{2,1,0:T(8,128)S(1)} %get-tuple-element.36), channel_id=1, source_target_pairs={{0,7},{1,2},{2,1},{3,4},{4,3},{5,6},{6,5},{7,0},{8,15},{9,10},{10,... | collective-permute-start | bytes 61448 | tf_op jit(solution)/shard_map/ppermute | solution.py:303
  46.0 3.8 %collective-permute-start.7 = (f32[8,320]{1,0:T(8,128)S(1)}, f32[8,320]{1,0:T(8,128)S(1)}, u32[]{:S(2)}, u32[]{:S(2)}) collective-permute-start(f32[8,320]{1,0:T(8,128)S(1)} %get-tuple-element.40.refs_8_), channel_id=1, source_target_pairs={{192,0},{200,8},{208,16},{216,24},{224,32},{232,40},{240,48},{248,... | collective-permute-start | bytes 30728 | tf_op jit(solution)/shard_map/ppermute | solution.py:282
  47.1 4.0 %collective-permute-start.6 = (f32[8,320]{1,0:T(8,128)S(1)}, f32[8,320]{1,0:T(8,128)S(1)}, u32[]{:S(2)}, u32[]{:S(2)}) collective-permute-start(f32[8,320]{1,0:T(8,128)S(1)} %get-tuple-element.40.refs_8_), channel_id=1, source_target_pairs={{128,0},{136,8},{144,16},{152,24},{160,32},{168,40},{176,48},{184,... | collective-permute-start | bytes 30728 | tf_op jit(solution)/shard_map/ppermute | solution.py:282
  48.0 3.2 %collective-permute-start.5 = (f32[8,320]{1,0:T(8,128)S(1)}, f32[8,320]{1,0:T(8,128)S(1)}, u32[]{:S(2)}, u32[]{:S(2)}) collective-permute-start(f32[8,320]{1,0:T(8,128)S(1)} %get-tuple-element.40.refs_8_), channel_id=1, source_target_pairs={{64,0},{72,8},{80,16},{88,24},{96,32},{104,40},{112,48},{120,56},{... | collective-permute-start | bytes 30728 | tf_op jit(solution)/shard_map/ppermute | solution.py:282
  51.9 7.2 %collective-permute-start.8 = (f32[2,8,320]{2,1,0:T(8,128)S(1)}, f32[2,8,320]{2,1,0:T(8,128)S(1)}, u32[]{:S(2)}, u32[]{:S(2)}) collective-permute-start(f32[2,8,320]{2,1,0:T(8,128)S(1)} %get-tuple-element.42), channel_id=1, source_target_pairs={{0,1},{1,0},{2,3},{3,2},{4,5},{5,4},{6,7},{7,6},{8,9},{9,8},{10,11... | collective-permute-start | bytes 61448 | tf_op jit(solution)/shard_map/ppermute | solution.py:302
  56.2 3.3 %collective-permute-start.9 = (f32[2,8,320]{2,1,0:T(8,128)S(1)}, f32[2,8,320]{2,1,0:T(8,128)S(1)}, u32[]{:S(2)}, u32[]{:S(2)}) collective-permute-start(f32[2,8,320]{2,1,0:T(8,128)S(1)} %get-tuple-element.43), channel_id=1, source_target_pairs={{0,7},{1,2},{2,1},{3,4},{4,3},{5,6},{6,5},{7,0},{8,15},{9,10},{10,... | collective-permute-start | bytes 61448 | tf_op jit(solution)/shard_map/ppermute | solution.py:303

commit v6 on v5

--- a/solution.py
+++ b/solution.py
@@ -299,8 +299,8 @@
     )(field, decay, *known[1:], *(() if first else (later, *lines)), pick, halo, couple)
     pairs = [(i, i ^ 1) for i in range(8)]
     across = [(i, (i + 1 if i % 2 else i - 1) % 8) for i in range(8)]
+    other = lax.ppermute(other, "space", across)
     mate = lax.ppermute(mate, "space", pairs)
-    other = lax.ppermute(other, "space", across)
     local = pl.pallas_call(
         local_kernel,
         out_shape=struct(SLABS, ELEMENTS, WIDTH),
@@ -325,7 +325,7 @@
         out[t] = value
 
 
-def middle_kernel(halo, local, mate, other, decay, image, out):
+def middle_kernel(halo, local, other, mate, decay, image, out):
     add_halo(halo, local, mate, other, image)
     offset = jnp.zeros((ELEMENTS, WIDTH), F32)
     for t in reversed(range(SLABS)):
@@ -338,7 +338,7 @@
     return jnp.sum(jnp.sum(x, axis=0), keepdims=True)
 
 
-def gram_kernel(halo, local, mate, other, source, image0, image1, out):
+def gram_kernel(halo, local, other, mate, source, image0, image1, out):
     add_halo(halo, local, mate, other, image1)
     s = source[...]
     largest = [
@@ -469,7 +469,7 @@
         in_specs=[VMEM] * 5,
         out_specs=(VMEM,) * 2,
         compiler_params=params(SMALL_MIB),
-    )(halo, local, mate, other, decay)
+    )(halo, local, other, mate, decay)
     chain1, local, mate, other, known = operate(
         False, image0, decay, offsets, known, tables, weights, couple
     )
@@ -479,7 +479,7 @@
         in_specs=[VMEM] * 6,
         out_specs=(VMEM,) * 2,
         compiler_params=params(SMALL_MIB),
-    )(halo, local, mate, other, source, image0)
+    )(halo, local, other, mate, source, image0)
     gram = lax.all_to_all(gram, ("tm", "space"), 0, 0, tiled=True)
     adjoint, residual = pl.pallas_call(
         last_kernel,

time: 80.4 us -> 79 us (0.983)
    ppermute x2, starting transfers between devices: 8.46 us -> 0.01 us  [operate(): mate = lax.ppermute(mate, 'space', pairs)]
    ppermute x2, starting transfers between devices: 1.48 us -> 9.71 us  [operate(): other = lax.ppermute(other, 'space', across)]
  transfers between devices with their start and end apart: 11 -> 11, of which waited for: 6 -> 5; matrix products, arithmetic and copies ran while one was open for 2% -> 2% of each run, Pallas kernels for 7% -> 8%
where the time goes in v6:
time: 79 us; the launch traced here: 78.7 us
  blocking collectives  28.4 us (36%)
  starting transfers between devices  25.6 us (32%)
  waiting for transfers between devices  12.1 us (15%)
  Pallas kernels  10.5 us (13%)
  local copies, waits for them, and re-layouts  1.19 us (2%)
  between operations  0.83 us (1%)
    all_to_all x1, blocking collectives, shards(): gram = lax.all_to_all(gram, ('tm', 'space'), 0, 0, tiled=True)  18.6 us
    all_to_all x1, blocking collectives, along(): return lax.all_to_all(x, 'tm', 0, 0, axis_index_groups=groups, tiled=True)  9.83 us
    ppermute x2, starting transfers between devices, operate(): other = lax.ppermute(other, 'space', across)  9.71 us
    all_to_all x1, starting transfers between devices, along(): return lax.all_to_all(x, 'tm', 0, 0, axis_index_groups=groups, tiled=True)  9.03 us
    ppermute x6, starting transfers between devices, operate(): lax.ppermute(line, 'tm', [(i ^ k * RING, i) for i in range(count)])  6.84 us
    all_to_all x1, waiting for transfers between devices, along(): return lax.all_to_all(x, 'tm', 0, 0, axis_index_groups=groups, tiled=True)  6.75 us
    ppermute x6, waiting for transfers between devices, operate(): lax.ppermute(line, 'tm', [(i ^ k * RING, i) for i in range(count)])  5.35 us
    pallas_call x2, Pallas kernels, operate(): pl.pallas_call(local_kernel, out_shape=struct(SLABS, ELEMENTS, WIDTH), in...  5.15 us
  transfers between devices with their start and end apart: 11, of which 5 were waited for; matrix products, arithmetic and copies ran while one was open for 2% of the time, Pallas kernels for 8%

profile of v6, /device:TPU:1, one launch (start us, length us, event | category | flops | bytes accessed | tf_op | source)
XLA Modules:
  0.0 78.7 jit_solution(18163610990930230249)
XLA Ops:
  0.6 0.0 copy-start.5
  0.6 0.0 copy-start
  0.7 0.0 copy-start.1
  0.7 0.0 copy-start.2
  0.7 0.0 copy-start.3
  0.7 0.0 copy-start.4
  0.7 1.7 %shard_map.87 = f32[8,16,320]{2,1,0:T(8,128)} custom-call(f32[8,8,320]{2,1,0:T(8,128)} %bitcast.23, f32[8,8,320]{2,1,0:T(8,128)} %bitcast.25), custom_call_target="tpu_custom_call" | custom-call | flops 10000000000 | bytes 1000000 | tf_op jit(solution)/shard_map/pallas_call | solution.py:438
  2.4 9.0 %all-to-all-start = ((f32[8,16,320]{2,1,0:T(8,128)}), f32[8,16,320]{2,1,0:T(8,128)S(1)}, u32[]{:S(2)}, u32[]{:S(2)}) async-start(f32[8,16,320]{2,1,0:T(8,128)} %shard_map.87), calls=%async_computation | async-start | bytes 393216 | tf_op jit(solution)/shard_map/all_to_all | solution.py:256
  11.5 0.0 copy-done.5
  11.5 1.1 %reshape.15.couple = bf16[2,2,320,320]{3,2,1,0:T(8,128)(2,1)S(1)} reshape(bf16[2,2,102400]{2,1,0:T(2,128)(2,1)S(1)} %copy-done.5) | data formatting | bytes 1638400 | tf_op jit(solution)/shard_map/reshape | solution.py:435
  12.6 0.1 pad_add_fusion.mine
  12.7 0.0 copy-done
  12.7 0.0 copy-done.1
  12.7 0.0 copy-done.2
  12.7 0.0 copy-done.3
  12.7 0.0 copy-done.4
  12.7 0.8 %shard_map.86 = (bf16[64,384]{1,0:T(8,128)(2,1)S(1)}, bf16[64,128]{1,0:T(8,128)(2,1)S(1)}, f32[8,8,320]{2,1,0:T(8,128)S(1)}, f32[8,8,320]{2,1,0:T(8,128)S(1)}, f...) custom-call(s32[2]{0:T(128)S(1)} %pad_add_fusion.mine, s32[6,8]{1,0:T(8,128)S(1)} %copy-done.2, ...), custom_call_target="tpu_custom_call" | custom-call | tf_op jit(solution)/shard_map/pallas_call | solution.py:448
  13.5 6.8 %all-to-all-done.refs_1_ = f32[8,16,320]{2,1,0:T(8,128)S(1)} async-done(((f32[8,16,320]{2,1,0:T(8,128)}), f32[8,16,320]{2,1,0:T(8,128)S(1)}, u32[]{:S(2)}, u32[]{:S(2)}) %all-to-all-start) | async-done | bytes 163872 | tf_op jit(solution)/shard_map/all_to_all | solution.py:256
  20.3 0.0 slice-start
  20.3 0.0 slice-start.1
  20.3 2.8 %collective-permute-start.2 = (f32[16,320]{1,0:T(8,128)S(1)}, f32[16,320]{1,0:T(8,128)S(1)}, u32[]{:S(2)}, u32[]{:S(2)}) collective-permute-start(f32[16,320]{1,0:T(8,128)S(1)} %get-tuple-element.30.refs_3_), channel_id=1, source_target_pairs={{192,0},{200,8},{208,16},{216,24},{224,32},{232,40},{240,48},{248,... | collective-permute-start | bytes 61448 | tf_op jit(solution)/shard_map/ppermute | solution.py:282
  23.1 0.3 collective-permute-start.1
  23.5 0.3 collective-permute-start
  23.8 0.5 collective-permute-done.2.refs_6_
  24.3 3.0 %collective-permute-done.1.refs_5_ = f32[16,320]{1,0:T(8,128)S(1)} collective-permute-done((f32[16,320]{1,0:T(8,128)S(1)}, f32[16,320]{1,0:T(8,128)S(1)}, u32[]{:S(2)}, u32[]{:S(2)}) %collective-permute-start.1) | collective-permute-done | bytes 20512 | tf_op jit(solution)/shard_map/ppermute | solution.py:282
  27.3 0.0 collective-permute-done.refs_4_
  27.3 0.0 slice-start.2
  27.3 0.7 shard_map.89
  28.0 5.2 %collective-permute-start.3 = (f32[2,8,320]{2,1,0:T(8,128)S(1)}, f32[2,8,320]{2,1,0:T(8,128)S(1)}, u32[]{:S(2)}, u32[]{:S(2)}) collective-permute-start(f32[2,8,320]{2,1,0:T(8,128)S(1)} %get-tuple-element.35), channel_id=1, source_target_pairs={{0,7},{1,2},{2,1},{3,4},{4,3},{5,6},{6,5},{7,0},{8,15},{9,10},{10,... | collective-permute-start | bytes 61448 | tf_op jit(solution)/shard_map/ppermute | solution.py:302
  33.2 0.0 collective-permute-start.4
  33.2 0.0 slice-done
  33.2 0.0 slice-done.1
  33.2 0.0 slice-done.2
  33.2 2.6 %shard_map.90.local = f32[8,8,320]{2,1,0:T(8,128)S(1)} custom-call(bf16[256,1280]{1,0:T(8,128)(2,1)S(1)} %get-tuple-element.33.spread, bf16[64,384]{1,0:T(8,128)(2,1)S(1)} %get-tuple-element.34.faces, bf16[7,1280,640]{2,1,0:T(8,128)(2,1)S(1)} %bitcast.19), custom_call_target="tpu_custom_call" | custom-call | flops 2936012800 | bytes 11468800 | tf_op jit(solution)/shard_map/pallas_call | solution.py:304
  35.9 0.0 collective-permute-done.3.other
  35.9 0.0 collective-permute-done.4.mate
  35.9 0.1 shard_map.91
  36.0 9.8 %all_to_all.21.refs_2_ = f32[8,8,320]{2,1,0:T(8,128)S(1)} all-to-all(f32[8,8,320]{2,1,0:T(8,128)S(1)} %get-tuple-element.38), channel_id=1, replica_groups={{0,8,16,24,32,40,48,56},{64,72,80,88,96,104,112,120},{128,136,144,152,1..., dimensions={0} | all-to-all | bytes 163840 | tf_op jit(solution)/shard_map/all_to_all | solution.py:256
  45.8 1.1 %collective-permute-start.7 = (f32[8,320]{1,0:T(8,128)S(1)}, f32[8,320]{1,0:T(8,128)S(1)}, u32[]{:S(2)}, u32[]{:S(2)}) collective-permute-start(f32[8,320]{1,0:T(8,128)S(1)} %get-tuple-element.40.refs_8_), channel_id=1, source_target_pairs={{192,0},{200,8},{208,16},{216,24},{224,32},{232,40},{240,48},{248,... | collective-permute-start | bytes 30728 | tf_op jit(solution)/shard_map/ppermute | solution.py:282
  46.9 0.8 %collective-permute-start.6 = (f32[8,320]{1,0:T(8,128)S(1)}, f32[8,320]{1,0:T(8,128)S(1)}, u32[]{:S(2)}, u32[]{:S(2)}) collective-permute-start(f32[8,320]{1,0:T(8,128)S(1)} %get-tuple-element.40.refs_8_), channel_id=1, source_target_pairs={{128,0},{136,8},{144,16},{152,24},{160,32},{168,40},{176,48},{184,... | collective-permute-start | bytes 30728 | tf_op jit(solution)/shard_map/ppermute | solution.py:282
  47.8 1.4 %collective-permute-start.5 = (f32[8,320]{1,0:T(8,128)S(1)}, f32[8,320]{1,0:T(8,128)S(1)}, u32[]{:S(2)}, u32[]{:S(2)}) collective-permute-start(f32[8,320]{1,0:T(8,128)S(1)} %get-tuple-element.40.refs_8_), channel_id=1, source_target_pairs={{64,0},{72,8},{80,16},{88,24},{96,32},{104,40},{112,48},{120,56},{... | collective-permute-start | bytes 30728 | tf_op jit(solution)/shard_map/ppermute | solution.py:282
  49.2 0.5 collective-permute-done.7.refs_11_
  49.7 1.3 %collective-permute-done.6.refs_10_ = f32[8,320]{1,0:T(8,128)S(1)} collective-permute-done((f32[8,320]{1,0:T(8,128)S(1)}, f32[8,320]{1,0:T(8,128)S(1)}, u32[]{:S(2)}, u32[]{:S(2)}) %collective-permute-start.6) | collective-permute-done | bytes 10272 | tf_op jit(solution)/shard_map/ppermute | solution.py:282
  51.0 0.0 collective-permute-done.5.refs_9_
  51.0 0.7 shard_map.93
  51.7 4.5 %collective-permute-start.8 = (f32[2,8,320]{2,1,0:T(8,128)S(1)}, f32[2,8,320]{2,1,0:T(8,128)S(1)}, u32[]{:S(2)}, u32[]{:S(2)}) collective-permute-start(f32[2,8,320]{2,1,0:T(8,128)S(1)} %get-tuple-element.42), channel_id=1, source_target_pairs={{0,7},{1,2},{2,1},{3,4},{4,3},{5,6},{6,5},{7,0},{8,15},{9,10},{10,... | collective-permute-start | bytes 61448 | tf_op jit(solution)/shard_map/ppermute | solution.py:302
  56.2 0.0 collective-permute-start.9
  56.2 2.5 %shard_map.94.local = f32[8,8,320]{2,1,0:T(8,128)S(1)} custom-call(bf16[256,1280]{1,0:T(8,128)(2,1)S(1)} %get-tuple-element.41.spread, bf16[64,384]{1,0:T(8,128)(2,1)S(1)} %get-tuple-element.34.faces, bf16[7,1280,640]{2,1,0:T(8,128)(2,1)S(1)} %bitcast.20), custom_call_target="tpu_custom_call" | custom-call | flops 2936012800 | bytes 11468800 | tf_op jit(solution)/shard_map/pallas_call | solution.py:304
  58.7 0.0 collective-permute-done.8.other
  58.7 0.0 collective-permute-done.9.mate
  58.7 0.3 shard_map.95
  59.1 18.6 %all_to_all.22 = f32[256,1,128]{2,1,0:T(1,128)S(1)} all-to-all(f32[256,1,128]{2,1,0:T(1,128)S(1)} %bitcast.22), channel_id=1, replica_groups=mesh['tm'=32,'space'=8] {'tm','space'}, dimensions={0} | all-to-all | bytes 262144 | tf_op jit(solution)/shard_map/all_to_all | solution.py:483
  77.7 1.0 %shard_map.96 = (f32[8,8,320]{2,1,0:T(8,128)}, f32[8,8,320]{2,1,0:T(8,128)}) custom-call(f32[256,128]{1,0:T(8,128)S(1)} %bitcast.21, f32[8,8,320]{2,1,0:T(8,128)S(1)} %get-tuple-element.27.refs_0_.source, f32[8,8,320]{2,1,0:T(8,128)S(1)} %get-tuple-element.45.first_chain, f32[8,8,320]{2,1,0:T(8,128)S(1)} %get-tuple-element.46.second_chain, ...), custom_call_target="tpu_custom_call" | custom-call | tf_op jit(solution)/shard_map/pallas_call | solution.py:484
  (3 shorter events, 0.0 us)
Async XLA Ops:
  0.6 10.8 %copy-start.5 = (bf16[2,2,102400]{2,1,0:T(2,128)(2,1)S(1)}, bf16[2,2,102400]{2,1,0:T(2,128)(2,1)}, u32[]{:S(2)}) copy-start(bf16[2,2,102400]{2,1,0:T(2,128)(2,1)} %param.11) | copy-start | bytes 2457604
  0.6 12.1 %copy-start = (f32[8,320,8]{1,2,0:T(8,128)S(1)}, f32[8,320,8]{1,2,0:T(8,128)}, u32[]{:S(2)}) copy-start(f32[8,320,8]{1,2,0:T(8,128)} %param.7) | copy-start | bytes 245764
  0.7 12.1 %copy-start.1 = (f32[8,320,8]{1,2,0:T(8,128)S(1)}, f32[8,320,8]{1,2,0:T(8,128)}, u32[]{:S(2)}) copy-start(f32[8,320,8]{1,2,0:T(8,128)} %param.8) | copy-start | bytes 245764
  0.7 12.0 %copy-start.2 = (s32[6,8]{1,0:T(8,128)S(1)}, s32[6,8]{1,0:T(8,128)}, u32[]{:S(2)}) copy-start(s32[6,8]{1,0:T(8,128)} %neighbours.1) | copy-start | bytes 580
  0.7 12.0 %copy-start.3 = (s32[2,2]{1,0:T(2,128)S(1)}, s32[2,2]{1,0:T(2,128)}, u32[]{:S(2)}) copy-start(s32[2,2]{1,0:T(2,128)} %owner.1) | copy-start | bytes 52
  0.7 12.0 %copy-start.4 = (s32[1,2]{1,0:T(1,128)S(1)}, s32[1,2]{1,0:T(1,128)}, u32[]{:S(2)}) copy-start(s32[1,2]{1,0:T(1,128)} %pairing.1) | copy-start | bytes 28
  2.4 17.8 %all-to-all-start = ((f32[8,16,320]{2,1,0:T(8,128)}), f32[8,16,320]{2,1,0:T(8,128)S(1)}, u32[]{:S(2)}, u32[]{:S(2)}) async-start(f32[8,16,320]{2,1,0:T(8,128)} %shard_map.87), calls=%async_computation | async-start | bytes 393216 | tf_op jit(solution)/shard_map/all_to_all | solution.py:256
  20.3 12.9 %slice-start = ((s8[11468800]{0:T(1024)(128)(4,1)}), s8[4194304]{0:T(1024)(128)(4,1)S(1)}, s32[]{:S(2)}) async-start(s8[11468800]{0:T(1024)(128)(4,1)} %bitcast.17), calls=%async_computation.3 | async-start | bytes 8388608
  20.3 12.9 %slice-start.1 = ((s8[11468800]{0:T(1024)(128)(4,1)}), s8[4194304]{0:T(1024)(128)(4,1)S(1)}, s32[]{:S(2)}) async-start(s8[11468800]{0:T(1024)(128)(4,1)} %bitcast.17), calls=%async_computation.4 | async-start | bytes 8388608
  20.3 4.0 %collective-permute-start.2 = (f32[16,320]{1,0:T(8,128)S(1)}, f32[16,320]{1,0:T(8,128)S(1)}, u32[]{:S(2)}, u32[]{:S(2)}) collective-permute-start(f32[16,320]{1,0:T(8,128)S(1)} %get-tuple-element.30.refs_3_), channel_id=1, source_target_pairs={{192,0},{200,8},{208,16},{216,24},{224,32},{232,40},{240,48},{248,... | collective-permute-start | bytes 61448 | tf_op jit(solution)/shard_map/ppermute | solution.py:282
  23.1 4.2 %collective-permute-start.1 = (f32[16,320]{1,0:T(8,128)S(1)}, f32[16,320]{1,0:T(8,128)S(1)}, u32[]{:S(2)}, u32[]{:S(2)}) collective-permute-start(f32[16,320]{1,0:T(8,128)S(1)} %get-tuple-element.30.refs_3_), channel_id=1, source_target_pairs={{128,0},{136,8},{144,16},{152,24},{160,32},{168,40},{176,48},{184,... | collective-permute-start | bytes 61448 | tf_op jit(solution)/shard_map/ppermute | solution.py:282
  23.5 3.9 %collective-permute-start = (f32[16,320]{1,0:T(8,128)S(1)}, f32[16,320]{1,0:T(8,128)S(1)}, u32[]{:S(2)}, u32[]{:S(2)}) collective-permute-start(f32[16,320]{1,0:T(8,128)S(1)} %get-tuple-element.30.refs_3_), channel_id=1, source_target_pairs={{64,0},{72,8},{80,16},{88,24},{96,32},{104,40},{112,48},{120,56},{... | collective-permute-start | bytes 61448 | tf_op jit(solution)/shard_map/ppermute | solution.py:282
  27.3 5.9 %slice-start.2 = ((s8[11468800]{0:T(1024)(128)(4,1)}), s8[3080192]{0:T(1024)(128)(4,1)S(1)}, s32[]{:S(2)}) async-start(s8[11468800]{0:T(1024)(128)(4,1)} %bitcast.17), calls=%async_computation.5 | async-start | bytes 6160384
  28.0 7.9 %collective-permute-start.3 = (f32[2,8,320]{2,1,0:T(8,128)S(1)}, f32[2,8,320]{2,1,0:T(8,128)S(1)}, u32[]{:S(2)}, u32[]{:S(2)}) collective-permute-start(f32[2,8,320]{2,1,0:T(8,128)S(1)} %get-tuple-element.35), channel_id=1, source_target_pairs={{0,7},{1,2},{2,1},{3,4},{4,3},{5,6},{6,5},{7,0},{8,15},{9,10},{10,... | collective-permute-start | bytes 61448 | tf_op jit(solution)/shard_map/ppermute | solution.py:302
  33.2 2.7 %collective-permute-start.4 = (f32[2,8,320]{2,1,0:T(8,128)S(1)}, f32[2,8,320]{2,1,0:T(8,128)S(1)}, u32[]{:S(2)}, u32[]{:S(2)}) collective-permute-start(f32[2,8,320]{2,1,0:T(8,128)S(1)} %get-tuple-element.36), channel_id=1, source_target_pairs={{0,1},{1,0},{2,3},{3,2},{4,5},{5,4},{6,7},{7,6},{8,9},{9,8},{10,11... | collective-permute-start | bytes 61448 | tf_op jit(solution)/shard_map/ppermute | solution.py:303
  45.8 3.8 %collective-permute-start.7 = (f32[8,320]{1,0:T(8,128)S(1)}, f32[8,320]{1,0:T(8,128)S(1)}, u32[]{:S(2)}, u32[]{:S(2)}) collective-permute-start(f32[8,320]{1,0:T(8,128)S(1)} %get-tuple-element.40.refs_8_), channel_id=1, source_target_pairs={{192,0},{200,8},{208,16},{216,24},{224,32},{232,40},{240,48},{248,... | collective-permute-start | bytes 30728 | tf_op jit(solution)/shard_map/ppermute | solution.py:282
  46.9 4.0 %collective-permute-start.6 = (f32[8,320]{1,0:T(8,128)S(1)}, f32[8,320]{1,0:T(8,128)S(1)}, u32[]{:S(2)}, u32[]{:S(2)}) collective-permute-start(f32[8,320]{1,0:T(8,128)S(1)} %get-tuple-element.40.refs_8_), channel_id=1, source_target_pairs={{128,0},{136,8},{144,16},{152,24},{160,32},{168,40},{176,48},{184,... | collective-permute-start | bytes 30728 | tf_op jit(solution)/shard_map/ppermute | solution.py:282
  47.8 3.2 %collective-permute-start.5 = (f32[8,320]{1,0:T(8,128)S(1)}, f32[8,320]{1,0:T(8,128)S(1)}, u32[]{:S(2)}, u32[]{:S(2)}) collective-permute-start(f32[8,320]{1,0:T(8,128)S(1)} %get-tuple-element.40.refs_8_), channel_id=1, source_target_pairs={{64,0},{72,8},{80,16},{88,24},{96,32},{104,40},{112,48},{120,56},{... | collective-permute-start | bytes 30728 | tf_op jit(solution)/shard_map/ppermute | solution.py:282
  51.7 7.0 %collective-permute-start.8 = (f32[2,8,320]{2,1,0:T(8,128)S(1)}, f32[2,8,320]{2,1,0:T(8,128)S(1)}, u32[]{:S(2)}, u32[]{:S(2)}) collective-permute-start(f32[2,8,320]{2,1,0:T(8,128)S(1)} %get-tuple-element.42), channel_id=1, source_target_pairs={{0,7},{1,2},{2,1},{3,4},{4,3},{5,6},{6,5},{7,0},{8,15},{9,10},{10,... | collective-permute-start | bytes 61448 | tf_op jit(solution)/shard_map/ppermute | solution.py:302
  56.2 2.5 %collective-permute-start.9 = (f32[2,8,320]{2,1,0:T(8,128)S(1)}, f32[2,8,320]{2,1,0:T(8,128)S(1)}, u32[]{:S(2)}, u32[]{:S(2)}) collective-permute-start(f32[2,8,320]{2,1,0:T(8,128)S(1)} %get-tuple-element.43), channel_id=1, source_target_pairs={{0,1},{1,0},{2,3},{3,2},{4,5},{5,4},{6,7},{7,6},{8,9},{9,8},{10,11... | collective-permute-start | bytes 61448 | tf_op jit(solution)/shard_map/ppermute | solution.py:303

commit v7 on v6

--- a/solution.py
+++ b/solution.py
@@ -239,16 +239,15 @@
             )
         return results
 
-    result = jnp.zeros((ROWS, WIDTH), F32)
     placed = []
     for some in ((1, 2), (3, 4), (5, 6)):
         placed += products(some)
+    result = products((0,))[0]
     placed = jnp.concatenate(placed, axis=0)
     high = placed.astype(BF16)
     low = (placed - high.astype(F32)).astype(BF16)
     for part in (high, low):
         result = result + jnp.dot(faces[...], part, preferred_element_type=F32)
-    result = result + products((0,))[0]
     local[...] = result.reshape(SLABS, ELEMENTS, WIDTH)
 
 

time: 79 us -> 78.9 us (level)
  transfers between devices with their start and end apart: 11 -> 11, of which waited for: 5 -> 5; matrix products, arithmetic and copies ran while one was open for 2% -> 2% of each run, Pallas kernels for 8% -> 7%
where the time goes in v7:
time: 78.9 us; the launch traced here: 78.6 us
  blocking collectives  28.9 us (37%)
  starting transfers between devices  25.5 us (32%)
  waiting for transfers between devices  12.1 us (15%)
  Pallas kernels  10 us (13%)
  local copies, waits for them, and re-layouts  1.19 us (2%)
  between operations  0.83 us (1%)
    all_to_all x1, blocking collectives, shards(): gram = lax.all_to_all(gram, ('tm', 'space'), 0, 0, tiled=True)  19 us
    all_to_all x1, blocking collectives, along(): return lax.all_to_all(x, 'tm', 0, 0, axis_index_groups=groups, tiled=True)  9.9 us
    ppermute x2, starting transfers between devices, operate(): other = lax.ppermute(other, 'space', across)  9.63 us
    all_to_all x1, starting transfers between devices, along(): return lax.all_to_all(x, 'tm', 0, 0, axis_index_groups=groups, tiled=True)  9.03 us
    ppermute x6, starting transfers between devices, operate(): lax.ppermute(line, 'tm', [(i ^ k * RING, i) for i in range(count)])  6.84 us
    all_to_all x1, waiting for transfers between devices, along(): return lax.all_to_all(x, 'tm', 0, 0, axis_index_groups=groups, tiled=True)  6.75 us
    ppermute x6, waiting for transfers between devices, operate(): lax.ppermute(line, 'tm', [(i ^ k * RING, i) for i in range(count)])  5.36 us
    pallas_call x2, Pallas kernels, operate(): pl.pallas_call(local_kernel, out_shape=struct(SLABS, ELEMENTS, WIDTH), in...  4.66 us
  transfers between devices with their start and end apart: 11, of which 5 were waited for; matrix products, arithmetic and copies ran while one was open for 2% of the time, Pallas kernels for 7%

profile of v7, /device:TPU:1, one launch (start us, length us, event | category | flops | bytes accessed | tf_op | source)
XLA Modules:
  0.0 78.6 jit_solution(7306483105937219290)
XLA Ops:
  0.6 0.0 copy-start.5
  0.6 0.0 copy-start
  0.7 0.0 copy-start.1
  0.7 0.0 copy-start.2
  0.7 0.0 copy-start.3
  0.7 0.0 copy-start.4
  0.7 1.7 %shard_map.87 = f32[8,16,320]{2,1,0:T(8,128)} custom-call(f32[8,8,320]{2,1,0:T(8,128)} %bitcast.23, f32[8,8,320]{2,1,0:T(8,128)} %bitcast.25), custom_call_target="tpu_custom_call" | custom-call | flops 10000000000 | bytes 1000000 | tf_op jit(solution)/shard_map/pallas_call | solution.py:437
  2.4 9.0 %all-to-all-start = ((f32[8,16,320]{2,1,0:T(8,128)}), f32[8,16,320]{2,1,0:T(8,128)S(1)}, u32[]{:S(2)}, u32[]{:S(2)}) async-start(f32[8,16,320]{2,1,0:T(8,128)} %shard_map.87), calls=%async_computation | async-start | bytes 393216 | tf_op jit(solution)/shard_map/all_to_all | solution.py:255
  11.5 0.0 copy-done.5
  11.5 1.1 %reshape.15.couple = bf16[2,2,320,320]{3,2,1,0:T(8,128)(2,1)S(1)} reshape(bf16[2,2,102400]{2,1,0:T(2,128)(2,1)S(1)} %copy-done.5) | data formatting | bytes 1638400 | tf_op jit(solution)/shard_map/reshape | solution.py:434
  12.6 0.1 pad_add_fusion.mine
  12.7 0.0 copy-done
  12.7 0.0 copy-done.1
  12.7 0.0 copy-done.2
  12.7 0.0 copy-done.3
  12.7 0.0 copy-done.4
  12.7 0.8 %shard_map.86 = (bf16[64,384]{1,0:T(8,128)(2,1)S(1)}, bf16[64,128]{1,0:T(8,128)(2,1)S(1)}, f32[8,8,320]{2,1,0:T(8,128)S(1)}, f32[8,8,320]{2,1,0:T(8,128)S(1)}, f...) custom-call(s32[2]{0:T(128)S(1)} %pad_add_fusion.mine, s32[6,8]{1,0:T(8,128)S(1)} %copy-done.2, ...), custom_call_target="tpu_custom_call" | custom-call | tf_op jit(solution)/shard_map/pallas_call | solution.py:447
  13.5 6.8 %all-to-all-done.refs_1_ = f32[8,16,320]{2,1,0:T(8,128)S(1)} async-done(((f32[8,16,320]{2,1,0:T(8,128)}), f32[8,16,320]{2,1,0:T(8,128)S(1)}, u32[]{:S(2)}, u32[]{:S(2)}) %all-to-all-start) | async-done | bytes 163872 | tf_op jit(solution)/shard_map/all_to_all | solution.py:255
  20.3 0.0 slice-start
  20.3 0.0 slice-start.1
  20.3 2.8 %collective-permute-start.2 = (f32[16,320]{1,0:T(8,128)S(1)}, f32[16,320]{1,0:T(8,128)S(1)}, u32[]{:S(2)}, u32[]{:S(2)}) collective-permute-start(f32[16,320]{1,0:T(8,128)S(1)} %get-tuple-element.30.refs_3_), channel_id=1, source_target_pairs={{192,0},{200,8},{208,16},{216,24},{224,32},{232,40},{240,48},{248,... | collective-permute-start | bytes 61448 | tf_op jit(solution)/shard_map/ppermute | solution.py:281
  23.1 0.3 collective-permute-start.1
  23.5 0.3 collective-permute-start
  23.8 0.5 collective-permute-done.2.refs_6_
  24.3 3.0 %collective-permute-done.1.refs_5_ = f32[16,320]{1,0:T(8,128)S(1)} collective-permute-done((f32[16,320]{1,0:T(8,128)S(1)}, f32[16,320]{1,0:T(8,128)S(1)}, u32[]{:S(2)}, u32[]{:S(2)}) %collective-permute-start.1) | collective-permute-done | bytes 20512 | tf_op jit(solution)/shard_map/ppermute | solution.py:281
  27.3 0.0 collective-permute-done.refs_4_
  27.3 0.0 slice-start.2
  27.3 0.7 shard_map.89
  28.0 5.2 %collective-permute-start.3 = (f32[2,8,320]{2,1,0:T(8,128)S(1)}, f32[2,8,320]{2,1,0:T(8,128)S(1)}, u32[]{:S(2)}, u32[]{:S(2)}) collective-permute-start(f32[2,8,320]{2,1,0:T(8,128)S(1)} %get-tuple-element.35), channel_id=1, source_target_pairs={{0,7},{1,2},{2,1},{3,4},{4,3},{5,6},{6,5},{7,0},{8,15},{9,10},{10,... | collective-permute-start | bytes 61448 | tf_op jit(solution)/shard_map/ppermute | solution.py:301
  33.2 0.0 collective-permute-start.4
  33.2 0.0 slice-done
  33.2 0.0 slice-done.1
  33.2 0.0 slice-done.2
  33.2 2.4 %shard_map.90.local = f32[8,8,320]{2,1,0:T(8,128)S(1)} custom-call(bf16[256,1280]{1,0:T(8,128)(2,1)S(1)} %get-tuple-element.33.spread, bf16[64,384]{1,0:T(8,128)(2,1)S(1)} %get-tuple-element.34.faces, bf16[7,1280,640]{2,1,0:T(8,128)(2,1)S(1)} %bitcast.19), custom_call_target="tpu_custom_call" | custom-call | flops 2936012800 | bytes 11468800 | tf_op jit(solution)/shard_map/pallas_call | solution.py:303
  35.6 0.0 collective-permute-done.3.other
  35.6 0.0 collective-permute-done.4.mate
  35.7 0.1 shard_map.91
  35.7 9.9 %all_to_all.21.refs_2_ = f32[8,8,320]{2,1,0:T(8,128)S(1)} all-to-all(f32[8,8,320]{2,1,0:T(8,128)S(1)} %get-tuple-element.38), channel_id=1, replica_groups={{0,8,16,24,32,40,48,56},{64,72,80,88,96,104,112,120},{128,136,144,152,1..., dimensions={0} | all-to-all | bytes 163840 | tf_op jit(solution)/shard_map/all_to_all | solution.py:255
  45.7 1.1 %collective-permute-start.7 = (f32[8,320]{1,0:T(8,128)S(1)}, f32[8,320]{1,0:T(8,128)S(1)}, u32[]{:S(2)}, u32[]{:S(2)}) collective-permute-start(f32[8,320]{1,0:T(8,128)S(1)} %get-tuple-element.40.refs_8_), channel_id=1, source_target_pairs={{192,0},{200,8},{208,16},{216,24},{224,32},{232,40},{240,48},{248,... | collective-permute-start | bytes 30728 | tf_op jit(solution)/shard_map/ppermute | solution.py:281
  46.8 0.8 %collective-permute-start.6 = (f32[8,320]{1,0:T(8,128)S(1)}, f32[8,320]{1,0:T(8,128)S(1)}, u32[]{:S(2)}, u32[]{:S(2)}) collective-permute-start(f32[8,320]{1,0:T(8,128)S(1)} %get-tuple-element.40.refs_8_), channel_id=1, source_target_pairs={{128,0},{136,8},{144,16},{152,24},{160,32},{168,40},{176,48},{184,... | collective-permute-start | bytes 30728 | tf_op jit(solution)/shard_map/ppermute | solution.py:281
  47.6 1.4 %collective-permute-start.5 = (f32[8,320]{1,0:T(8,128)S(1)}, f32[8,320]{1,0:T(8,128)S(1)}, u32[]{:S(2)}, u32[]{:S(2)}) collective-permute-start(f32[8,320]{1,0:T(8,128)S(1)} %get-tuple-element.40.refs_8_), channel_id=1, source_target_pairs={{64,0},{72,8},{80,16},{88,24},{96,32},{104,40},{112,48},{120,56},{... | collective-permute-start | bytes 30728 | tf_op jit(solution)/shard_map/ppermute | solution.py:281
  49.0 0.5 collective-permute-done.7.refs_11_
  49.5 1.3 %collective-permute-done.6.refs_10_ = f32[8,320]{1,0:T(8,128)S(1)} collective-permute-done((f32[8,320]{1,0:T(8,128)S(1)}, f32[8,320]{1,0:T(8,128)S(1)}, u32[]{:S(2)}, u32[]{:S(2)}) %collective-permute-start.6) | collective-permute-done | bytes 10272 | tf_op jit(solution)/shard_map/ppermute | solution.py:281
  50.8 0.0 collective-permute-done.5.refs_9_
  50.8 0.7 shard_map.93
  51.5 4.4 %collective-permute-start.8 = (f32[2,8,320]{2,1,0:T(8,128)S(1)}, f32[2,8,320]{2,1,0:T(8,128)S(1)}, u32[]{:S(2)}, u32[]{:S(2)}) collective-permute-start(f32[2,8,320]{2,1,0:T(8,128)S(1)} %get-tuple-element.42), channel_id=1, source_target_pairs={{0,7},{1,2},{2,1},{3,4},{4,3},{5,6},{6,5},{7,0},{8,15},{9,10},{10,... | collective-permute-start | bytes 61448 | tf_op jit(solution)/shard_map/ppermute | solution.py:301
  55.9 0.0 collective-permute-start.9
  55.9 2.3 %shard_map.94.local = f32[8,8,320]{2,1,0:T(8,128)S(1)} custom-call(bf16[256,1280]{1,0:T(8,128)(2,1)S(1)} %get-tuple-element.41.spread, bf16[64,384]{1,0:T(8,128)(2,1)S(1)} %get-tuple-element.34.faces, bf16[7,1280,640]{2,1,0:T(8,128)(2,1)S(1)} %bitcast.20), custom_call_target="tpu_custom_call" | custom-call | flops 2936012800 | bytes 11468800 | tf_op jit(solution)/shard_map/pallas_call | solution.py:303
  58.2 0.0 collective-permute-done.8.other
  58.2 0.0 collective-permute-done.9.mate
  58.2 0.3 shard_map.95
  58.6 19.0 %all_to_all.22 = f32[256,1,128]{2,1,0:T(1,128)S(1)} all-to-all(f32[256,1,128]{2,1,0:T(1,128)S(1)} %bitcast.22), channel_id=1, replica_groups=mesh['tm'=32,'space'=8] {'tm','space'}, dimensions={0} | all-to-all | bytes 262144 | tf_op jit(solution)/shard_map/all_to_all | solution.py:482
  77.6 1.0 %shard_map.96 = (f32[8,8,320]{2,1,0:T(8,128)}, f32[8,8,320]{2,1,0:T(8,128)}) custom-call(f32[256,128]{1,0:T(8,128)S(1)} %bitcast.21, f32[8,8,320]{2,1,0:T(8,128)S(1)} %get-tuple-element.27.refs_0_.source, f32[8,8,320]{2,1,0:T(8,128)S(1)} %get-tuple-element.45.first_chain, f32[8,8,320]{2,1,0:T(8,128)S(1)} %get-tuple-element.46.second_chain, ...), custom_call_target="tpu_custom_call" | custom-call | tf_op jit(solution)/shard_map/pallas_call | solution.py:483
  (3 shorter events, 0.0 us)
Async XLA Ops:
  0.6 10.8 %copy-start.5 = (bf16[2,2,102400]{2,1,0:T(2,128)(2,1)S(1)}, bf16[2,2,102400]{2,1,0:T(2,128)(2,1)}, u32[]{:S(2)}) copy-start(bf16[2,2,102400]{2,1,0:T(2,128)(2,1)} %param.11) | copy-start | bytes 2457604
  0.6 12.1 %copy-start = (f32[8,320,8]{1,2,0:T(8,128)S(1)}, f32[8,320,8]{1,2,0:T(8,128)}, u32[]{:S(2)}) copy-start(f32[8,320,8]{1,2,0:T(8,128)} %param.7) | copy-start | bytes 245764
  0.7 12.1 %copy-start.1 = (f32[8,320,8]{1,2,0:T(8,128)S(1)}, f32[8,320,8]{1,2,0:T(8,128)}, u32[]{:S(2)}) copy-start(f32[8,320,8]{1,2,0:T(8,128)} %param.8) | copy-start | bytes 245764
  0.7 12.0 %copy-start.2 = (s32[6,8]{1,0:T(8,128)S(1)}, s32[6,8]{1,0:T(8,128)}, u32[]{:S(2)}) copy-start(s32[6,8]{1,0:T(8,128)} %neighbours.1) | copy-start | bytes 580
  0.7 12.0 %copy-start.3 = (s32[2,2]{1,0:T(2,128)S(1)}, s32[2,2]{1,0:T(2,128)}, u32[]{:S(2)}) copy-start(s32[2,2]{1,0:T(2,128)} %owner.1) | copy-start | bytes 52
  0.7 12.0 %copy-start.4 = (s32[1,2]{1,0:T(1,128)S(1)}, s32[1,2]{1,0:T(1,128)}, u32[]{:S(2)}) copy-start(s32[1,2]{1,0:T(1,128)} %pairing.1) | copy-start | bytes 28
  2.4 17.8 %all-to-all-start = ((f32[8,16,320]{2,1,0:T(8,128)}), f32[8,16,320]{2,1,0:T(8,128)S(1)}, u32[]{:S(2)}, u32[]{:S(2)}) async-start(f32[8,16,320]{2,1,0:T(8,128)} %shard_map.87), calls=%async_computation | async-start | bytes 393216 | tf_op jit(solution)/shard_map/all_to_all | solution.py:255
  20.3 12.9 %slice-start = ((s8[11468800]{0:T(1024)(128)(4,1)}), s8[4194304]{0:T(1024)(128)(4,1)S(1)}, s32[]{:S(2)}) async-start(s8[11468800]{0:T(1024)(128)(4,1)} %bitcast.17), calls=%async_computation.3 | async-start | bytes 8388608
  20.3 12.9 %slice-start.1 = ((s8[11468800]{0:T(1024)(128)(4,1)}), s8[4194304]{0:T(1024)(128)(4,1)S(1)}, s32[]{:S(2)}) async-start(s8[11468800]{0:T(1024)(128)(4,1)} %bitcast.17), calls=%async_computation.4 | async-start | bytes 8388608
  20.3 4.0 %collective-permute-start.2 = (f32[16,320]{1,0:T(8,128)S(1)}, f32[16,320]{1,0:T(8,128)S(1)}, u32[]{:S(2)}, u32[]{:S(2)}) collective-permute-start(f32[16,320]{1,0:T(8,128)S(1)} %get-tuple-element.30.refs_3_), channel_id=1, source_target_pairs={{192,0},{200,8},{208,16},{216,24},{224,32},{232,40},{240,48},{248,... | collective-permute-start | bytes 61448 | tf_op jit(solution)/shard_map/ppermute | solution.py:281
  23.1 4.2 %collective-permute-start.1 = (f32[16,320]{1,0:T(8,128)S(1)}, f32[16,320]{1,0:T(8,128)S(1)}, u32[]{:S(2)}, u32[]{:S(2)}) collective-permute-start(f32[16,320]{1,0:T(8,128)S(1)} %get-tuple-element.30.refs_3_), channel_id=1, source_target_pairs={{128,0},{136,8},{144,16},{152,24},{160,32},{168,40},{176,48},{184,... | collective-permute-start | bytes 61448 | tf_op jit(solution)/shard_map/ppermute | solution.py:281
  23.5 3.9 %collective-permute-start = (f32[16,320]{1,0:T(8,128)S(1)}, f32[16,320]{1,0:T(8,128)S(1)}, u32[]{:S(2)}, u32[]{:S(2)}) collective-permute-start(f32[16,320]{1,0:T(8,128)S(1)} %get-tuple-element.30.refs_3_), channel_id=1, source_target_pairs={{64,0},{72,8},{80,16},{88,24},{96,32},{104,40},{112,48},{120,56},{... | collective-permute-start | bytes 61448 | tf_op jit(solution)/shard_map/ppermute | solution.py:281
  27.3 5.9 %slice-start.2 = ((s8[11468800]{0:T(1024)(128)(4,1)}), s8[3080192]{0:T(1024)(128)(4,1)S(1)}, s32[]{:S(2)}) async-start(s8[11468800]{0:T(1024)(128)(4,1)} %bitcast.17), calls=%async_computation.5 | async-start | bytes 6160384
  28.0 7.6 %collective-permute-start.3 = (f32[2,8,320]{2,1,0:T(8,128)S(1)}, f32[2,8,320]{2,1,0:T(8,128)S(1)}, u32[]{:S(2)}, u32[]{:S(2)}) collective-permute-start(f32[2,8,320]{2,1,0:T(8,128)S(1)} %get-tuple-element.35), channel_id=1, source_target_pairs={{0,7},{1,2},{2,1},{3,4},{4,3},{5,6},{6,5},{7,0},{8,15},{9,10},{10,... | collective-permute-start | bytes 61448 | tf_op jit(solution)/shard_map/ppermute | solution.py:301
  33.2 2.4 %collective-permute-start.4 = (f32[2,8,320]{2,1,0:T(8,128)S(1)}, f32[2,8,320]{2,1,0:T(8,128)S(1)}, u32[]{:S(2)}, u32[]{:S(2)}) collective-permute-start(f32[2,8,320]{2,1,0:T(8,128)S(1)} %get-tuple-element.36), channel_id=1, source_target_pairs={{0,1},{1,0},{2,3},{3,2},{4,5},{5,4},{6,7},{7,6},{8,9},{9,8},{10,11... | collective-permute-start | bytes 61448 | tf_op jit(solution)/shard_map/ppermute | solution.py:302
  45.7 3.8 %collective-permute-start.7 = (f32[8,320]{1,0:T(8,128)S(1)}, f32[8,320]{1,0:T(8,128)S(1)}, u32[]{:S(2)}, u32[]{:S(2)}) collective-permute-start(f32[8,320]{1,0:T(8,128)S(1)} %get-tuple-element.40.refs_8_), channel_id=1, source_target_pairs={{192,0},{200,8},{208,16},{216,24},{224,32},{232,40},{240,48},{248,... | collective-permute-start | bytes 30728 | tf_op jit(solution)/shard_map/ppermute | solution.py:281
  46.8 4.0 %collective-permute-start.6 = (f32[8,320]{1,0:T(8,128)S(1)}, f32[8,320]{1,0:T(8,128)S(1)}, u32[]{:S(2)}, u32[]{:S(2)}) collective-permute-start(f32[8,320]{1,0:T(8,128)S(1)} %get-tuple-element.40.refs_8_), channel_id=1, source_target_pairs={{128,0},{136,8},{144,16},{152,24},{160,32},{168,40},{176,48},{184,... | collective-permute-start | bytes 30728 | tf_op jit(solution)/shard_map/ppermute | solution.py:281
  47.6 3.2 %collective-permute-start.5 = (f32[8,320]{1,0:T(8,128)S(1)}, f32[8,320]{1,0:T(8,128)S(1)}, u32[]{:S(2)}, u32[]{:S(2)}) collective-permute-start(f32[8,320]{1,0:T(8,128)S(1)} %get-tuple-element.40.refs_8_), channel_id=1, source_target_pairs={{64,0},{72,8},{80,16},{88,24},{96,32},{104,40},{112,48},{120,56},{... | collective-permute-start | bytes 30728 | tf_op jit(solution)/shard_map/ppermute | solution.py:281
  51.5 6.7 %collective-permute-start.8 = (f32[2,8,320]{2,1,0:T(8,128)S(1)}, f32[2,8,320]{2,1,0:T(8,128)S(1)}, u32[]{:S(2)}, u32[]{:S(2)}) collective-permute-start(f32[2,8,320]{2,1,0:T(8,128)S(1)} %get-tuple-element.42), channel_id=1, source_target_pairs={{0,7},{1,2},{2,1},{3,4},{4,3},{5,6},{6,5},{7,0},{8,15},{9,10},{10,... | collective-permute-start | bytes 61448 | tf_op jit(solution)/shard_map/ppermute | solution.py:301
  55.9 2.3 %collective-permute-start.9 = (f32[2,8,320]{2,1,0:T(8,128)S(1)}, f32[2,8,320]{2,1,0:T(8,128)S(1)}, u32[]{:S(2)}, u32[]{:S(2)}) collective-permute-start(f32[2,8,320]{2,1,0:T(8,128)S(1)} %get-tuple-element.43), channel_id=1, source_target_pairs={{0,1},{1,0},{2,3},{3,2},{4,5},{5,4},{6,7},{7,6},{8,9},{9,8},{10,11... | collective-permute-start | bytes 61448 | tf_op jit(solution)/shard_map/ppermute | solution.py:302
